TPU v7x, 256 devices: a whole 4x4x8 slice. The times are simulated.
256 devices in a mesh: ctx: 64 (over z, y, core), tp: 4 (over x).
Axes of the slice: x: 4, y: 4, z: 8, core: 2. Of those that a mesh axis runs over, the one named last changes fastest.
Arguments:
- gate_query: bfloat16 [16384, 4096], P('ctx', 'tp'), may hold values from -6 to 6
- gate_key: bfloat16 [16384, 4096], P('ctx', 'tp'), may hold values from -6 to 6
- value_in: bfloat16 [16384, 4096], P('ctx', 'tp'), may hold values from -6 to 6
- residues: float32 [4096, 16], P('tp'), may hold values from -1.5 to 1.5
- decay_rate: float32 [4096, 16], P('tp'), may hold values from 6.1035156e-05 to 0.03
- skip_gain: float32 [4096], P('tp'), may hold values from -4 to 4
- out_weight: bfloat16 [4096, 4096], P('tp'), may hold values from -0.09375 to 0.09375
Outputs:
- mixed: bfloat16 [16384, 4096], P('ctx', 'tp')
All inputs are finite; a program needn't handle non-finite values.
Results may differ from a plain program's by a relative error of at most 0.02.
Values may be sent and summed in bfloat16 or wider, within the bound.
No kernel may reach another device: no remote copies, remote signals or barrier semaphores. Data moves between devices by JAX's collectives and lax.ppermute only.
A program may use at most 128 MiB of HBM per device.

v0:
```python
import math

import jax
import jax.numpy as jnp
from jax import lax
from jax.sharding import PartitionSpec as P


def for_sending(array):

    def short(part):
        return part.astype(jnp.bfloat16) if part.dtype == jnp.float32 else part

    return jax.tree.map(short, array)


def circle(turns, period):
    angle = 2.0 * math.pi / period * turns.astype(jnp.float32)
    return (jnp.cos(angle), jnp.sin(angle))


def cross_forward(rows, index):
    parts, span, chans = rows.shape
    first = 2 * parts
    total = first * span * parts
    freq = jnp.arange(first)
    posit = jnp.arange(parts)
    cos_t, sin_t = circle(freq[:, None] * posit[None, :] % first, first)
    flat = rows.reshape(parts, span * chans)
    real = jnp.dot(cos_t, flat, precision=lax.Precision.HIGHEST).reshape(first, span, chans)
    imag = -jnp.dot(sin_t, flat, precision=lax.Precision.HIGHEST).reshape(first, span, chans)
    offset = index * span + jnp.arange(span)
    tw_cos, tw_sin = circle(freq[:, None] * offset[None, :] % total, total)
    tw_cos = tw_cos[:, :, None]
    tw_sin = tw_sin[:, :, None]
    return (real * tw_cos + imag * tw_sin, imag * tw_cos - real * tw_sin)


def local_transform(real, imag, sign):
    length = real.shape[1]
    posit = jnp.arange(length)
    tab_cos, tab_sin = circle(posit[:, None] * posit[None, :] % length, length)
    tab_sin = sign * tab_sin
    hp = lax.Precision.HIGHEST
    out_real = jnp.einsum("mb,jbc->jmc", tab_cos, real, precision=hp) - jnp.einsum(
        "mb,jbc->jmc", tab_sin, imag, precision=hp
    )
    out_imag = jnp.einsum("mb,jbc->jmc", tab_cos, imag, precision=hp) + jnp.einsum(
        "mb,jbc->jmc", tab_sin, real, precision=hp
    )
    return (out_real, out_imag)


def cross_inverse(real, imag, index, parts):
    first, span, chans = real.shape
    total = first * span * parts
    freq = jnp.arange(first)
    offset = index * span + jnp.arange(span)
    tw_cos, tw_sin = circle(freq[:, None] * offset[None, :] % total, total)
    tw_cos = tw_cos[:, :, None]
    tw_sin = tw_sin[:, :, None]
    turned_real = (real * tw_cos - imag * tw_sin).reshape(first, span * chans)
    turned_imag = (real * tw_sin + imag * tw_cos).reshape(first, span * chans)
    posit = jnp.arange(parts)
    back_cos, back_sin = circle(posit[:, None] * freq[None, :] % first, first)
    hp = lax.Precision.HIGHEST
    result = jnp.dot(back_cos, turned_real, precision=hp) - jnp.dot(
        back_sin, turned_imag, precision=hp
    )
    return (result / total).reshape(parts, span, chans)


def on_device(gate_query, gate_key, value_in, residues, decay_rate, skip_gain, out_weight):
    parts = lax.axis_size("ctx")
    index = lax.axis_index("ctx")
    length, chans = gate_key.shape
    keyed = gate_key.astype(jnp.float32) * value_in.astype(jnp.float32)
    where = (index * length + jnp.arange(length)).astype(jnp.float32)
    filt = jnp.zeros((length, chans), jnp.float32)
    for mode in range(residues.shape[1]):
        decay = decay_rate[:, mode]
        scale = residues[:, mode] * jnp.sqrt(-jnp.expm1(-2.0 * decay))
        filt = filt + scale[None, :] * jnp.exp(-decay[None, :] * where[:, None])
    keyed_rows, filt_rows = (
        lax.all_to_all(
            keyed.reshape(1, length, chans).astype(jnp.bfloat16),
            "ctx",
            split_axis=1,
            concat_axis=0,
            tiled=True,
        ).astype(jnp.float32),
        lax.all_to_all(
            filt.reshape(1, length, chans).astype(jnp.bfloat16),
            "ctx",
            split_axis=1,
            concat_axis=0,
            tiled=True,
        ).astype(jnp.float32),
    )
    key_re, key_im = cross_forward(keyed_rows, index)
    fil_re, fil_im = cross_forward(filt_rows, index)
    key_re, key_im, fil_re, fil_im = (
        lax.all_to_all(for_sending(key_re), "ctx", split_axis=0, concat_axis=1, tiled=True).astype(
            key_re.dtype
        ),
        lax.all_to_all(for_sending(key_im), "ctx", split_axis=0, concat_axis=1, tiled=True).astype(
            key_im.dtype
        ),
        lax.all_to_all(for_sending(fil_re), "ctx", split_axis=0, concat_axis=1, tiled=True).astype(
            fil_re.dtype
        ),
        lax.all_to_all(for_sending(fil_im), "ctx", split_axis=0, concat_axis=1, tiled=True).astype(
            fil_im.dtype
        ),
    )
    key_re, key_im = local_transform(key_re, key_im, -1.0)
    spec_re, spec_im = local_transform(fil_re, fil_im, -1.0)
    prod_re = key_re * spec_re - key_im * spec_im
    prod_im = key_re * spec_im + key_im * spec_re
    back_re, back_im = local_transform(prod_re, prod_im, 1.0)
    back_re, back_im = (
        lax.all_to_all(for_sending(back_re), "ctx", split_axis=1, concat_axis=0, tiled=True).astype(
            back_re.dtype
        ),
        lax.all_to_all(for_sending(back_im), "ctx", split_axis=1, concat_axis=0, tiled=True).astype(
            back_im.dtype
        ),
    )
    conv_rows = cross_inverse(back_re, back_im, index, parts)
    conv = (
        lax.all_to_all(for_sending(conv_rows), "ctx", split_axis=0, concat_axis=1, tiled=True)
        .astype(conv_rows.dtype)
        .reshape(length, chans)
    )
    mixing = conv + skip_gain[None, :] * keyed
    gated = (gate_query.astype(jnp.float32) * mixing).astype(jnp.bfloat16)
    return (
        lax.psum_scatter(
            lax.dot_general(
                out_weight, gated, (((0,), (1,)), ((), ())), preferred_element_type=jnp.float32
            ).astype(jnp.bfloat16),
            "tp",
            scatter_dimension=0,
            tiled=True,
        )
        .astype(jnp.float32)
        .T.astype(jnp.bfloat16)
    )


def solution(mesh):
    in_specs = (
        P("ctx", "tp"),
        P("ctx", "tp"),
        P("ctx", "tp"),
        P("tp", None),
        P("tp", None),
        P("tp"),
        P("tp", None),
    )
    out_specs = P("ctx", "tp")
    return jax.shard_map(
        on_device, mesh=mesh, in_specs=in_specs, out_specs=out_specs, check_vma=False
    )
```

profile of v0, /device:TPU:32, one launch (start us, length us, event | category | flops | bytes accessed | tf_op | source)
XLA Modules:
  0.0 392.3 jit_solution(4054103656590942700)
XLA Ops:
  14.1 12.0 %all-to-all-start = ((bf16[64,2,2048]{2,1,0:T(2,128)(2,1)}), bf16[64,2,2048]{2,1,0:T(2,128)(2,1)S(1)}, u32[]{:S(2)}, u32[]{:S(2)}) async-start(bf16[64,2,2048]{2,1,0:T(2,128)(2,1)} %reshape.1731), calls=%async_computation | async-start | bytes 1048576 | tf_op jit(solution)/shard_map/all_to_all | solution.py:85
  35.1 7.7 %all-to-all-done = bf16[64,2,2048]{2,1,0:T(2,128)(2,1)S(1)} async-done(((bf16[64,2,2048]{2,1,0:T(2,128)(2,1)}), bf16[64,2,2048]{2,1,0:T(2,128)(2,1)S(1)}, u32[]{:S(2)}, u32[]{:S(2)}) %all-to-all-start) | async-done | bytes 524320 | tf_op jit(solution)/shard_map/all_to_all | solution.py:85
  42.8 7.3 %all-to-all-start.3 = ((bf16[64,2,2048]{2,1,0:T(2,128)(2,1)}), bf16[64,2,2048]{2,1,0:T(2,128)(2,1)}, u32[]{:S(2)}, u32[]{:S(2)}) async-start(bf16[64,2,2048]{2,1,0:T(2,128)(2,1)} %reshape.1733), calls=%async_computation.3 | async-start | bytes 1048576 | tf_op jit(solution)/shard_map/all_to_all | solution.py:92
  57.8 8.8 %all-to-all-done.3 = bf16[64,2,2048]{2,1,0:T(2,128)(2,1)} async-done(((bf16[64,2,2048]{2,1,0:T(2,128)(2,1)}), bf16[64,2,2048]{2,1,0:T(2,128)(2,1)}, u32[]{:S(2)}, u32[]{:S(2)}) %all-to-all-start.3) | async-done | bytes 524320 | tf_op jit(solution)/shard_map/all_to_all | solution.py:92
  66.6 4.0 %reshape.1734 = bf16[256,1,1024]{2,1,0:T(2,128)(2,1)S(1)} reshape(bf16[64,2,2048]{2,1,0:T(2,128)(2,1)} %all-to-all-done.3) | data formatting | bytes 1048576
  70.6 3.8 bitcast_reduce_fusion
  77.4 3.8 subtract_convert_fusion.1
  83.1 6.7 %all-to-all-start.4 = ((bf16[128,4,1024]{2,1,0:T(4,128)(2,1)}), bf16[128,4,1024]{2,1,0:T(4,128)(2,1)S(1)}, u32[]{:S(2)}, u32[]{:S(2)}) async-start(bf16[128,4,1024]{2,1,0:T(4,128)(2,1)} %copy.111), calls=%async_computation.4 | async-start | bytes 2097152 | tf_op jit(solution)/shard_map/all_to_all | solution.py:109
  91.6 26.1 %all-to-all-done.4 = bf16[128,4,1024]{2,1,0:T(4,128)(2,1)S(1)} async-done(((bf16[128,4,1024]{2,1,0:T(4,128)(2,1)}), bf16[128,4,1024]{2,1,0:T(4,128)(2,1)S(1)}, u32[]{:S(2)}, u32[]{:S(2)}) %all-to-all-start.4) | async-done | bytes 1048608 | tf_op jit(solution)/shard_map/all_to_all | solution.py:109
  117.7 6.7 %all-to-all-start.5 = ((bf16[128,4,1024]{2,1,0:T(4,128)(2,1)}), bf16[128,4,1024]{2,1,0:T(4,128)(2,1)}, u32[]{:S(2)}, u32[]{:S(2)}) async-start(bf16[128,4,1024]{2,1,0:T(4,128)(2,1)} %copy.114), calls=%async_computation.5 | async-start | bytes 2097152 | tf_op jit(solution)/shard_map/all_to_all | solution.py:112
  126.2 26.0 %all-to-all-done.5 = bf16[128,4,1024]{2,1,0:T(4,128)(2,1)} async-done(((bf16[128,4,1024]{2,1,0:T(4,128)(2,1)}), bf16[128,4,1024]{2,1,0:T(4,128)(2,1)}, u32[]{:S(2)}, u32[]{:S(2)}) %all-to-all-start.5) | async-done | bytes 1048608 | tf_op jit(solution)/shard_map/all_to_all | solution.py:112
  152.3 6.5 %all-to-all-start.1 = ((bf16[128,4,1024]{2,1,0:T(4,128)(2,1)}), bf16[128,4,1024]{2,1,0:T(4,128)(2,1)S(1)}, u32[]{:S(2)}, u32[]{:S(2)}) async-start(bf16[128,4,1024]{2,1,0:T(4,128)(2,1)} %copy.102), calls=%async_computation.1 | async-start | bytes 2097152 | tf_op jit(solution)/shard_map/all_to_all | solution.py:103
  160.6 26.1 %all-to-all-done.1 = bf16[128,4,1024]{2,1,0:T(4,128)(2,1)S(1)} async-done(((bf16[128,4,1024]{2,1,0:T(4,128)(2,1)}), bf16[128,4,1024]{2,1,0:T(4,128)(2,1)S(1)}, u32[]{:S(2)}, u32[]{:S(2)}) %all-to-all-start.1) | async-done | bytes 1048608 | tf_op jit(solution)/shard_map/all_to_all | solution.py:103
  186.7 6.7 %all-to-all-start.2 = ((bf16[128,4,1024]{2,1,0:T(4,128)(2,1)}), bf16[128,4,1024]{2,1,0:T(4,128)(2,1)}, u32[]{:S(2)}, u32[]{:S(2)}) async-start(bf16[128,4,1024]{2,1,0:T(4,128)(2,1)} %copy.105), calls=%async_computation.2 | async-start | bytes 2097152 | tf_op jit(solution)/shard_map/all_to_all | solution.py:106
  243.8 9.3 %all-to-all-start.6 = ((bf16[2,256,1024]{2,0,1:T(2,128)(2,1)}), bf16[2,256,1024]{2,0,1:T(2,128)(2,1)S(1)}, u32[]{:S(2)}, u32[]{:S(2)}) async-start(bf16[2,256,1024]{2,0,1:T(2,128)(2,1)} %copy.121), calls=%async_computation.6 | async-start | bytes 2097152 | tf_op jit(solution)/shard_map/all_to_all | solution.py:122
  253.2 4.4 %fusion.3 = f32[2,1024,256]{2,1,0:T(8,128)S(1)} fusion(f32[2,1024,256]{2,1,0:T(8,128)} %copy-done.2), kind=kOutput, calls=%fused_computation.7 | convolution fusion | flops 1611530240 | bytes 4194304 | tf_op jit(solution)/shard_map/mb,jbc->jmc/dot_general | solution.py:48
  257.6 3.8 fusion.25
  261.4 3.7 copy.125
  265.1 16.0 %all-to-all-done.6 = bf16[2,256,1024]{2,0,1:T(2,128)(2,1)S(1)} async-done(((bf16[2,256,1024]{2,0,1:T(2,128)(2,1)}), bf16[2,256,1024]{2,0,1:T(2,128)(2,1)S(1)}, u32[]{:S(2)}, u32[]{:S(2)}) %all-to-all-start.6) | async-done | bytes 1048608 | tf_op jit(solution)/shard_map/all_to_all | solution.py:122
  281.1 6.7 %all-to-all-start.7 = ((bf16[2,256,1024]{2,0,1:T(2,128)(2,1)}), bf16[2,256,1024]{2,0,1:T(2,128)(2,1)}, u32[]{:S(2)}, u32[]{:S(2)}) async-start(bf16[2,256,1024]{2,0,1:T(2,128)(2,1)} %copy.125), calls=%async_computation.7 | async-start | bytes 2097152 | tf_op jit(solution)/shard_map/all_to_all | solution.py:125
  300.6 15.0 %all-to-all-done.7 = bf16[2,256,1024]{2,0,1:T(2,128)(2,1)} async-done(((bf16[2,256,1024]{2,0,1:T(2,128)(2,1)}), bf16[2,256,1024]{2,0,1:T(2,128)(2,1)}, u32[]{:S(2)}, u32[]{:S(2)}) %all-to-all-start.7) | async-done | bytes 1048608 | tf_op jit(solution)/shard_map/all_to_all | solution.py:125
  324.8 23.2 %all_to_all.117 = bf16[64,4,1024]{2,1,0:T(4,128)(2,1)S(1)} all-to-all(bf16[64,4,1024]{2,1,0:T(4,128)(2,1)S(1)} %convert_element_type.202), channel_id=1, replica_groups=mesh['ctx'=64,'tp'=4] {'ctx'}, dimensions={0} | all-to-all | bytes 1048576 | tf_op jit(solution)/shard_map/all_to_all | solution.py:131
  348.1 7.1 %fusion = bf16[4096,256]{0,1:T(8,128)(2,1)} fusion(bf16[1024,4096]{1,0:T(8,128)(2,1)} %param.13, f32[256,1024]{1,0:T(8,128)S(1)} %reshape.1721, bf16[256,1024]{1,0:T(8,128)(2,1)S(1)} %copy-done.16, bf16[256,1024]{1,0:T(8,128)(2,1)S(1)} %copy-done.12, bf16[256,1024]{1,0:T(8,128)(2,1)S(1)} %copy-done.13, f32[1024]{0:T(1024)S(1)} %copy-done.17), kind=kOutput, calls=%fused_computation.1 | convolution fusion | flops 2150629376 | bytes 13111296 | tf_op jit(solution)/shard_map/dot_general | solution.py:139
  355.3 29.9 %reduce-scatter.2.cloned.1.call-done = bf16[1024,256]{0,1:T(8,128)(2,1)} async-done(((bf16[4096,256]{0,1:T(8,128)(2,1)}), bf16[1024,256]{0,1:T(8,128)(2,1)}) %reduce-scatter.2.cloned.1.call-update) | async-done | bytes 524304 | tf_op jit(solution)/shard_map/reduce_scatter | solution.py:138
  (98 shorter events, 106.4 us)
Async XLA Ops:
  8.7 17.5 %copy-start.14 = (f32[1024,16]{0,1:T(8,128)S(1)}, f32[1024,16]{0,1:T(8,128)}, u32[]{:S(2)}) copy-start(f32[1024,16]{0,1:T(8,128)} %param.11) | copy-start | bytes 196612
  8.8 17.5 %copy-start.15 = (f32[1024,16]{0,1:T(8,128)S(1)}, f32[1024,16]{0,1:T(8,128)}, u32[]{:S(2)}) copy-start(f32[1024,16]{0,1:T(8,128)} %param.10) | copy-start | bytes 196612
  14.1 28.7 %all-to-all-start = ((bf16[64,2,2048]{2,1,0:T(2,128)(2,1)}), bf16[64,2,2048]{2,1,0:T(2,128)(2,1)S(1)}, u32[]{:S(2)}, u32[]{:S(2)}) async-start(bf16[64,2,2048]{2,1,0:T(2,128)(2,1)} %reshape.1731), calls=%async_computation | async-start | bytes 1048576 | tf_op jit(solution)/shard_map/all_to_all | solution.py:85
  42.8 23.8 %all-to-all-start.3 = ((bf16[64,2,2048]{2,1,0:T(2,128)(2,1)}), bf16[64,2,2048]{2,1,0:T(2,128)(2,1)}, u32[]{:S(2)}, u32[]{:S(2)}) async-start(bf16[64,2,2048]{2,1,0:T(2,128)(2,1)} %reshape.1733), calls=%async_computation.3 | async-start | bytes 1048576 | tf_op jit(solution)/shard_map/all_to_all | solution.py:92
  81.2 8.5 %copy-start.9 = (bf16[128,4,1024]{2,0,1:T(8,128)(2,1)S(1)}, bf16[128,4,1024]{2,0,1:T(8,128)(2,1)}, u32[]{:S(2)}) copy-start(bf16[128,4,1024]{2,0,1:T(8,128)(2,1)} %get-tuple-element.7) | copy-start | bytes 3145732
  83.1 34.6 %all-to-all-start.4 = ((bf16[128,4,1024]{2,1,0:T(4,128)(2,1)}), bf16[128,4,1024]{2,1,0:T(4,128)(2,1)S(1)}, u32[]{:S(2)}, u32[]{:S(2)}) async-start(bf16[128,4,1024]{2,1,0:T(4,128)(2,1)} %copy.111), calls=%async_computation.4 | async-start | bytes 2097152 | tf_op jit(solution)/shard_map/all_to_all | solution.py:109
  89.8 34.6 %copy-start.8 = (bf16[128,4,1024]{2,0,1:T(8,128)(2,1)S(1)}, bf16[128,4,1024]{2,0,1:T(8,128)(2,1)}, u32[]{:S(2)}) copy-start(bf16[128,4,1024]{2,0,1:T(8,128)(2,1)} %get-tuple-element.44) | copy-start | bytes 3145732
  117.7 34.6 %all-to-all-start.5 = ((bf16[128,4,1024]{2,1,0:T(4,128)(2,1)}), bf16[128,4,1024]{2,1,0:T(4,128)(2,1)}, u32[]{:S(2)}, u32[]{:S(2)}) async-start(bf16[128,4,1024]{2,1,0:T(4,128)(2,1)} %copy.114), calls=%async_computation.5 | async-start | bytes 2097152 | tf_op jit(solution)/shard_map/all_to_all | solution.py:112
  124.4 34.4 %copy-start.7 = (bf16[128,4,1024]{2,0,1:T(8,128)(2,1)S(1)}, bf16[128,4,1024]{2,0,1:T(8,128)(2,1)}, u32[]{:S(2)}) copy-start(bf16[128,4,1024]{2,0,1:T(8,128)(2,1)} %get-tuple-element.43) | copy-start | bytes 3145732
  152.3 34.5 %all-to-all-start.1 = ((bf16[128,4,1024]{2,1,0:T(4,128)(2,1)}), bf16[128,4,1024]{2,1,0:T(4,128)(2,1)S(1)}, u32[]{:S(2)}, u32[]{:S(2)}) async-start(bf16[128,4,1024]{2,1,0:T(4,128)(2,1)} %copy.102), calls=%async_computation.1 | async-start | bytes 2097152 | tf_op jit(solution)/shard_map/all_to_all | solution.py:103
  186.7 8.8 %copy-start.10 = (bf16[128,4,1024]{2,1,0:T(4,128)(2,1)}, bf16[128,4,1024]{2,1,0:T(4,128)(2,1)S(1)}, u32[]{:S(2)}) copy-start(bf16[128,4,1024]{2,1,0:T(4,128)(2,1)S(1)} %all-to-all-done.1) | copy-start | bytes 3145732
  186.7 34.6 %all-to-all-start.2 = ((bf16[128,4,1024]{2,1,0:T(4,128)(2,1)}), bf16[128,4,1024]{2,1,0:T(4,128)(2,1)}, u32[]{:S(2)}, u32[]{:S(2)}) async-start(bf16[128,4,1024]{2,1,0:T(4,128)(2,1)} %copy.105), calls=%async_computation.2 | async-start | bytes 2097152 | tf_op jit(solution)/shard_map/all_to_all | solution.py:106
  197.9 5.8 %copy-start.11 = (bf16[128,4,1024]{2,1,0:T(4,128)(2,1)S(1)}, bf16[128,4,1024]{2,1,0:T(4,128)(2,1)}, u32[]{:S(2)}) copy-start(bf16[128,4,1024]{2,1,0:T(4,128)(2,1)} %copy-done.10) | copy-start | bytes 3145732
  229.4 2.1 copy-start.4
  231.5 2.1 copy-start.6
  235.8 2.9 copy-start.2
  243.8 37.3 %all-to-all-start.6 = ((bf16[2,256,1024]{2,0,1:T(2,128)(2,1)}), bf16[2,256,1024]{2,0,1:T(2,128)(2,1)S(1)}, u32[]{:S(2)}, u32[]{:S(2)}) async-start(bf16[2,256,1024]{2,0,1:T(2,128)(2,1)} %copy.121), calls=%async_computation.6 | async-start | bytes 2097152 | tf_op jit(solution)/shard_map/all_to_all | solution.py:122
  281.1 34.6 %all-to-all-start.7 = ((bf16[2,256,1024]{2,0,1:T(2,128)(2,1)}), bf16[2,256,1024]{2,0,1:T(2,128)(2,1)}, u32[]{:S(2)}, u32[]{:S(2)}) async-start(bf16[2,256,1024]{2,0,1:T(2,128)(2,1)} %copy.125), calls=%async_computation.7 | async-start | bytes 2097152 | tf_op jit(solution)/shard_map/all_to_all | solution.py:125
  287.8 97.3 %reduce-scatter.2.cloned.1.call-start = ((), (), s32[]{:S(2)}) async-start(), calls=%async_computation.10 | async-start | bytes 2621440 | tf_op jit(solution)/shard_map/reduce_scatter | solution.py:138
  318.7 2.2 copy-start.1
  324.4 23.7 %copy-start.12 = (bf16[256,1024]{1,0:T(8,128)(2,1)S(1)}, bf16[256,1024]{1,0:T(8,128)(2,1)}, u32[]{:S(2)}) copy-start(bf16[256,1024]{1,0:T(8,128)(2,1)} %param.9) | copy-start | bytes 1572868
  324.4 23.7 %copy-start.13 = (bf16[256,1024]{1,0:T(8,128)(2,1)S(1)}, bf16[256,1024]{1,0:T(8,128)(2,1)}, u32[]{:S(2)}) copy-start(bf16[256,1024]{1,0:T(8,128)(2,1)} %param.8) | copy-start | bytes 1572868
  324.4 23.7 %copy-start.17 = (f32[1024]{0:T(1024)S(1)}, f32[1024]{0:T(1024)}, u32[]{:S(2)}) copy-start(f32[1024]{0:T(1024)} %param.12) | copy-start | bytes 12292
  324.8 23.3 %copy-start.16 = (bf16[256,1024]{1,0:T(8,128)(2,1)S(1)}, bf16[256,1024]{1,0:T(8,128)(2,1)}, u32[]{:S(2)}) copy-start(bf16[256,1024]{1,0:T(8,128)(2,1)} %param.7) | copy-start | bytes 1572868
  (3 other events, 5.3 us)
Sparse Core Ops, SparseCore 0:
  355.4 29.7 reduce-scatter.1
where the time goes:
time: 400 us; the launch traced here: 392 us
  waiting for transfers between devices  157 us (39%)
  local copies, waits for them, and re-layouts  67.5 us (17%)
  starting transfers between devices  62 us (16%)
  matrix products  53.6 us (13%)
  blocking collectives  23.2 us (6%)
  other arithmetic  15.1 us (4%)
  between operations  14.3 us (4%)
    reduce_scatter x1, waiting for transfers between devices, on_device(): lax.psum_scatter(lax.dot_general(out_weight, gated, (((0,), (1,)), ((), (...  29.9 us
    all_to_all x1, waiting for transfers between devices, on_device(): lax.all_to_all(for_sending(key_re), 'ctx', split_axis=0, concat_axis=1, t...  26.1 us
    all_to_all x1, waiting for transfers between devices, on_device(): lax.all_to_all(for_sending(fil_re), 'ctx', split_axis=0, concat_axis=1, t...  26.1 us
    all_to_all x1, waiting for transfers between devices, on_device(): lax.all_to_all(for_sending(fil_im), 'ctx', split_axis=0, concat_axis=1, t...  26 us
    all_to_all x1, blocking collectives, on_device(): lax.all_to_all(for_sending(conv_rows), 'ctx', split_axis=0, concat_axis=1...  23.2 us
    all_to_all x1, waiting for transfers between devices, on_device(): lax.all_to_all(for_sending(back_re), 'ctx', split_axis=1, concat_axis=0,...  16 us
    all_to_all x1, waiting for transfers between devices, on_device(): lax.all_to_all(for_sending(back_im), 'ctx', split_axis=1, concat_axis=0,...  15 us
    convert_element_type x7, local copies, waits for them, and re-layouts, short(): return part.astype(jnp.bfloat16) if part.dtype == jnp.float32 else part  13.4 us
  transfers between devices with their start and end apart: 9, of which 9 were waited for; matrix products, arithmetic and copies ran while one was open for 19% of the time, Pallas kernels for 0%

commit v1 on v0

v1 whole, which is shorter than its diff:
```python
import functools

import jax
import jax.numpy as jnp
from jax import lax
from jax.experimental import pallas as pl
from jax.experimental.pallas import tpu as pltpu
from jax.sharding import PartitionSpec as P

MODES = 16
LANES = 128
SUB = 8
ROWS = 16


def local_kernel(key_ref, value_ref, decay_ref, scale_ref, skip_ref, local_ref, state_ref, keyed_ref):
    groups = key_ref.shape[1] // LANES
    span = groups * SUB
    length = key_ref.shape[0]
    step = [jnp.exp(-decay_ref[r]) for r in range(MODES)]
    scale = [scale_ref[r] for r in range(MODES)]
    skip = skip_ref[...]

    def block(i, held):
        rows = pl.ds(pl.multiple_of(i * ROWS, ROWS), ROWS)
        keyed = key_ref[rows, :].astype(jnp.float32) * value_ref[rows, :].astype(jnp.float32)
        for half in range(ROWS // SUB):
            base = (i * (ROWS // SUB) + half) * span
            for g in range(groups):
                keyed_ref[pl.ds(pl.multiple_of(base + g * SUB, SUB), SUB), :] = keyed[
                    half * SUB : (half + 1) * SUB, g * LANES : (g + 1) * LANES
                ]
        for half in range(ROWS // SUB):
            base = (i * (ROWS // SUB) + half) * span
            for s in range(SUB):
                at = pl.ds(base + s, groups, stride=SUB)
                now = keyed_ref[at, :]
                held = [a * h + now for a, h in zip(step, held)]
                terms = [c * h for c, h in zip(scale, held)] + [skip * now]
                while len(terms) > 1:
                    terms = [sum(terms[j : j + 2]) for j in range(0, len(terms), 2)]
                local_ref[at, :] = terms[0]
        return held

    held = lax.fori_loop(0, length // ROWS, block, [jnp.zeros((groups, LANES), jnp.float32)] * MODES)
    for r in range(MODES):
        state_ref[r] = held[r]


def local_part(gate_key, value_in, decay, scale, skip):
    length, chans = gate_key.shape
    groups = chans // LANES
    return pl.pallas_call(
        local_kernel,
        out_shape=(
            jax.ShapeDtypeStruct((length * groups, LANES), jnp.float32),
            jax.ShapeDtypeStruct((MODES, groups, LANES), jnp.float32),
        ),
        scratch_shapes=[pltpu.VMEM((length * groups, LANES), jnp.float32)],
        compiler_params=pltpu.CompilerParams(vmem_limit_bytes=32 * 2**20),
        cost_estimate=pl.CostEstimate(flops=8 * 2**20, bytes_accessed=2 * 2**20, transcendentals=0),
    )(gate_key, value_in, decay, scale, skip)


def carry_kernel(place_ref, local_ref, query_ref, decay_ref, scale_ref, carry_ref, weight_ref,
                 gated_ref, part_ref, tail_ref, weight_buf, sem):
    length, chans = query_ref.shape
    groups = chans // LANES
    span = groups * SUB
    width = part_ref.shape[1]
    fetch = pltpu.make_async_copy(
        weight_ref.at[:, pl.ds(pl.multiple_of(place_ref[0] * width, width), width)], weight_buf, sem
    )
    fetch.start()
    step = [jnp.exp(-decay_ref[r]) for r in range(MODES)]
    start = [scale_ref[r] * step[r] * carry_ref[r] for r in range(MODES)]

    def block(i, held):
        rows = pl.ds(pl.multiple_of(i * ROWS, ROWS), ROWS)
        for half in range(ROWS // SUB):
            for s in range(SUB):
                terms = held
                while len(terms) > 1:
                    terms = [sum(terms[j : j + 2]) for j in range(0, len(terms), 2)]
                tail_ref[pl.ds(half * span + s, groups, stride=SUB), :] = terms[0]
                held = [a * h for a, h in zip(step, held)]
        for g in range(groups):
            parts = []
            for half in range(ROWS // SUB):
                base = (i * (ROWS // SUB) + half) * span + g * SUB
                parts.append(
                    local_ref[pl.ds(pl.multiple_of(base, SUB), SUB), :]
                    + tail_ref[half * span + g * SUB : half * span + (g + 1) * SUB, :]
                )
            mixing = jnp.concatenate(parts, axis=0)
            cols = slice(g * LANES, (g + 1) * LANES)
            gated_ref[rows, cols] = (query_ref[rows, cols].astype(jnp.float32) * mixing).astype(
                jnp.bfloat16
            )
        return held

    lax.fori_loop(0, length // ROWS, block, start)
    fetch.wait()
    part_ref[...] = jnp.dot(
        gated_ref[...], weight_buf[...], preferred_element_type=jnp.float32
    ).astype(jnp.bfloat16)


VMEM = pl.BlockSpec(memory_space=pltpu.VMEM)


def carry_part(place, local, gate_query, decay, scale, carry, weight):
    length, chans = gate_query.shape
    groups = chans // LANES
    width = weight.shape[1] // 4
    return pl.pallas_call(
        carry_kernel,
        out_shape=(
            jax.ShapeDtypeStruct((length, chans), jnp.bfloat16),
            jax.ShapeDtypeStruct((length, width), jnp.bfloat16),
        ),
        in_specs=[pl.BlockSpec(memory_space=pltpu.SMEM)] + [VMEM] * 5 + [pl.BlockSpec(memory_space=pl.ANY)],
        out_specs=(VMEM, VMEM),
        scratch_shapes=[
            pltpu.VMEM((ROWS * groups, LANES), jnp.float32),
            pltpu.VMEM((chans, width), jnp.bfloat16),
            pltpu.SemaphoreType.DMA,
        ],
        compiler_params=pltpu.CompilerParams(vmem_limit_bytes=32 * 2**20),
        cost_estimate=pl.CostEstimate(flops=2**30, bytes_accessed=5 * 2**20, transcendentals=0),
    )(place, local, gate_query, decay, scale, carry, weight)


def project_kernel(place_ref, gated_ref, weight_ref, out_ref):
    out_ref[...] = jnp.dot(gated_ref[...], weight_ref[...], preferred_element_type=jnp.float32)[None]


def project(places, gated, weight):
    length, chans = gated.shape
    width = weight.shape[1] // 4
    count = places.shape[0]
    return pl.pallas_call(
        project_kernel,
        out_shape=jax.ShapeDtypeStruct((count, length, width), jnp.float32),
        grid_spec=pltpu.PrefetchScalarGridSpec(
            num_scalar_prefetch=1,
            grid=(count,),
            in_specs=[
                pl.BlockSpec((length, chans), lambda i, p: (0, 0)),
                pl.BlockSpec((chans, width), lambda i, p: (0, p[i])),
            ],
            out_specs=pl.BlockSpec((1, length, width), lambda i, p: (i, 0, 0)),
        ),
        compiler_params=pltpu.CompilerParams(vmem_limit_bytes=32 * 2**20),
        cost_estimate=pl.CostEstimate(
            flops=2 * count * length * chans * width,
            bytes_accessed=2 * count * chans * width,
            transcendentals=0,
        ),
    )(places, gated, weight)


def scan_over_ctx(state, decay, length, index):
    groups = lax.axis_size("ctx")

    def power(blocks):
        blocks = jnp.asarray(blocks)
        return jnp.where(blocks >= 0, jnp.exp(-decay * (length * jnp.maximum(blocks, 0)).astype(jnp.float32)), 0.0)

    total, before = state, jnp.zeros_like(state)
    span = 1
    for bits in (1, 2, 1, 2):
        members = 1 << bits
        mine = index // span % members
        inside = index % span
        sent = total.astype(jnp.bfloat16)
        got = [(0, total)]
        for k in range(1, members):
            pairs = [(i, i ^ (k * span)) for i in range(groups)]
            got.append((k, lax.ppermute(sent, "ctx", pairs).astype(jnp.float32)))
        for k, theirs in got[1:]:
            other = mine ^ k
            before = before + theirs * power(
                jnp.where(other < mine, (mine - 1 - other) * span + inside, -1)
            )
        total = sum(theirs * power((members - 1 - (mine ^ k)) * span) for k, theirs in got)
        span *= members
    return before


def on_device(gate_query, gate_key, value_in, residues, decay_rate, skip_gain, out_weight):
    index = lax.axis_index("ctx")
    mine = lax.axis_index("tp")
    length, chans = gate_key.shape
    groups = chans // LANES
    decay = decay_rate.T.reshape(MODES, groups, LANES)
    scale = residues.T.reshape(MODES, groups, LANES) * jnp.sqrt(-jnp.expm1(-2.0 * decay))
    skip = skip_gain.reshape(groups, LANES)
    local, state = local_part(gate_key, value_in, decay, scale, skip)
    carry = scan_over_ctx(state, decay, length, index)

    ring = lax.axis_size("tp")
    after, prior = (mine + 1) % ring, (mine + ring - 1) % ring
    far = (mine + 2) % ring
    forth = [(i, (i + 1) % ring) for i in range(ring)]
    back = [(i, (i + ring - 1) % ring) for i in range(ring)]
    half = length // 2
    gated, far_part = carry_part(far[None], local, gate_query, decay, scale, carry, out_weight)
    far_a = lax.ppermute(far_part[:half], "tp", forth)
    far_b = lax.ppermute(far_part[half:], "tp", back)
    parts = project(jnp.stack([after, prior, mine]), gated, out_weight)
    near_b = lax.ppermute(parts[0, half:].astype(jnp.bfloat16), "tp", forth)
    near_a = lax.ppermute(parts[1, :half].astype(jnp.bfloat16), "tp", back)
    both_a = lax.ppermute((parts[0, :half] + far_a.astype(jnp.float32)).astype(jnp.bfloat16), "tp", forth)
    both_b = lax.ppermute((parts[1, half:] + far_b.astype(jnp.float32)).astype(jnp.bfloat16), "tp", back)
    first = parts[2, :half] + near_a.astype(jnp.float32) + both_a.astype(jnp.float32)
    second = parts[2, half:] + near_b.astype(jnp.float32) + both_b.astype(jnp.float32)
    return jnp.concatenate([first, second]).astype(jnp.bfloat16)


def solution(mesh):
    in_specs = (
        P("ctx", "tp"),
        P("ctx", "tp"),
        P("ctx", "tp"),
        P("tp", None),
        P("tp", None),
        P("tp"),
        P("tp", None),
    )
    return jax.shard_map(
        on_device, mesh=mesh, in_specs=in_specs, out_specs=P("ctx", "tp"), check_vma=False
    )
```

time: 400 us -> 65.3 us (0.16); the launches traced: 392 us -> 64.4 us
  waiting for transfers between devices: 157 us -> 23 us
  local copies, waits for them, and re-layouts: 67.5 us -> 7.99 us
  matrix products: 53.6 us -> 0 us
  starting transfers between devices: 62 us -> 23.2 us
  blocking collectives: 23.2 us -> 0 us
  between operations: 14.3 us -> 0.29 us
  other arithmetic: 15.1 us -> 1.88 us
  Pallas kernels: 0 us -> 8.05 us
    all_to_all x8 -> x0, waiting for transfers between devices: 127 us -> none  [the longest x1 26.1 us: on_device(): lax.all_to_all(for_sending(key_re), 'ctx', split_axis=0, concat_axis=1, t...]
    all_to_all x8 -> x0, starting transfers between devices: 62 us -> none  [the longest x1 12 us: on_device(): lax.all_to_all(keyed.reshape(1, length, chans).astype(jnp.bfloat16), 'ctx...]
    dot_general x19 -> x0, matrix products: 53.6 us -> none  [the longest x3 9.73 us: local_transform(): jnp.einsum('mb,jbc->jmc', tab_cos, imag, precision=hp)]
    reduce_scatter x1 -> x0, waiting for transfers between devices: 29.9 us -> none  [on_device(): lax.psum_scatter(lax.dot_general(out_weight, gated, (((0,), (1,)), ((), (...]
    all_to_all x10 -> x0, local copies, waits for them, and re-layouts: 27.8 us -> none  [the longest x2 6.1 us: on_device(): lax.all_to_all(for_sending(key_im), 'ctx', split_axis=0, concat_axis=1, t...]
    ppermute x0 -> x14, starting transfers between devices: none -> 23.2 us  [the longest x8 12.7 us: scan_over_ctx(): got.append((k, lax.ppermute(sent, 'ctx', pairs).astype(jnp.float32)))]
    all_to_all x1 -> x0, blocking collectives: 23.2 us -> none  [on_device(): lax.all_to_all(for_sending(conv_rows), 'ctx', split_axis=0, concat_axis=1...]
    ppermute x0 -> x14, waiting for transfers between devices: none -> 23 us  [the longest x8 14.5 us: scan_over_ctx(): got.append((k, lax.ppermute(sent, 'ctx', pairs).astype(jnp.float32)))]
  transfers between devices with their start and end apart: 9 -> 14, of which waited for: 9 -> 9; matrix products, arithmetic and copies ran while one was open for 19% -> 1% of each run, Pallas kernels for 0% -> 5%
where the time goes in v1:
time: 65.3 us; the launch traced here: 64.4 us
  starting transfers between devices  23.2 us (36%)
  waiting for transfers between devices  23 us (35%)
  Pallas kernels  8.05 us (12%)
  local copies, waits for them, and re-layouts  7.99 us (12%)
  other arithmetic  1.88 us (3%)
    ppermute x8, waiting for transfers between devices, scan_over_ctx(): got.append((k, lax.ppermute(sent, 'ctx', pairs).astype(jnp.float32)))  14.5 us
    ppermute x8, starting transfers between devices, scan_over_ctx(): got.append((k, lax.ppermute(sent, 'ctx', pairs).astype(jnp.float32)))  12.7 us
    unnamed x14, local copies, waits for them, and re-layouts  7.92 us
    ppermute x1, waiting for transfers between devices, on_device(): lax.ppermute((parts[1, half:] + far_b.astype(jnp.float32)).astype(jnp.bfl...  3.86 us
    pallas_call x1, Pallas kernels, project(): pl.pallas_call(project_kernel, out_shape=jax.ShapeDtypeStruct((count, len...  3.14 us
    ppermute x1, waiting for transfers between devices, on_device(): lax.ppermute((parts[0, :half] + far_a.astype(jnp.float32)).astype(jnp.bfl...  2.89 us
    pallas_call x1, Pallas kernels, local_part(): pl.pallas_call(local_kernel, out_shape=(jax.ShapeDtypeStruct((length * gr...  2.61 us
    ppermute x1, starting transfers between devices, on_device(): near_b = lax.ppermute(parts[0, half:].astype(jnp.bfloat16), 'tp', forth)  2.48 us
  transfers between devices with their start and end apart: 14, of which 9 were waited for; matrix products, arithmetic and copies ran while one was open for 1% of the time, Pallas kernels for 5%

profile of v1, /device:TPU:32, one launch (start us, length us, event | category | flops | bytes accessed | tf_op | source)
XLA Modules:
  0.0 64.4 jit_solution(5976315507422004416)
XLA Ops:
  1.8 1.0 %copy-done.3 = bf16[256,1024]{1,0:T(8,128)(2,1)S(1)} copy-done((bf16[256,1024]{1,0:T(8,128)(2,1)S(1)}, bf16[256,1024]{1,0:T(8,128)(2,1)}, u32[]{:S(2)}) %copy-start.3) | copy-done | bytes 524312
  2.9 1.0 %copy-done.4 = bf16[256,1024]{1,0:T(8,128)(2,1)S(1)} copy-done((bf16[256,1024]{1,0:T(8,128)(2,1)S(1)}, bf16[256,1024]{1,0:T(8,128)(2,1)}, u32[]{:S(2)}) %copy-start.4) | copy-done | bytes 524312
  4.6 2.6 %shard_map.73 = (f32[2048,128]{1,0:T(8,128)S(1)}, f32[16,8,128]{2,1,0:T(8,128)S(1)}) custom-call(bf16[256,1024]{1,0:T(8,128)(2,1)S(1)} %copy-done.3, bf16[256,1024]{1,0:T(8,128)(2,1)S(1)} %copy-done.4, f32[16,8,128]{2,1,0:T(8,128)S(1)} %bitcast.50, f32[16,8,128]{2,1,0:T(8,128)S(1)} %bitcast_multiply_fusion.scale_ref, f32[8,128]{1,0:T(8,128)S(1)} %bitcast.52), custom_call_target="tpu_custom_call" | custom-call | flops 8388608 | bytes 2097152 | tf_op jit(solution)/shard_map/pallas_call | solution.py:53
  7.4 1.2 %collective-permute-done = bf16[16,8,128]{2,1,0:T(8,128)(2,1)S(1)} collective-permute-done((bf16[16,8,128]{2,1,0:T(8,128)(2,1)S(1)}, bf16[16,8,128]{2,1,0:T(8,128)(2,1)S(1)}, u32[]{:S(2)}, u32[]{:S(2)}) %collective-permute-start) | collective-permute-done | bytes 32800 | tf_op jit(solution)/shard_map/ppermute | solution.py:180
  8.6 3.1 %collective-permute-start.3 = (bf16[16,8,128]{2,1,0:T(8,128)(2,1)S(1)}, bf16[16,8,128]{2,1,0:T(8,128)(2,1)S(1)}, u32[]{:S(2)}, u32[]{:S(2)}) collective-permute-start(bf16[16,8,128]{2,1,0:T(8,128)(2,1)S(1)} %fusion.23), channel_id=1, source_target_pairs={{0,24},{4,28},{8,16},{12,20},{16,8},{20,12},{24,0},{28,4},{32,56},... | collective-permute-start | bytes 98312 | tf_op jit(solution)/shard_map/ppermute | solution.py:180
  12.8 1.0 %collective-permute-done.3 = bf16[16,8,128]{2,1,0:T(8,128)(2,1)S(1)} collective-permute-done((bf16[16,8,128]{2,1,0:T(8,128)(2,1)S(1)}, bf16[16,8,128]{2,1,0:T(8,128)(2,1)S(1)}, u32[]{:S(2)}, u32[]{:S(2)}) %collective-permute-start.3) | collective-permute-done | bytes 32800 | tf_op jit(solution)/shard_map/ppermute | solution.py:180
  13.8 3.3 %collective-permute-done.2 = bf16[16,8,128]{2,1,0:T(8,128)(2,1)S(1)} collective-permute-done((bf16[16,8,128]{2,1,0:T(8,128)(2,1)S(1)}, bf16[16,8,128]{2,1,0:T(8,128)(2,1)S(1)}, u32[]{:S(2)}, u32[]{:S(2)}) %collective-permute-start.2) | collective-permute-done | bytes 32800 | tf_op jit(solution)/shard_map/ppermute | solution.py:180
  17.4 3.8 %collective-permute-done.4 = bf16[16,8,128]{2,1,0:T(8,128)(2,1)S(1)} collective-permute-done((bf16[16,8,128]{2,1,0:T(8,128)(2,1)S(1)}, bf16[16,8,128]{2,1,0:T(8,128)(2,1)S(1)}, u32[]{:S(2)}, u32[]{:S(2)}) %collective-permute-start.4) | collective-permute-done | bytes 32800 | tf_op jit(solution)/shard_map/ppermute | solution.py:180
  21.2 5.8 %collective-permute-start.7 = (bf16[16,8,128]{2,1,0:T(8,128)(2,1)S(1)}, bf16[16,8,128]{2,1,0:T(8,128)(2,1)S(1)}, u32[]{:S(2)}, u32[]{:S(2)}) collective-permute-start(bf16[16,8,128]{2,1,0:T(8,128)(2,1)S(1)} %fusion.22), channel_id=1, source_target_pairs={{0,192},{4,196},{8,200},{12,204},{16,208},{20,212},{24,216},{28,22... | collective-permute-start | bytes 98312 | tf_op jit(solution)/shard_map/ppermute | solution.py:180
  27.0 1.2 %collective-permute-start.6 = (bf16[16,8,128]{2,1,0:T(8,128)(2,1)S(1)}, bf16[16,8,128]{2,1,0:T(8,128)(2,1)S(1)}, u32[]{:S(2)}, u32[]{:S(2)}) collective-permute-start(bf16[16,8,128]{2,1,0:T(8,128)(2,1)S(1)} %fusion.22), channel_id=1, source_target_pairs={{0,128},{4,132},{8,136},{12,140},{16,144},{20,148},{24,152},{28,15... | collective-permute-start | bytes 98312 | tf_op jit(solution)/shard_map/ppermute | solution.py:180
  28.2 1.3 %collective-permute-start.5 = (bf16[16,8,128]{2,1,0:T(8,128)(2,1)S(1)}, bf16[16,8,128]{2,1,0:T(8,128)(2,1)S(1)}, u32[]{:S(2)}, u32[]{:S(2)}) collective-permute-start(bf16[16,8,128]{2,1,0:T(8,128)(2,1)S(1)} %fusion.22), channel_id=1, source_target_pairs={{0,64},{4,68},{8,72},{12,76},{16,80},{20,84},{24,88},{28,92},{32,9... | collective-permute-start | bytes 98312 | tf_op jit(solution)/shard_map/ppermute | solution.py:180
  29.7 5.2 %collective-permute-done.6 = bf16[16,8,128]{2,1,0:T(8,128)(2,1)S(1)} collective-permute-done((bf16[16,8,128]{2,1,0:T(8,128)(2,1)S(1)}, bf16[16,8,128]{2,1,0:T(8,128)(2,1)S(1)}, u32[]{:S(2)}, u32[]{:S(2)}) %collective-permute-start.6) | collective-permute-done | bytes 32800 | tf_op jit(solution)/shard_map/ppermute | solution.py:180
  35.0 3.4 %copy-done = bf16[1024,4096]{1,0:T(8,128)(2,1)S(1)} copy-done((bf16[1024,4096]{1,0:T(8,128)(2,1)S(1)}, bf16[1024,4096]{1,0:T(8,128)(2,1)}, u32[]{:S(2)}) %copy-start) | copy-done | bytes 8388632
  38.4 2.3 %shard_map.74 = (bf16[256,1024]{1,0:T(8,128)(2,1)S(1)}, bf16[256,1024]{1,0:T(8,128)(2,1)S(1)}) custom-call(s32[1]{0:T(128)} %bitcast.3.place_ref, f32[2048,128]{1,0:T(8,128)S(1)} %get-tuple-element.9.local_ref, bf16[256,1024]{1,0:T(8,128)(2,1)S(1)} %copy-done.2, f32[16,8,128]{2,1,0:T(8,128)S(1)} %bitcast.51, ...), custom_call_target="tpu_custom_call" | custom-call | flops 1073741824 | bytes 5242880 | tf_op jit(solution)/shard_map/pallas_call | solution.py:116
  40.7 1.6 %collective-permute-start.9 = (bf16[128,1024]{1,0:T(8,128)(2,1)S(1)}, bf16[128,1024]{1,0:T(8,128)(2,1)S(1)}, u32[]{:S(2)}, u32[]{:S(2)}) collective-permute-start(bf16[128,1024]{1,0:T(8,128)(2,1)S(1)} %get-tuple-element.19), channel_id=1, source_target_pairs={{0,1},{1,2},{2,3},{3,0},{4,5},{5,6},{6,7},{7,4},{8,9},{9,10},{10,1... | collective-permute-start | bytes 786440 | tf_op jit(solution)/shard_map/ppermute | solution.py:209
  42.3 1.8 %collective-permute-start.12 = (bf16[128,1024]{1,0:T(8,128)(2,1)S(1)}, bf16[128,1024]{1,0:T(8,128)(2,1)S(1)}, u32[]{:S(2)}, u32[]{:S(2)}) collective-permute-start(bf16[128,1024]{1,0:T(8,128)(2,1)S(1)} %get-tuple-element.20), channel_id=1, source_target_pairs={{0,3},{1,0},{2,1},{3,2},{4,7},{5,4},{6,5},{7,6},{8,11},{9,8},{10,9... | collective-permute-start | bytes 786440 | tf_op jit(solution)/shard_map/ppermute | solution.py:210
  44.1 3.1 %shard_map.75 = f32[3,256,1024]{2,1,0:T(8,128)S(1)} custom-call(s32[3]{0:T(128)S(1)} %pad_add_fusion.place_ref, bf16[256,1024]{1,0:T(8,128)(2,1)S(1)} %get-tuple-element.11.gated_ref, bf16[1024,4096]{1,0:T(8,128)(2,1)S(1)} %copy-done.1), custom_call_target="tpu_custom_call" | custom-call | flops 1610612736 | bytes 6291456 | tf_op jit(solution)/shard_map/pallas_call | solution.py:142
  47.5 1.6 %collective-permute-start.8 = (bf16[128,1024]{1,0:T(8,128)(2,1)S(1)}, bf16[128,1024]{1,0:T(8,128)(2,1)S(1)}, u32[]{:S(2)}, u32[]{:S(2)}) collective-permute-start(bf16[128,1024]{1,0:T(8,128)(2,1)S(1)} %get-tuple-element.17), channel_id=1, source_target_pairs={{0,3},{1,0},{2,1},{3,2},{4,7},{5,4},{6,5},{7,6},{8,11},{9,8},{10,9... | collective-permute-start | bytes 786440 | tf_op jit(solution)/shard_map/ppermute | solution.py:213
  49.2 1.1 %collective-permute-start.10 = (bf16[128,1024]{1,0:T(8,128)(2,1)S(1)}, bf16[128,1024]{1,0:T(8,128)(2,1)S(1)}, u32[]{:S(2)}, u32[]{:S(2)}) collective-permute-start(bf16[128,1024]{1,0:T(8,128)(2,1)S(1)} %fusion.6), channel_id=1, source_target_pairs={{0,1},{1,2},{2,3},{3,0},{4,5},{5,6},{6,7},{7,4},{8,9},{9,10},{10,1... | collective-permute-start | bytes 786440 | tf_op jit(solution)/shard_map/ppermute | solution.py:214
  50.3 2.5 %collective-permute-start.11 = (bf16[128,1024]{1,0:T(8,128)(2,1)S(1)}, bf16[128,1024]{1,0:T(8,128)(2,1)S(1)}, u32[]{:S(2)}, u32[]{:S(2)}) collective-permute-start(bf16[128,1024]{1,0:T(8,128)(2,1)S(1)} %get-tuple-element.18), channel_id=1, source_target_pairs={{0,1},{1,2},{2,3},{3,0},{4,5},{5,6},{6,7},{7,4},{8,9},{9,10},{10,1... | collective-permute-start | bytes 786440 | tf_op jit(solution)/shard_map/ppermute | solution.py:212
  52.8 1.1 %collective-permute-done.8 = bf16[128,1024]{1,0:T(8,128)(2,1)S(1)} collective-permute-done((bf16[128,1024]{1,0:T(8,128)(2,1)S(1)}, bf16[128,1024]{1,0:T(8,128)(2,1)S(1)}, u32[]{:S(2)}, u32[]{:S(2)}) %collective-permute-start.8) | collective-permute-done | bytes 262176 | tf_op jit(solution)/shard_map/ppermute | solution.py:213
  53.9 2.9 %collective-permute-done.10 = bf16[128,1024]{1,0:T(8,128)(2,1)S(1)} collective-permute-done((bf16[128,1024]{1,0:T(8,128)(2,1)S(1)}, bf16[128,1024]{1,0:T(8,128)(2,1)S(1)}, u32[]{:S(2)}, u32[]{:S(2)}) %collective-permute-start.10) | collective-permute-done | bytes 262176 | tf_op jit(solution)/shard_map/ppermute | solution.py:214
  57.1 2.0 %collective-permute-start.13 = (bf16[128,1024]{1,0:T(8,128)(2,1)S(1)}, bf16[128,1024]{1,0:T(8,128)(2,1)S(1)}, u32[]{:S(2)}, u32[]{:S(2)}) collective-permute-start(bf16[128,1024]{1,0:T(8,128)(2,1)S(1)} %get-tuple-element.16), channel_id=1, source_target_pairs={{0,3},{1,0},{2,1},{3,2},{4,7},{5,4},{6,5},{7,6},{8,11},{9,8},{10,9... | collective-permute-start | bytes 786440 | tf_op jit(solution)/shard_map/ppermute | solution.py:215
  59.6 3.9 %collective-permute-done.13 = bf16[128,1024]{1,0:T(8,128)(2,1)S(1)} collective-permute-done((bf16[128,1024]{1,0:T(8,128)(2,1)S(1)}, bf16[128,1024]{1,0:T(8,128)(2,1)S(1)}, u32[]{:S(2)}, u32[]{:S(2)}) %collective-permute-start.13) | collective-permute-done | bytes 262176 | tf_op jit(solution)/shard_map/ppermute | solution.py:215
  (35 shorter events, 6.4 us)
Async XLA Ops:
  0.0 35.0 %copy-start.2 = (bf16[256,1024]{1,0:T(8,128)(2,1)S(1)}, bf16[256,1024]{1,0:T(8,128)(2,1)}, u32[]{:S(2)}) copy-start(bf16[256,1024]{1,0:T(8,128)(2,1)} %query_ref.1) | copy-start | bytes 1572868
  1.8 1.0 %copy-start.3 = (bf16[256,1024]{1,0:T(8,128)(2,1)S(1)}, bf16[256,1024]{1,0:T(8,128)(2,1)}, u32[]{:S(2)}) copy-start(bf16[256,1024]{1,0:T(8,128)(2,1)} %key_ref.1) | copy-start | bytes 1572868
  2.9 1.0 %copy-start.4 = (bf16[256,1024]{1,0:T(8,128)(2,1)S(1)}, bf16[256,1024]{1,0:T(8,128)(2,1)}, u32[]{:S(2)}) copy-start(bf16[256,1024]{1,0:T(8,128)(2,1)} %value_ref.1) | copy-start | bytes 1572868
  3.9 0.7 %copy-start.5 = (f32[1024]{0:T(1024)S(1)}, f32[1024]{0:T(1024)}, u32[]{:S(2)}) copy-start(f32[1024]{0:T(1024)} %param.12) | copy-start | bytes 12292
  7.2 1.3 %collective-permute-start = (bf16[16,8,128]{2,1,0:T(8,128)(2,1)S(1)}, bf16[16,8,128]{2,1,0:T(8,128)(2,1)S(1)}, u32[]{:S(2)}, u32[]{:S(2)}) collective-permute-start(bf16[16,8,128]{2,1,0:T(8,128)(2,1)S(1)} %convert_element_type.117), channel_id=1, source_target_pairs={{0,4},{4,0},{8,12},{12,8},{16,20},{20,16},{24,28},{28,24},{32,36},... | collective-permute-start | bytes 98312 | tf_op jit(solution)/shard_map/ppermute | solution.py:180
  8.6 5.2 %collective-permute-start.3 = (bf16[16,8,128]{2,1,0:T(8,128)(2,1)S(1)}, bf16[16,8,128]{2,1,0:T(8,128)(2,1)S(1)}, u32[]{:S(2)}, u32[]{:S(2)}) collective-permute-start(bf16[16,8,128]{2,1,0:T(8,128)(2,1)S(1)} %fusion.23), channel_id=1, source_target_pairs={{0,24},{4,28},{8,16},{12,20},{16,8},{20,12},{24,0},{28,4},{32,56},... | collective-permute-start | bytes 98312 | tf_op jit(solution)/shard_map/ppermute | solution.py:180
  11.7 5.4 %collective-permute-start.2 = (bf16[16,8,128]{2,1,0:T(8,128)(2,1)S(1)}, bf16[16,8,128]{2,1,0:T(8,128)(2,1)S(1)}, u32[]{:S(2)}, u32[]{:S(2)}) collective-permute-start(bf16[16,8,128]{2,1,0:T(8,128)(2,1)S(1)} %fusion.23), channel_id=1, source_target_pairs={{0,16},{4,20},{8,24},{12,28},{16,0},{20,4},{24,8},{28,12},{32,48},... | collective-permute-start | bytes 98312 | tf_op jit(solution)/shard_map/ppermute | solution.py:180
  12.3 4.8 %collective-permute-start.1 = (bf16[16,8,128]{2,1,0:T(8,128)(2,1)S(1)}, bf16[16,8,128]{2,1,0:T(8,128)(2,1)S(1)}, u32[]{:S(2)}, u32[]{:S(2)}) collective-permute-start(bf16[16,8,128]{2,1,0:T(8,128)(2,1)S(1)} %fusion.23), channel_id=1, source_target_pairs={{0,8},{4,12},{8,0},{12,4},{16,24},{20,28},{24,16},{28,20},{32,40},... | collective-permute-start | bytes 98312 | tf_op jit(solution)/shard_map/ppermute | solution.py:180
  17.2 4.0 %collective-permute-start.4 = (bf16[16,8,128]{2,1,0:T(8,128)(2,1)S(1)}, bf16[16,8,128]{2,1,0:T(8,128)(2,1)S(1)}, u32[]{:S(2)}, u32[]{:S(2)}) collective-permute-start(bf16[16,8,128]{2,1,0:T(8,128)(2,1)S(1)} %get-tuple-element.13), channel_id=1, source_target_pairs={{0,32},{4,36},{8,40},{12,44},{16,48},{20,52},{24,56},{28,60},{32,0... | collective-permute-start | bytes 98312 | tf_op jit(solution)/shard_map/ppermute | solution.py:180
  21.2 8.4 %collective-permute-start.7 = (bf16[16,8,128]{2,1,0:T(8,128)(2,1)S(1)}, bf16[16,8,128]{2,1,0:T(8,128)(2,1)S(1)}, u32[]{:S(2)}, u32[]{:S(2)}) collective-permute-start(bf16[16,8,128]{2,1,0:T(8,128)(2,1)S(1)} %fusion.22), channel_id=1, source_target_pairs={{0,192},{4,196},{8,200},{12,204},{16,208},{20,212},{24,216},{28,22... | collective-permute-start | bytes 98312 | tf_op jit(solution)/shard_map/ppermute | solution.py:180
  27.0 7.8 %collective-permute-start.6 = (bf16[16,8,128]{2,1,0:T(8,128)(2,1)S(1)}, bf16[16,8,128]{2,1,0:T(8,128)(2,1)S(1)}, u32[]{:S(2)}, u32[]{:S(2)}) collective-permute-start(bf16[16,8,128]{2,1,0:T(8,128)(2,1)S(1)} %fusion.22), channel_id=1, source_target_pairs={{0,128},{4,132},{8,136},{12,140},{16,144},{20,148},{24,152},{28,15... | collective-permute-start | bytes 98312 | tf_op jit(solution)/shard_map/ppermute | solution.py:180
  28.2 6.7 %collective-permute-start.5 = (bf16[16,8,128]{2,1,0:T(8,128)(2,1)S(1)}, bf16[16,8,128]{2,1,0:T(8,128)(2,1)S(1)}, u32[]{:S(2)}, u32[]{:S(2)}) collective-permute-start(bf16[16,8,128]{2,1,0:T(8,128)(2,1)S(1)} %fusion.22), channel_id=1, source_target_pairs={{0,64},{4,68},{8,72},{12,76},{16,80},{20,84},{24,88},{28,92},{32,9... | collective-permute-start | bytes 98312 | tf_op jit(solution)/shard_map/ppermute | solution.py:180
  35.0 3.4 %copy-start = (bf16[1024,4096]{1,0:T(8,128)(2,1)S(1)}, bf16[1024,4096]{1,0:T(8,128)(2,1)}, u32[]{:S(2)}) copy-start(bf16[1024,4096]{1,0:T(8,128)(2,1)} %weight_ref.3) | copy-start | bytes 25165828
  38.4 5.7 %copy-start.1 = (bf16[1024,4096]{1,0:T(8,128)(2,1)S(1)}, bf16[1024,4096]{1,0:T(8,128)(2,1)}, u32[]{:S(2)}) copy-start(bf16[1024,4096]{1,0:T(8,128)(2,1)} %weight_ref.3) | copy-start | bytes 25165828
  40.7 8.4 %collective-permute-start.9 = (bf16[128,1024]{1,0:T(8,128)(2,1)S(1)}, bf16[128,1024]{1,0:T(8,128)(2,1)S(1)}, u32[]{:S(2)}, u32[]{:S(2)}) collective-permute-start(bf16[128,1024]{1,0:T(8,128)(2,1)S(1)} %get-tuple-element.19), channel_id=1, source_target_pairs={{0,1},{1,2},{2,3},{3,0},{4,5},{5,6},{6,7},{7,4},{8,9},{9,10},{10,1... | collective-permute-start | bytes 786440 | tf_op jit(solution)/shard_map/ppermute | solution.py:209
  42.3 10.5 %collective-permute-start.12 = (bf16[128,1024]{1,0:T(8,128)(2,1)S(1)}, bf16[128,1024]{1,0:T(8,128)(2,1)S(1)}, u32[]{:S(2)}, u32[]{:S(2)}) collective-permute-start(bf16[128,1024]{1,0:T(8,128)(2,1)S(1)} %get-tuple-element.20), channel_id=1, source_target_pairs={{0,3},{1,0},{2,1},{3,2},{4,7},{5,4},{6,5},{7,6},{8,11},{9,8},{10,9... | collective-permute-start | bytes 786440 | tf_op jit(solution)/shard_map/ppermute | solution.py:210
  47.5 6.4 %collective-permute-start.8 = (bf16[128,1024]{1,0:T(8,128)(2,1)S(1)}, bf16[128,1024]{1,0:T(8,128)(2,1)S(1)}, u32[]{:S(2)}, u32[]{:S(2)}) collective-permute-start(bf16[128,1024]{1,0:T(8,128)(2,1)S(1)} %get-tuple-element.17), channel_id=1, source_target_pairs={{0,3},{1,0},{2,1},{3,2},{4,7},{5,4},{6,5},{7,6},{8,11},{9,8},{10,9... | collective-permute-start | bytes 786440 | tf_op jit(solution)/shard_map/ppermute | solution.py:213
  49.2 7.7 %collective-permute-start.10 = (bf16[128,1024]{1,0:T(8,128)(2,1)S(1)}, bf16[128,1024]{1,0:T(8,128)(2,1)S(1)}, u32[]{:S(2)}, u32[]{:S(2)}) collective-permute-start(bf16[128,1024]{1,0:T(8,128)(2,1)S(1)} %fusion.6), channel_id=1, source_target_pairs={{0,1},{1,2},{2,3},{3,0},{4,5},{5,6},{6,7},{7,4},{8,9},{9,10},{10,1... | collective-permute-start | bytes 786440 | tf_op jit(solution)/shard_map/ppermute | solution.py:214
  50.3 9.3 %collective-permute-start.11 = (bf16[128,1024]{1,0:T(8,128)(2,1)S(1)}, bf16[128,1024]{1,0:T(8,128)(2,1)S(1)}, u32[]{:S(2)}, u32[]{:S(2)}) collective-permute-start(bf16[128,1024]{1,0:T(8,128)(2,1)S(1)} %get-tuple-element.18), channel_id=1, source_target_pairs={{0,1},{1,2},{2,3},{3,0},{4,5},{5,6},{6,7},{7,4},{8,9},{9,10},{10,1... | collective-permute-start | bytes 786440 | tf_op jit(solution)/shard_map/ppermute | solution.py:212
  57.1 6.4 %collective-permute-start.13 = (bf16[128,1024]{1,0:T(8,128)(2,1)S(1)}, bf16[128,1024]{1,0:T(8,128)(2,1)S(1)}, u32[]{:S(2)}, u32[]{:S(2)}) collective-permute-start(bf16[128,1024]{1,0:T(8,128)(2,1)S(1)} %get-tuple-element.16), channel_id=1, source_target_pairs={{0,3},{1,0},{2,1},{3,2},{4,7},{5,4},{6,5},{7,6},{8,11},{9,8},{10,9... | collective-permute-start | bytes 786440 | tf_op jit(solution)/shard_map/ppermute | solution.py:215

commit v2 on v1

v2 whole, which is shorter than its diff:
```python
import functools

import jax
import jax.numpy as jnp
from jax import lax
from jax.experimental import pallas as pl
from jax.experimental.pallas import tpu as pltpu
from jax.sharding import PartitionSpec as P

MODES = 16
LANES = 128
SUB = 8
ROWS = 16


CHUNKS = 4
FAR, AFTER, PRIOR, MINE = 2, 1, 3, 0
STAGES = (
    (2, ((1, 1),), False),
    (4, ((1, 2), (3, 6), (2, 4)), False),
    (4, ((1, 8), (2, 16), (3, 24)), False),
    (2, ((1, 56),), False),
)
HBM = pl.BlockSpec(memory_space=pltpu.HBM)
VMEM = pl.BlockSpec(memory_space=pltpu.VMEM)
DMA = pltpu.SemaphoreType.DMA


def in_hbm(array):
    return pltpu.with_memory_space_constraint(array, pltpu.HBM)


def params():
    return pltpu.CompilerParams(vmem_limit_bytes=24 * 2**20)


def cost(flops, size):
    return pl.CostEstimate(flops=flops, bytes_accessed=size, transcendentals=0)


def wide(*shape):
    return jax.ShapeDtypeStruct(shape, jnp.float32)


def short(*shape):
    return jax.ShapeDtypeStruct(shape, jnp.bfloat16)


def total_of(terms):
    while len(terms) > 1:
        terms = [sum(terms[j : j + 2]) for j in range(0, len(terms), 2)]
    return terms[0]


def fetch_columns(weight_hbm, turn, out_ref, sems, first=0):
    chans, width = out_ref.shape
    owner = lax.rem(lax.axis_index("tp") + turn, weight_hbm.shape[1] // width)
    columns = pl.ds(pl.multiple_of(owner * width, width), width)
    part = chans // CHUNKS
    copies = []
    for c in range(CHUNKS):
        rows = pl.ds(c * part, part)
        copies.append(
            pltpu.make_async_copy(weight_hbm.at[rows, columns], out_ref.at[rows, :], sems.at[first + c])
        )
        copies[-1].start()
    return copies


def wait_all(copies):
    for copy in copies:
        copy.wait()


def state_kernel(key_hbm, value_hbm, decay_hbm, residue_hbm, skip_hbm,
                 state_ref, keyed_ref, decay_ref, residue_ref, skip_ref,
                 key_buf, value_buf, mode_buf, turn_buf, sems):
    length, chans = key_buf.shape
    groups = chans // LANES
    span = groups * SUB
    part = length // CHUNKS
    small = []
    for n, src in enumerate((decay_hbm, residue_hbm)):
        small.append(pltpu.make_async_copy(src, mode_buf.at[n], sems.at[2 * CHUNKS + n]))
    small[0].start()
    copies = []
    for c in range(CHUNKS):
        rows = pl.ds(c * part, part)
        copies.append((
            pltpu.make_async_copy(key_hbm.at[rows, :], key_buf.at[rows, :], sems.at[2 * c]),
            pltpu.make_async_copy(value_hbm.at[rows, :], value_buf.at[rows, :], sems.at[2 * c + 1]),
        ))
        for copy in copies[-1]:
            copy.start()
    small[1].start()
    skip = pltpu.make_async_copy(skip_hbm, skip_ref, sems.at[2 * CHUNKS + 2])
    skip.start()

    def turn(which, out_ref):
        small[which].wait()
        for m in range(MODES // SUB):
            for g in range(groups):
                turn_buf[(m * groups + g) * SUB : (m * groups + g + 1) * SUB, :] = mode_buf[
                    which, m * SUB : (m + 1) * SUB, g * LANES : (g + 1) * LANES
                ]
        for r in range(MODES):
            out_ref[r] = turn_buf[pl.ds(r // SUB * span + r % SUB, groups, stride=SUB), :]

    turn(0, decay_ref)
    step = [jnp.exp(-decay_ref[r]) for r in range(MODES)]

    def block(i, held):
        rows = pl.ds(pl.multiple_of(i * ROWS, ROWS), ROWS)
        keyed = key_buf[rows, :].astype(jnp.float32) * value_buf[rows, :].astype(jnp.float32)
        for half in range(ROWS // SUB):
            base = (i * (ROWS // SUB) + half) * span
            for g in range(groups):
                keyed_ref[pl.ds(pl.multiple_of(base + g * SUB, SUB), SUB), :] = keyed[
                    half * SUB : (half + 1) * SUB, g * LANES : (g + 1) * LANES
                ]
        for half in range(ROWS // SUB):
            base = (i * (ROWS // SUB) + half) * span
            for s in range(SUB):
                now = keyed_ref[pl.ds(base + s, groups, stride=SUB), :]
                held = [a * h + now for a, h in zip(step, held)]
        return held

    held = [jnp.zeros((groups, LANES), jnp.float32)] * MODES
    for c in range(CHUNKS):
        for copy in copies[c]:
            copy.wait()
        held = lax.fori_loop(c * (part // ROWS), (c + 1) * (part // ROWS), block, held)
    for r in range(MODES):
        state_ref[r] = held[r]
    turn(1, residue_ref)
    skip.wait()


def block_state(gate_key, value_in, decay, residue, skip):
    length, chans = gate_key.shape
    groups = chans // LANES
    modes = wide(MODES, groups, LANES)
    return pl.pallas_call(
        state_kernel,
        out_shape=(modes, wide(length * groups, LANES), modes, modes, wide(groups, LANES)),
        in_specs=[HBM] * 5,
        out_specs=(VMEM,) * 5,
        scratch_shapes=[
            pltpu.VMEM((length, chans), jnp.bfloat16),
            pltpu.VMEM((length, chans), jnp.bfloat16),
            pltpu.VMEM((2, MODES, chans), jnp.float32),
            pltpu.VMEM((MODES * groups, LANES), jnp.float32),
            DMA((2 * CHUNKS + 3,)),
        ],
        compiler_params=params(),
        cost_estimate=cost(2**23, 2**23),
    )(*(in_hbm(x) for x in (gate_key, value_in, decay, residue, skip)))


def local_kernel(keyed_ref, decay_ref, scale_ref, _, skip_ref, local_ref, ahead_ref):
    groups = decay_ref.shape[1]
    span = groups * SUB
    ahead = (3 - lax.axis_index("ctx") // 2 % 4) * 2 * (keyed_ref.shape[0] // groups)
    for r in range(MODES):
        ahead_ref[r] = jnp.exp(-decay_ref[r] * ahead.astype(jnp.float32))
    step = [jnp.exp(-decay_ref[r]) for r in range(MODES)]
    scale = [scale_ref[r] for r in range(MODES)]
    skip = skip_ref[...]

    def block(i, held):
        for s in range(SUB):
            at = pl.ds(i * span + s, groups, stride=SUB)
            now = keyed_ref[at, :]
            held = [a * h + now for a, h in zip(step, held)]
            local_ref[at, :] = total_of([c * h for c, h in zip(scale, held)] + [skip * now])
        return held

    lax.fori_loop(0, keyed_ref.shape[0] // span, block, [jnp.zeros((groups, LANES), jnp.float32)] * MODES)


def local_part(keyed, decay, scale, behind, skip):
    return pl.pallas_call(
        local_kernel,
        out_shape=(wide(*keyed.shape), wide(*decay.shape)),
        in_specs=[VMEM] * 5,
        out_specs=(VMEM, VMEM),
        compiler_params=params(),
        cost_estimate=cost(2**23, 2**22),
    )(keyed, decay, scale, behind, skip)


def fetch_kernel(query_hbm, weight_hbm, _, query_ref, far_ref, sems):
    copies = fetch_columns(weight_hbm, FAR, far_ref, sems)
    copies.append(pltpu.make_async_copy(query_hbm, query_ref, sems.at[CHUNKS]))
    copies[-1].start()
    wait_all(copies)


def fetch(gate_query, weight, behind, ring):
    return pl.pallas_call(
        fetch_kernel,
        out_shape=(short(*gate_query.shape), short(weight.shape[0], weight.shape[1] // ring)),
        in_specs=[HBM, HBM, VMEM],
        out_specs=(VMEM,) * 2,
        scratch_shapes=[DMA((CHUNKS + 1,))],
        compiler_params=params(),
        cost_estimate=cost(2**10, 2**22),
    )(in_hbm(gate_query), in_hbm(weight), behind)


def carry_kernel(local_ref, query_ref, decay_ref, start_ref, far_ref, weight_hbm,
                 gated_ref, far_top, far_low, after_ref, tail_ref, sems):
    copies = fetch_columns(weight_hbm, AFTER, after_ref, sems)
    length, chans = gated_ref.shape
    groups = chans // LANES
    span = groups * SUB
    step = [jnp.exp(-decay_ref[r]) for r in range(MODES)]

    def block(i, held):
        rows = pl.ds(pl.multiple_of(i * ROWS, ROWS), ROWS)
        for half in range(ROWS // SUB):
            for s in range(SUB):
                tail_ref[pl.ds(half * span + s, groups, stride=SUB), :] = total_of(held)
                held = [a * h for a, h in zip(step, held)]
        for g in range(groups):
            parts = []
            for half in range(ROWS // SUB):
                base = (i * (ROWS // SUB) + half) * span + g * SUB
                parts.append(
                    local_ref[pl.ds(pl.multiple_of(base, SUB), SUB), :]
                    + tail_ref[half * span + g * SUB : half * span + (g + 1) * SUB, :]
                )
            cols = slice(g * LANES, (g + 1) * LANES)
            gated_ref[rows, cols] = (
                query_ref[rows, cols].astype(jnp.float32) * jnp.concatenate(parts, axis=0)
            ).astype(jnp.bfloat16)
        return held

    lax.fori_loop(0, length // ROWS, block, [start_ref[r] for r in range(MODES)])
    half = length // 2
    for n, out in enumerate((far_top, far_low)):
        out[...] = jnp.dot(
            gated_ref[n * half : (n + 1) * half, :], far_ref[...], preferred_element_type=jnp.float32
        ).astype(jnp.bfloat16)
    wait_all(copies)


def carry_part(local, query, decay, start, far, weight):
    length, chans = query.shape
    groups = chans // LANES
    part = short(length // 2, far.shape[1])
    return pl.pallas_call(
        carry_kernel,
        out_shape=(short(length, chans), part, part, short(*far.shape)),
        in_specs=[VMEM] * 5 + [HBM],
        out_specs=(VMEM,) * 4,
        scratch_shapes=[pltpu.VMEM((ROWS * groups, LANES), jnp.float32), DMA((CHUNKS,))],
        compiler_params=params(),
        cost_estimate=cost(2**29, 2**20),
    )(local, query, decay, start, far, in_hbm(weight))


def near_kernel(gated_ref, after_ref, weight_hbm, after_top, after_low, prior_top, prior_low, prior_buf, sems):
    half = after_top.shape[0]
    copies = fetch_columns(weight_hbm, PRIOR, prior_buf, sems)
    top, low = slice(0, half), slice(half, 2 * half)
    for out, rows, weight in (
        (after_low, low, after_ref),
        (after_top, top, after_ref),
        (prior_top, top, prior_buf),
        (prior_low, low, prior_buf),
    ):
        if out is prior_top:
            wait_all(copies)
        out[...] = jnp.dot(gated_ref[rows, :], weight[...], preferred_element_type=jnp.float32).astype(out.dtype)


def near_part(gated, after, weight):
    shape = (gated.shape[0] // 2, after.shape[1])
    return pl.pallas_call(
        near_kernel,
        out_shape=(wide(*shape), short(*shape), short(*shape), wide(*shape)),
        in_specs=[VMEM, VMEM, HBM],
        out_specs=(VMEM,) * 4,
        scratch_shapes=[pltpu.VMEM(after.shape, jnp.bfloat16), DMA((CHUNKS,))],
        compiler_params=params(),
        cost_estimate=cost(2**30, 2**20),
    )(gated, after, in_hbm(weight))


def own_kernel(gated_ref, weight_hbm, mine_top, mine_low, mine_buf, sems):
    half = mine_top.shape[0]
    wait_all(fetch_columns(weight_hbm, MINE, mine_buf, sems))
    for n, out in enumerate((mine_top, mine_low)):
        out[...] = jnp.dot(
            gated_ref[n * half : (n + 1) * half, :], mine_buf[...], preferred_element_type=jnp.float32
        )


def own_part(gated, weight, ring):
    length, chans = gated.shape
    width = weight.shape[1] // ring
    part = wide(length // 2, width)
    return pl.pallas_call(
        own_kernel,
        out_shape=(part, part),
        in_specs=[VMEM, HBM],
        out_specs=(VMEM,) * 2,
        scratch_shapes=[pltpu.VMEM((chans, width), jnp.bfloat16), DMA((CHUNKS,))],
        compiler_params=params(),
        cost_estimate=cost(2**29, 2**20),
    )(gated, in_hbm(weight))


def finish_kernel(mine_top, near_top, both_top, mine_low, near_low, both_low, out_hbm, out_buf, sems):
    half = mine_top.shape[0]
    copies = []
    for n, (mine, near, both) in enumerate(
        ((mine_top, near_top, both_top), (mine_low, near_low, both_low))
    ):
        rows = pl.ds(n * half, half)
        out_buf[rows, :] = (
            mine[...] + near[...].astype(jnp.float32) + both[...].astype(jnp.float32)
        ).astype(jnp.bfloat16)
        copies.append(pltpu.make_async_copy(out_buf.at[rows, :], out_hbm.at[rows, :], sems.at[n]))
        copies[-1].start()
    for copy in copies:
        copy.wait()


def finish(*parts):
    half, width = parts[0].shape
    return pl.pallas_call(
        finish_kernel,
        out_shape=short(2 * half, width),
        in_specs=[VMEM] * 6,
        out_specs=HBM,
        scratch_shapes=[pltpu.VMEM((2 * half, width), jnp.bfloat16), DMA((2,))],
        compiler_params=params(),
        cost_estimate=cost(2**19, 2**21),
    )(*parts)


def scan_over_ctx(state, decay, length, index, work, load):
    devices = lax.axis_size("ctx")

    def power(blocks):
        blocks = jnp.asarray(blocks)
        reach = (length * jnp.maximum(blocks, 0)).astype(jnp.float32)
        return jnp.where(blocks >= 0, jnp.exp(-decay * reach), 0.0)

    total, before = state, jnp.zeros_like(state)
    span = 1
    for stage, (members, moves, forward) in enumerate(STAGES):
        mine, inside = index // span % members, index % span
        sent = total.astype(jnp.bfloat16)
        own = work(sent) if stage == 1 else power((members - 1 - mine) * span)
        if stage == len(STAGES) - 1:
            load(sent)
        got = []
        for k, flip in moves:
            pairs = [(i, i ^ flip) for i in range(devices)]
            if forward:
                pairs = [(i, j) for i, j in pairs if i < j]
            got.append((k, lax.ppermute(sent, "ctx", pairs).astype(jnp.float32)))
        total = total * own
        for k, theirs in got:
            other = mine ^ k
            before = before + theirs * power(
                jnp.where(other < mine, (mine - 1 - other) * span + inside, -1)
            )
            total = total + theirs * power((members - 1 - other) * span)
        span *= members
    return before


def on_device(gate_query, gate_key, value_in, residues, decay_rate, skip_gain, out_weight):
    index = lax.axis_index("ctx")
    length, chans = gate_key.shape
    groups = chans // LANES
    ring = lax.axis_size("tp")
    forth = [(i, (i + 1) % ring) for i in range(ring)]
    back = [(i, (i + ring - 1) % ring) for i in range(ring)]

    state, keyed, decay, residue, skip = block_state(
        gate_key, value_in, decay_rate.T, residues.T, skip_gain.reshape(groups, LANES)
    )
    scale = residue * jnp.sqrt(-jnp.expm1(-2.0 * decay))
    local = None

    def work(sent):
        nonlocal local
        local, ahead = local_part(keyed, decay, scale, sent, skip)
        return ahead

    def load(sent):
        nonlocal columns
        columns = fetch(gate_query, out_weight, sent, ring)

    columns = None
    carry = scan_over_ctx(state, decay, length, index, work, load)
    query, far = columns
    start = scale * jnp.exp(-decay) * carry
    gated, far_top, far_low, after = carry_part(local, query, decay, start, far, out_weight)
    far_a = lax.ppermute(far_top, "tp", forth)
    far_b = lax.ppermute(far_low, "tp", back)
    after_top, after_low, prior_top, prior_low = near_part(gated, after, out_weight)
    mine_top, mine_low = own_part(gated, out_weight, ring)
    near_b = lax.ppermute(after_low, "tp", forth)
    near_a = lax.ppermute(prior_top, "tp", back)
    both_a = lax.ppermute((after_top + far_a.astype(jnp.float32)).astype(jnp.bfloat16), "tp", forth)
    both_b = lax.ppermute((prior_low + far_b.astype(jnp.float32)).astype(jnp.bfloat16), "tp", back)
    return finish(mine_top, near_a, both_a, mine_low, near_b, both_b)


def solution(mesh):
    in_specs = (
        P("ctx", "tp"),
        P("ctx", "tp"),
        P("ctx", "tp"),
        P("tp", None),
        P("tp", None),
        P("tp"),
        P("tp", None),
    )
    return jax.shard_map(
        on_device, mesh=mesh, in_specs=in_specs, out_specs=P("ctx", "tp"), check_vma=False
    )
```

time: 65.3 us -> 50 us (0.77)
  waiting for transfers between devices: 23 us -> 9.39 us
  local copies, waits for them, and re-layouts: 7.99 us -> 0 us
  Pallas kernels: 8.05 us -> 14.8 us
  starting transfers between devices: 23.2 us -> 24.9 us
  other arithmetic: 1.88 us -> 0.53 us
    ppermute x8, waiting for transfers between devices: 14.5 us -> 5.45 us  [scan_over_ctx(): got.append((k, lax.ppermute(sent, 'ctx', pairs).astype(jnp.float32)))]
    unnamed x14 -> x0, local copies, waits for them, and re-layouts: 7.92 us -> none
    pallas_call x3 -> x7, Pallas kernels: 8.05 us -> 14.8 us  [the longest x1 2.8 us: near_part(): pl.pallas_call(near_kernel, out_shape=(wide(*shape), short(*shape), short...]
    ppermute x6, waiting for transfers between devices: 8.52 us -> 3.95 us  [the longest x1 2.81 us: on_device(): lax.ppermute((after_top + far_a.astype(jnp.float32)).astype(jnp.bfloat16)...]
    ppermute x8, starting transfers between devices: 12.7 us -> 15.2 us  [scan_over_ctx(): got.append((k, lax.ppermute(sent, 'ctx', pairs).astype(jnp.float32)))]
    concatenate x1 -> x0, other arithmetic: 0.83 us -> none  [on_device(): return jnp.concatenate([first, second]).astype(jnp.bfloat16)]
    ppermute x6, starting transfers between devices: 10.5 us -> 9.72 us  [the longest x1 2.96 us: on_device(): lax.ppermute((prior_low + far_b.astype(jnp.float32)).astype(jnp.bfloat16)...]
  transfers between devices with their start and end apart: 14 -> 14, of which waited for: 9 -> 7; matrix products, arithmetic and copies ran while one was open for 1% -> 0% of each run, Pallas kernels for 5% -> 19%
where the time goes in v2:
time: 50 us; the launch traced here: 49.7 us
  starting transfers between devices  24.9 us (50%)
  Pallas kernels  14.8 us (30%)
  waiting for transfers between devices  9.39 us (19%)
  other arithmetic  0.53 us (1%)
    ppermute x8, starting transfers between devices, scan_over_ctx(): got.append((k, lax.ppermute(sent, 'ctx', pairs).astype(jnp.float32)))  15.2 us
    ppermute x8, waiting for transfers between devices, scan_over_ctx(): got.append((k, lax.ppermute(sent, 'ctx', pairs).astype(jnp.float32)))  5.45 us
    ppermute x1, starting transfers between devices, on_device(): lax.ppermute((prior_low + far_b.astype(jnp.float32)).astype(jnp.bfloat16)...  2.96 us
    ppermute x1, waiting for transfers between devices, on_device(): lax.ppermute((after_top + far_a.astype(jnp.float32)).astype(jnp.bfloat16)...  2.81 us
    pallas_call x1, Pallas kernels, near_part(): pl.pallas_call(near_kernel, out_shape=(wide(*shape), short(*shape), short...  2.8 us
    pallas_call x1, Pallas kernels, local_part(): pl.pallas_call(local_kernel, out_shape=(wide(*keyed.shape), wide(*decay.s...  2.52 us
    pallas_call x1, Pallas kernels, block_state(): pl.pallas_call(state_kernel, out_shape=(modes, wide(length * groups, LANE...  2.51 us
    pallas_call x1, Pallas kernels, own_part(): pl.pallas_call(own_kernel, out_shape=(part, part), in_specs=[VMEM, HBM],...  2.29 us
  transfers between devices with their start and end apart: 14, of which 7 were waited for; matrix products, arithmetic and copies ran while one was open for 0% of the time, Pallas kernels for 19%

profile of v2, /device:TPU:32, one launch (start us, length us, event | category | flops | bytes accessed | tf_op | source)
XLA Modules:
  0.0 49.7 jit_solution(4099562614426251169)
XLA Ops:
  0.0 2.5 %shard_map.73 = (f32[16,8,128]{2,1,0:T(8,128)S(1)}, f32[2048,128]{1,0:T(8,128)S(1)}, f32[16,8,128]{2,1,0:T(8,128)S(1)}, f32[16,8,128]{2,1,0:T(8,128)S(1)}, f32[8,128]{1,0:T(8,128)S(1)}) custom-call(bf16[256,1024]{1,0:T(8,128)(2,1)} %key_hbm.1, bf16[256,1024]{1,0:T(8,128)(2,1)} %value_hbm.1, f32[16,1024]{1,0:T(8,128)} %bitcast.3, f32[16,1024]{1,0:T(8,128)} %bitcast.4, ...), custom_call_target="tpu_custom_call" | custom-call | flops 8388608 | bytes 8388608 | tf_op jit(solution)/shard_map/pallas_call | solution.py:143
  2.7 1.2 %collective-permute-done = bf16[16,8,128]{2,1,0:T(8,128)(2,1)S(1)} collective-permute-done((bf16[16,8,128]{2,1,0:T(8,128)(2,1)S(1)}, bf16[16,8,128]{2,1,0:T(8,128)(2,1)S(1)}, u32[]{:S(2)}, u32[]{:S(2)}) %collective-permute-start) | collective-permute-done | bytes 32800 | tf_op jit(solution)/shard_map/ppermute | solution.py:365
  3.9 3.3 %collective-permute-start.3 = (bf16[16,8,128]{2,1,0:T(8,128)(2,1)S(1)}, bf16[16,8,128]{2,1,0:T(8,128)(2,1)S(1)}, u32[]{:S(2)}, u32[]{:S(2)}) collective-permute-start(bf16[16,8,128]{2,1,0:T(8,128)(2,1)S(1)} %get-tuple-element.45._), channel_id=1, source_target_pairs={{0,16},{4,20},{8,24},{12,28},{16,0},{20,4},{24,8},{28,12},{32,48},... | collective-permute-start | bytes 98312 | tf_op jit(solution)/shard_map/ppermute | solution.py:365
  7.2 1.1 %collective-permute-start.2 = (bf16[16,8,128]{2,1,0:T(8,128)(2,1)S(1)}, bf16[16,8,128]{2,1,0:T(8,128)(2,1)S(1)}, u32[]{:S(2)}, u32[]{:S(2)}) collective-permute-start(bf16[16,8,128]{2,1,0:T(8,128)(2,1)S(1)} %get-tuple-element.45._), channel_id=1, source_target_pairs={{0,24},{4,28},{8,16},{12,20},{16,8},{20,12},{24,0},{28,4},{32,56},... | collective-permute-start | bytes 98312 | tf_op jit(solution)/shard_map/ppermute | solution.py:365
  8.2 2.5 %shard_map.74 = (f32[2048,128]{1,0:T(8,128)S(1)}, f32[16,8,128]{2,1,0:T(8,128)S(1)}) custom-call(f32[2048,128]{1,0:T(8,128)S(1)} %get-tuple-element.24.keyed_ref, f32[16,8,128]{2,1,0:T(8,128)S(1)} %get-tuple-element.25.decay_ref, f32[16,8,128]{2,1,0:T(8,128)S(1)} %get-tuple-element.46.scale_ref, bf16[16,8,128]{2,1,0:T(8,128)(2,1)S(1)} %get-tuple-element.45._, ...), custom_call_target="tpu_custom_call" | custom-call | flops 8388608 | bytes 4194304 | tf_op jit(solution)/shard_map/pallas_call | solution.py:182
  10.8 1.5 %collective-permute-done.2 = bf16[16,8,128]{2,1,0:T(8,128)(2,1)S(1)} collective-permute-done((bf16[16,8,128]{2,1,0:T(8,128)(2,1)S(1)}, bf16[16,8,128]{2,1,0:T(8,128)(2,1)S(1)}, u32[]{:S(2)}, u32[]{:S(2)}) %collective-permute-start.2) | collective-permute-done | bytes 32800 | tf_op jit(solution)/shard_map/ppermute | solution.py:365
  12.4 2.0 %collective-permute-start.6 = (bf16[16,8,128]{2,1,0:T(8,128)(2,1)S(1)}, bf16[16,8,128]{2,1,0:T(8,128)(2,1)S(1)}, u32[]{:S(2)}, u32[]{:S(2)}) collective-permute-start(bf16[16,8,128]{2,1,0:T(8,128)(2,1)S(1)} %get-tuple-element.43), channel_id=1, source_target_pairs={{0,96},{4,100},{8,104},{12,108},{16,112},{20,116},{24,120},{28,124... | collective-permute-start | bytes 98312 | tf_op jit(solution)/shard_map/ppermute | solution.py:365
  14.4 1.5 %collective-permute-start.5 = (bf16[16,8,128]{2,1,0:T(8,128)(2,1)S(1)}, bf16[16,8,128]{2,1,0:T(8,128)(2,1)S(1)}, u32[]{:S(2)}, u32[]{:S(2)}) collective-permute-start(bf16[16,8,128]{2,1,0:T(8,128)(2,1)S(1)} %get-tuple-element.43), channel_id=1, source_target_pairs={{0,64},{4,68},{8,72},{12,76},{16,80},{20,84},{24,88},{28,92},{32,9... | collective-permute-start | bytes 98312 | tf_op jit(solution)/shard_map/ppermute | solution.py:365
  15.9 1.4 %collective-permute-start.4 = (bf16[16,8,128]{2,1,0:T(8,128)(2,1)S(1)}, bf16[16,8,128]{2,1,0:T(8,128)(2,1)S(1)}, u32[]{:S(2)}, u32[]{:S(2)}) collective-permute-start(bf16[16,8,128]{2,1,0:T(8,128)(2,1)S(1)} %get-tuple-element.43), channel_id=1, source_target_pairs={{0,32},{4,36},{8,40},{12,44},{16,48},{20,52},{24,56},{28,60},{32,0... | collective-permute-start | bytes 98312 | tf_op jit(solution)/shard_map/ppermute | solution.py:365
  17.2 2.3 %collective-permute-done.5 = bf16[16,8,128]{2,1,0:T(8,128)(2,1)S(1)} collective-permute-done((bf16[16,8,128]{2,1,0:T(8,128)(2,1)S(1)}, bf16[16,8,128]{2,1,0:T(8,128)(2,1)S(1)}, u32[]{:S(2)}, u32[]{:S(2)}) %collective-permute-start.5) | collective-permute-done | bytes 32800 | tf_op jit(solution)/shard_map/ppermute | solution.py:365
  19.9 5.9 %collective-permute-start.7 = (bf16[16,8,128]{2,1,0:T(8,128)(2,1)S(1)}, bf16[16,8,128]{2,1,0:T(8,128)(2,1)S(1)}, u32[]{:S(2)}, u32[]{:S(2)}) collective-permute-start(bf16[16,8,128]{2,1,0:T(8,128)(2,1)S(1)} %fusion.15._), channel_id=1, source_target_pairs={{0,224},{4,228},{8,232},{12,236},{16,240},{20,244},{24,248},{28,25... | collective-permute-start | bytes 98312 | tf_op jit(solution)/shard_map/ppermute | solution.py:365
  25.8 1.7 %shard_map.75 = (bf16[256,1024]{1,0:T(8,128)(2,1)S(1)}, bf16[1024,1024]{1,0:T(8,128)(2,1)S(1)}) custom-call(bf16[256,1024]{1,0:T(8,128)(2,1)} %query_hbm.1, bf16[1024,4096]{1,0:T(8,128)(2,1)} %weight_hbm.7, bf16[16,8,128]{2,1,0:T(8,128)(2,1)S(1)} %fusion.15._), custom_call_target="tpu_custom_call" | custom-call | flops 1024 | bytes 4194304 | tf_op jit(solution)/shard_map/pallas_call | solution.py:200
  27.9 2.1 %shard_map.76 = (bf16[256,1024]{1,0:T(8,128)(2,1)S(1)}, bf16[128,1024]{1,0:T(8,128)(2,1)S(1)}, bf16[128,1024]{1,0:T(8,128)(2,1)S(1)}, bf16[1024,1024]{1,0:T(8,128)(2,1)S(1)}) custom-call(f32[2048,128]{1,0:T(8,128)S(1)} %get-tuple-element.29.local_ref, bf16[256,1024]{1,0:T(8,128)(2,1)S(1)} %get-tuple-element.31.query_ref, ...), custom_call_target="tpu_custom_call" | custom-call | flops 536870912 | bytes 1048576 | tf_op jit(solution)/shard_map/pallas_call | solution.py:252
  29.9 1.6 %collective-permute-start.9 = (bf16[128,1024]{1,0:T(8,128)(2,1)S(1)}, bf16[128,1024]{1,0:T(8,128)(2,1)S(1)}, u32[]{:S(2)}, u32[]{:S(2)}) collective-permute-start(bf16[128,1024]{1,0:T(8,128)(2,1)S(1)} %get-tuple-element.38), channel_id=1, source_target_pairs={{0,1},{1,2},{2,3},{3,0},{4,5},{5,6},{6,7},{7,4},{8,9},{9,10},{10,1... | collective-permute-start | bytes 786440 | tf_op jit(solution)/shard_map/ppermute | solution.py:405
  31.5 1.7 %collective-permute-start.12 = (bf16[128,1024]{1,0:T(8,128)(2,1)S(1)}, bf16[128,1024]{1,0:T(8,128)(2,1)S(1)}, u32[]{:S(2)}, u32[]{:S(2)}) collective-permute-start(bf16[128,1024]{1,0:T(8,128)(2,1)S(1)} %get-tuple-element.42), channel_id=1, source_target_pairs={{0,3},{1,0},{2,1},{3,2},{4,7},{5,4},{6,5},{7,6},{8,11},{9,8},{10,9... | collective-permute-start | bytes 786440 | tf_op jit(solution)/shard_map/ppermute | solution.py:406
  33.3 2.8 %shard_map.78 = (f32[128,1024]{1,0:T(8,128)S(1)}, bf16[128,1024]{1,0:T(8,128)(2,1)S(1)}, bf16[128,1024]{1,0:T(8,128)(2,1)S(1)}, f32[128,1024]{1,0:T(8,128)S(1)}) custom-call(bf16[256,1024]{1,0:T(8,128)(2,1)S(1)} %get-tuple-element.33.gated_ref, bf16[1024,1024]{1,0:T(8,128)(2,1)S(1)} %get-tuple-element.35.after_ref, bf16[1024,4096]{1,0:T(8,128)(2,1)} %weight_hbm.7), custom_call_target="tpu_custom_call" | custom-call | flops 1073741824 | bytes 1048576 | tf_op jit(solution)/shard_map/pallas_call | solution.py:280
  36.1 1.6 %collective-permute-start.8 = (bf16[128,1024]{1,0:T(8,128)(2,1)S(1)}, bf16[128,1024]{1,0:T(8,128)(2,1)S(1)}, u32[]{:S(2)}, u32[]{:S(2)}) collective-permute-start(bf16[128,1024]{1,0:T(8,128)(2,1)S(1)} %get-tuple-element.36), channel_id=1, source_target_pairs={{0,3},{1,0},{2,1},{3,2},{4,7},{5,4},{6,5},{7,6},{8,11},{9,8},{10,9... | collective-permute-start | bytes 786440 | tf_op jit(solution)/shard_map/ppermute | solution.py:410
  37.7 0.5 collective-permute-start.11
  38.2 1.3 %collective-permute-start.10 = (bf16[128,1024]{1,0:T(8,128)(2,1)S(1)}, bf16[128,1024]{1,0:T(8,128)(2,1)S(1)}, u32[]{:S(2)}, u32[]{:S(2)}) collective-permute-start(bf16[128,1024]{1,0:T(8,128)(2,1)S(1)} %add_convert_fusion.1), channel_id=1, source_target_pairs={{0,1},{1,2},{2,3},{3,0},{4,5},{5,6},{6,7},{7,4},{8,9},{9,10},{10,1... | collective-permute-start | bytes 786440 | tf_op jit(solution)/shard_map/ppermute | solution.py:411
  39.6 1.1 %collective-permute-done.12 = bf16[128,1024]{1,0:T(8,128)(2,1)S(1)} collective-permute-done((bf16[128,1024]{1,0:T(8,128)(2,1)S(1)}, bf16[128,1024]{1,0:T(8,128)(2,1)S(1)}, u32[]{:S(2)}, u32[]{:S(2)}) %collective-permute-start.12) | collective-permute-done | bytes 262176 | tf_op jit(solution)/shard_map/ppermute | solution.py:406
  40.7 3.0 %collective-permute-start.13 = (bf16[128,1024]{1,0:T(8,128)(2,1)S(1)}, bf16[128,1024]{1,0:T(8,128)(2,1)S(1)}, u32[]{:S(2)}, u32[]{:S(2)}) collective-permute-start(bf16[128,1024]{1,0:T(8,128)(2,1)S(1)} %add_convert_fusion), channel_id=1, source_target_pairs={{0,3},{1,0},{2,1},{3,2},{4,7},{5,4},{6,5},{7,6},{8,11},{9,8},{10,9... | collective-permute-start | bytes 786440 | tf_op jit(solution)/shard_map/ppermute | solution.py:412
  43.7 2.3 %shard_map.77 = (f32[128,1024]{1,0:T(8,128)S(1)}, f32[128,1024]{1,0:T(8,128)S(1)}) custom-call(bf16[256,1024]{1,0:T(8,128)(2,1)S(1)} %get-tuple-element.33.gated_ref, bf16[1024,4096]{1,0:T(8,128)(2,1)} %weight_hbm.7), custom_call_target="tpu_custom_call" | custom-call | flops 536870912 | bytes 1048576 | tf_op jit(solution)/shard_map/pallas_call | solution.py:304
  46.0 2.8 %collective-permute-done.10.both_top = bf16[128,1024]{1,0:T(8,128)(2,1)S(1)} collective-permute-done((bf16[128,1024]{1,0:T(8,128)(2,1)S(1)}, bf16[128,1024]{1,0:T(8,128)(2,1)S(1)}, u32[]{:S(2)}, u32[]{:S(2)}) %collective-permute-start.10) | collective-permute-done | bytes 262176 | tf_op jit(solution)/shard_map/ppermute | solution.py:411
  48.8 0.9 %shard_map.79 = bf16[256,1024]{1,0:T(8,128)(2,1)} custom-call(f32[128,1024]{1,0:T(8,128)S(1)} %get-tuple-element.34.mine_top, bf16[128,1024]{1,0:T(8,128)(2,1)S(1)} %collective-permute-done.8.near_top, bf16[128,1024]{1,0:T(8,128)(2,1)S(1)} %collective-permute-done.10.both_top, f32[128,1024]{1,0:T(8,128)S(1)} %get-tuple-element.39.mine_low, ...), custom_call_target="tpu_custom_call" | custom-call | flops 524288 | bytes 2097152 | tf_op jit(solution)/shard_map/pallas_call | solution.py:333
  (18 shorter events, 1.1 us)
Async XLA Ops:
  2.5 1.3 %collective-permute-start = (bf16[16,8,128]{2,1,0:T(8,128)(2,1)S(1)}, bf16[16,8,128]{2,1,0:T(8,128)(2,1)S(1)}, u32[]{:S(2)}, u32[]{:S(2)}) collective-permute-start(bf16[16,8,128]{2,1,0:T(8,128)(2,1)S(1)} %convert_element_type.100), channel_id=1, source_target_pairs={{0,4},{4,0},{8,12},{12,8},{16,20},{20,16},{24,28},{28,24},{32,36},... | collective-permute-start | bytes 98312 | tf_op jit(solution)/shard_map/ppermute | solution.py:365
  3.9 6.9 %collective-permute-start.3 = (bf16[16,8,128]{2,1,0:T(8,128)(2,1)S(1)}, bf16[16,8,128]{2,1,0:T(8,128)(2,1)S(1)}, u32[]{:S(2)}, u32[]{:S(2)}) collective-permute-start(bf16[16,8,128]{2,1,0:T(8,128)(2,1)S(1)} %get-tuple-element.45._), channel_id=1, source_target_pairs={{0,16},{4,20},{8,24},{12,28},{16,0},{20,4},{24,8},{28,12},{32,48},... | collective-permute-start | bytes 98312 | tf_op jit(solution)/shard_map/ppermute | solution.py:365
  7.2 5.1 %collective-permute-start.2 = (bf16[16,8,128]{2,1,0:T(8,128)(2,1)S(1)}, bf16[16,8,128]{2,1,0:T(8,128)(2,1)S(1)}, u32[]{:S(2)}, u32[]{:S(2)}) collective-permute-start(bf16[16,8,128]{2,1,0:T(8,128)(2,1)S(1)} %get-tuple-element.45._), channel_id=1, source_target_pairs={{0,24},{4,28},{8,16},{12,20},{16,8},{20,12},{24,0},{28,4},{32,56},... | collective-permute-start | bytes 98312 | tf_op jit(solution)/shard_map/ppermute | solution.py:365
  8.2 4.1 %collective-permute-start.1 = (bf16[16,8,128]{2,1,0:T(8,128)(2,1)S(1)}, bf16[16,8,128]{2,1,0:T(8,128)(2,1)S(1)}, u32[]{:S(2)}, u32[]{:S(2)}) collective-permute-start(bf16[16,8,128]{2,1,0:T(8,128)(2,1)S(1)} %get-tuple-element.45._), channel_id=1, source_target_pairs={{0,8},{4,12},{8,0},{12,4},{16,24},{20,28},{24,16},{28,20},{32,40},... | collective-permute-start | bytes 98312 | tf_op jit(solution)/shard_map/ppermute | solution.py:365
  12.4 4.8 %collective-permute-start.6 = (bf16[16,8,128]{2,1,0:T(8,128)(2,1)S(1)}, bf16[16,8,128]{2,1,0:T(8,128)(2,1)S(1)}, u32[]{:S(2)}, u32[]{:S(2)}) collective-permute-start(bf16[16,8,128]{2,1,0:T(8,128)(2,1)S(1)} %get-tuple-element.43), channel_id=1, source_target_pairs={{0,96},{4,100},{8,104},{12,108},{16,112},{20,116},{24,120},{28,124... | collective-permute-start | bytes 98312 | tf_op jit(solution)/shard_map/ppermute | solution.py:365
  14.4 5.1 %collective-permute-start.5 = (bf16[16,8,128]{2,1,0:T(8,128)(2,1)S(1)}, bf16[16,8,128]{2,1,0:T(8,128)(2,1)S(1)}, u32[]{:S(2)}, u32[]{:S(2)}) collective-permute-start(bf16[16,8,128]{2,1,0:T(8,128)(2,1)S(1)} %get-tuple-element.43), channel_id=1, source_target_pairs={{0,64},{4,68},{8,72},{12,76},{16,80},{20,84},{24,88},{28,92},{32,9... | collective-permute-start | bytes 98312 | tf_op jit(solution)/shard_map/ppermute | solution.py:365
  15.9 4.0 %collective-permute-start.4 = (bf16[16,8,128]{2,1,0:T(8,128)(2,1)S(1)}, bf16[16,8,128]{2,1,0:T(8,128)(2,1)S(1)}, u32[]{:S(2)}, u32[]{:S(2)}) collective-permute-start(bf16[16,8,128]{2,1,0:T(8,128)(2,1)S(1)} %get-tuple-element.43), channel_id=1, source_target_pairs={{0,32},{4,36},{8,40},{12,44},{16,48},{20,52},{24,56},{28,60},{32,0... | collective-permute-start | bytes 98312 | tf_op jit(solution)/shard_map/ppermute | solution.py:365
  19.9 7.8 %collective-permute-start.7 = (bf16[16,8,128]{2,1,0:T(8,128)(2,1)S(1)}, bf16[16,8,128]{2,1,0:T(8,128)(2,1)S(1)}, u32[]{:S(2)}, u32[]{:S(2)}) collective-permute-start(bf16[16,8,128]{2,1,0:T(8,128)(2,1)S(1)} %fusion.15._), channel_id=1, source_target_pairs={{0,224},{4,228},{8,232},{12,236},{16,240},{20,244},{24,248},{28,25... | collective-permute-start | bytes 98312 | tf_op jit(solution)/shard_map/ppermute | solution.py:365
  29.9 8.2 %collective-permute-start.9 = (bf16[128,1024]{1,0:T(8,128)(2,1)S(1)}, bf16[128,1024]{1,0:T(8,128)(2,1)S(1)}, u32[]{:S(2)}, u32[]{:S(2)}) collective-permute-start(bf16[128,1024]{1,0:T(8,128)(2,1)S(1)} %get-tuple-element.38), channel_id=1, source_target_pairs={{0,1},{1,2},{2,3},{3,0},{4,5},{5,6},{6,7},{7,4},{8,9},{9,10},{10,1... | collective-permute-start | bytes 786440 | tf_op jit(solution)/shard_map/ppermute | solution.py:405
  31.5 9.2 %collective-permute-start.12 = (bf16[128,1024]{1,0:T(8,128)(2,1)S(1)}, bf16[128,1024]{1,0:T(8,128)(2,1)S(1)}, u32[]{:S(2)}, u32[]{:S(2)}) collective-permute-start(bf16[128,1024]{1,0:T(8,128)(2,1)S(1)} %get-tuple-element.42), channel_id=1, source_target_pairs={{0,3},{1,0},{2,1},{3,2},{4,7},{5,4},{6,5},{7,6},{8,11},{9,8},{10,9... | collective-permute-start | bytes 786440 | tf_op jit(solution)/shard_map/ppermute | solution.py:406
  36.1 10.0 %collective-permute-start.8 = (bf16[128,1024]{1,0:T(8,128)(2,1)S(1)}, bf16[128,1024]{1,0:T(8,128)(2,1)S(1)}, u32[]{:S(2)}, u32[]{:S(2)}) collective-permute-start(bf16[128,1024]{1,0:T(8,128)(2,1)S(1)} %get-tuple-element.36), channel_id=1, source_target_pairs={{0,3},{1,0},{2,1},{3,2},{4,7},{5,4},{6,5},{7,6},{8,11},{9,8},{10,9... | collective-permute-start | bytes 786440 | tf_op jit(solution)/shard_map/ppermute | solution.py:410
  37.7 8.4 %collective-permute-start.11 = (bf16[128,1024]{1,0:T(8,128)(2,1)S(1)}, bf16[128,1024]{1,0:T(8,128)(2,1)S(1)}, u32[]{:S(2)}, u32[]{:S(2)}) collective-permute-start(bf16[128,1024]{1,0:T(8,128)(2,1)S(1)} %get-tuple-element.40), channel_id=1, source_target_pairs={{0,1},{1,2},{2,3},{3,0},{4,5},{5,6},{6,7},{7,4},{8,9},{9,10},{10,1... | collective-permute-start | bytes 786440 | tf_op jit(solution)/shard_map/ppermute | solution.py:409
  38.2 10.6 %collective-permute-start.10 = (bf16[128,1024]{1,0:T(8,128)(2,1)S(1)}, bf16[128,1024]{1,0:T(8,128)(2,1)S(1)}, u32[]{:S(2)}, u32[]{:S(2)}) collective-permute-start(bf16[128,1024]{1,0:T(8,128)(2,1)S(1)} %add_convert_fusion.1), channel_id=1, source_target_pairs={{0,1},{1,2},{2,3},{3,0},{4,5},{5,6},{6,7},{7,4},{8,9},{9,10},{10,1... | collective-permute-start | bytes 786440 | tf_op jit(solution)/shard_map/ppermute | solution.py:411
  40.7 8.1 %collective-permute-start.13 = (bf16[128,1024]{1,0:T(8,128)(2,1)S(1)}, bf16[128,1024]{1,0:T(8,128)(2,1)S(1)}, u32[]{:S(2)}, u32[]{:S(2)}) collective-permute-start(bf16[128,1024]{1,0:T(8,128)(2,1)S(1)} %add_convert_fusion), channel_id=1, source_target_pairs={{0,3},{1,0},{2,1},{3,2},{4,7},{5,4},{6,5},{7,6},{8,11},{9,8},{10,9... | collective-permute-start | bytes 786440 | tf_op jit(solution)/shard_map/ppermute | solution.py:412

commit v3 on v2

v3 whole, which is shorter than its diff:
```python
import functools

import jax
import jax.numpy as jnp
from jax import lax
from jax.experimental import pallas as pl
from jax.experimental.pallas import tpu as pltpu
from jax.sharding import PartitionSpec as P

MODES = 16
LANES = 128
SUB = 8
ROWS = 16


CHUNKS = 4
CUT = 9
FAR, NEXT, LAST, MINE = 2, 1, 3, 0
STAGES = (
    (2, ((1, 1),), False),
    (4, ((1, 2), (3, 6), (2, 4)), False),
    (4, ((1, 8), (3, 24), (2, 16)), False),
    (2, ((1, 48),), False),
)
WORK = 1
HBM = pl.BlockSpec(memory_space=pltpu.HBM)
VMEM = pl.BlockSpec(memory_space=pltpu.VMEM)
DMA = pltpu.SemaphoreType.DMA


def in_hbm(array):
    return pltpu.with_memory_space_constraint(array, pltpu.HBM)


def params():
    return pltpu.CompilerParams(vmem_limit_bytes=24 * 2**20)


def cost(flops, size):
    return pl.CostEstimate(flops=flops, bytes_accessed=size, transcendentals=0)


def wide(*shape):
    return jax.ShapeDtypeStruct(shape, jnp.float32)


def short(*shape):
    return jax.ShapeDtypeStruct(shape, jnp.bfloat16)


def total_of(terms):
    while len(terms) > 1:
        terms = [sum(terms[j : j + 2]) for j in range(0, len(terms), 2)]
    return terms[0]


def fetch_columns(weight_hbm, turn, out_ref, sems, first=0):
    chans, width = out_ref.shape
    owner = lax.rem(lax.axis_index("tp") + turn, weight_hbm.shape[1] // width)
    columns = pl.ds(pl.multiple_of(owner * width, width), width)
    part = chans // CHUNKS
    copies = []
    for c in range(CHUNKS):
        rows = pl.ds(c * part, part)
        copies.append(
            pltpu.make_async_copy(weight_hbm.at[rows, columns], out_ref.at[rows, :], sems.at[first + c])
        )
        copies[-1].start()
    return copies


def wait_all(copies):
    for copy in copies:
        copy.wait()


def state_kernel(key_hbm, value_hbm, decay_hbm, residue_hbm, skip_hbm,
                 state_ref, keyed_ref, decay_ref, residue_ref, skip_ref,
                 key_buf, value_buf, mode_buf, turn_buf, sems):
    length, chans = key_buf.shape
    groups = chans // LANES
    span = groups * SUB
    part = length // CHUNKS
    small = []
    for n, src in enumerate((decay_hbm, residue_hbm)):
        small.append(pltpu.make_async_copy(src, mode_buf.at[n], sems.at[2 * CHUNKS + n]))
    small[0].start()
    copies = []
    for c in range(CHUNKS):
        rows = pl.ds(c * part, part)
        copies.append((
            pltpu.make_async_copy(key_hbm.at[rows, :], key_buf.at[rows, :], sems.at[2 * c]),
            pltpu.make_async_copy(value_hbm.at[rows, :], value_buf.at[rows, :], sems.at[2 * c + 1]),
        ))
        for copy in copies[-1]:
            copy.start()
    small[1].start()
    skip = pltpu.make_async_copy(skip_hbm, skip_ref, sems.at[2 * CHUNKS + 2])
    skip.start()

    def turn(which, out_ref):
        small[which].wait()
        for m in range(MODES // SUB):
            for g in range(groups):
                turn_buf[(m * groups + g) * SUB : (m * groups + g + 1) * SUB, :] = mode_buf[
                    which, m * SUB : (m + 1) * SUB, g * LANES : (g + 1) * LANES
                ]
        for r in range(MODES):
            out_ref[r] = turn_buf[pl.ds(r // SUB * span + r % SUB, groups, stride=SUB), :]

    turn(0, decay_ref)
    step = [jnp.exp(-decay_ref[r]) for r in range(MODES)]

    def block(i, held):
        rows = pl.ds(pl.multiple_of(i * ROWS, ROWS), ROWS)
        keyed = key_buf[rows, :].astype(jnp.float32) * value_buf[rows, :].astype(jnp.float32)
        for half in range(ROWS // SUB):
            base = (i * (ROWS // SUB) + half) * span
            for g in range(groups):
                keyed_ref[pl.ds(pl.multiple_of(base + g * SUB, SUB), SUB), :] = keyed[
                    half * SUB : (half + 1) * SUB, g * LANES : (g + 1) * LANES
                ]
        for half in range(ROWS // SUB):
            base = (i * (ROWS // SUB) + half) * span
            for s in range(SUB):
                now = keyed_ref[pl.ds(base + s, groups, stride=SUB), :]
                held = [a * h + now for a, h in zip(step, held)]
        return held

    held = [jnp.zeros((groups, LANES), jnp.float32)] * MODES
    for c in range(CHUNKS):
        for copy in copies[c]:
            copy.wait()
        held = lax.fori_loop(c * (part // ROWS), (c + 1) * (part // ROWS), block, held)
    for r in range(MODES):
        state_ref[r] = held[r]
    turn(1, residue_ref)
    skip.wait()


def block_state(gate_key, value_in, decay, residue, skip):
    length, chans = gate_key.shape
    groups = chans // LANES
    modes = wide(MODES, groups, LANES)
    return pl.pallas_call(
        state_kernel,
        out_shape=(modes, wide(length * groups, LANES), modes, modes, wide(groups, LANES)),
        in_specs=[HBM] * 5,
        out_specs=(VMEM,) * 5,
        scratch_shapes=[
            pltpu.VMEM((length, chans), jnp.bfloat16),
            pltpu.VMEM((length, chans), jnp.bfloat16),
            pltpu.VMEM((2, MODES, chans), jnp.float32),
            pltpu.VMEM((MODES * groups, LANES), jnp.float32),
            DMA((2 * CHUNKS + 3,)),
        ],
        compiler_params=params(),
        cost_estimate=cost(2**23, 2**23),
    )(*(in_hbm(x) for x in (gate_key, value_in, decay, residue, skip)))


def local_kernel(members, apart, keyed_ref, decay_ref, scale_ref, _, skip_ref, local_ref, ahead_ref):
    groups = decay_ref.shape[1]
    span = groups * SUB
    ahead = (members - 1 - lax.axis_index("ctx") // apart % members) * apart * (keyed_ref.shape[0] // groups)
    for r in range(MODES):
        ahead_ref[r] = jnp.exp(-decay_ref[r] * ahead.astype(jnp.float32))
    step = [jnp.exp(-decay_ref[r]) for r in range(MODES)]
    scale = [scale_ref[r] for r in range(MODES)]
    skip = skip_ref[...]

    def block(i, held):
        for s in range(SUB):
            at = pl.ds(i * span + s, groups, stride=SUB)
            now = keyed_ref[at, :]
            held = [a * h + now for a, h in zip(step, held)]
            local_ref[at, :] = total_of([c * h for c, h in zip(scale, held)] + [skip * now])
        return held

    lax.fori_loop(0, keyed_ref.shape[0] // span, block, [jnp.zeros((groups, LANES), jnp.float32)] * MODES)


def local_part(members, apart, keyed, decay, scale, behind, skip):
    return pl.pallas_call(
        functools.partial(local_kernel, members, apart),
        out_shape=(wide(*keyed.shape), wide(*decay.shape)),
        in_specs=[VMEM] * 5,
        out_specs=(VMEM, VMEM),
        compiler_params=params(),
        cost_estimate=cost(2**23, 2**22),
    )(keyed, decay, scale, behind, skip)


def apply_gate(mixing, query_ref, gated_ref):
    length, chans = gated_ref.shape
    groups = chans // LANES

    def block(i, _):
        rows = pl.ds(pl.multiple_of(i * ROWS, ROWS), ROWS)
        for g in range(groups):
            cols = slice(g * LANES, (g + 1) * LANES)
            tiles = [mixing(i * (ROWS // SUB) + half, g) for half in range(ROWS // SUB)]
            gated_ref[rows, cols] = (
                query_ref[rows, cols].astype(jnp.float32) * jnp.concatenate(tiles, axis=0)
            ).astype(jnp.bfloat16)
        return 0

    lax.fori_loop(0, length // ROWS, block, 0)


def add_tail(base_ref, decay_ref, start_ref, mix_ref):
    groups = decay_ref.shape[1]
    span = groups * SUB
    step = [jnp.exp(-decay_ref[r]) for r in range(MODES)]

    def block(i, held):
        for s in range(SUB):
            at = pl.ds(i * span + s, groups, stride=SUB)
            mix_ref[at, :] = base_ref[at, :] + total_of(held)
            held = [a * h for a, h in zip(step, held)]
        return held

    lax.fori_loop(0, mix_ref.shape[0] // span, block, [start_ref[r] for r in range(MODES)])


def tile_of(mix_ref, groups):
    def tile(i, g):
        return mix_ref[pl.ds(pl.multiple_of((i * groups + g) * SUB, SUB), SUB), :]

    return tile


def in_upper_half():
    return lax.axis_index("ctx") >= lax.axis_size("ctx") // 2


def begin_kernel(local_ref, decay_ref, start_ref, _, query_hbm, weight_hbm,
                 mix_ref, query_ref, far_ref, next_ref, gated_ref, far_top, far_low, sems):
    upper = in_upper_half()
    query_copy = pltpu.make_async_copy(query_hbm, query_ref, sems.at[CHUNKS])
    query_copy.start()
    far_copies = fetch_columns(weight_hbm, FAR, far_ref, sems)
    next_copies = fetch_columns(weight_hbm, NEXT, next_ref, sems, CHUNKS + 1)
    add_tail(local_ref, decay_ref, start_ref, mix_ref)
    query_copy.wait()

    @pl.when(jnp.logical_not(upper))
    def _():
        apply_gate(tile_of(mix_ref, decay_ref.shape[1]), query_ref, gated_ref)

    wait_all(far_copies)

    @pl.when(jnp.logical_not(upper))
    def _():
        project(gated_ref, far_ref, far_top, far_low)

    wait_all(next_copies)


def begin_part(local, decay, start, behind, gate_query, weight, ring):
    length, chans = gate_query.shape
    width = weight.shape[1] // ring
    columns = short(chans, width)
    top, low = cut_rows(length, width)
    return pl.pallas_call(
        begin_kernel,
        out_shape=(wide(*local.shape), short(length, chans), columns, columns, short(length, chans), short(*top), short(*low)),
        in_specs=[VMEM] * 4 + [HBM] * 2,
        out_specs=(VMEM,) * 7,
        scratch_shapes=[DMA((2 * CHUNKS + 1,))],
        compiler_params=params(),
        cost_estimate=cost(2**23, 2**22),
    )(local, decay, start, behind, in_hbm(gate_query), in_hbm(weight))


def end_kernel(mix_ref, query_ref, far_ref, gated_in, top_in, low_in, decay_ref, start_ref,
               gated_ref, far_top, far_low, sum_ref):
    upper = in_upper_half()

    @pl.when(upper)
    def _():
        add_tail(mix_ref, decay_ref, start_ref, sum_ref)
        apply_gate(tile_of(sum_ref, decay_ref.shape[1]), query_ref, gated_ref)
        project(gated_ref, far_ref, far_top, far_low)

    @pl.when(jnp.logical_not(upper))
    def _():
        for source, out in ((gated_in, gated_ref), (top_in, far_top), (low_in, far_low)):
            out[...] = source[...]


def end_part(begun, decay, start):
    mix, query, far, _, gated, top, low = begun
    return pl.pallas_call(
        end_kernel,
        out_shape=(short(*gated.shape), short(*top.shape), short(*low.shape)),
        in_specs=[VMEM] * 8,
        out_specs=(VMEM,) * 3,
        scratch_shapes=[pltpu.VMEM(mix.shape, jnp.float32)],
        compiler_params=params(),
        cost_estimate=cost(2**29, 2**20),
    )(mix, query, far, gated, top, low, decay, start)


def cut_rows(length, width):
    cut = length * CUT // 16
    return (cut, width), (length - cut, width)


def project(gated_ref, columns_ref, *outs):
    row = 0
    for out in outs:
        rows = slice(row, row + out.shape[0])
        out[...] = jnp.dot(
            gated_ref[rows, :], columns_ref[...], preferred_element_type=jnp.float32
        ).astype(out.dtype)
        row += out.shape[0]


def next_part(gated, columns):
    top, low = cut_rows(gated.shape[0], columns.shape[1])
    return pl.pallas_call(
        project,
        out_shape=(wide(*top), short(*low)),
        in_specs=[VMEM, VMEM],
        out_specs=(VMEM, VMEM),
        compiler_params=params(),
        cost_estimate=cost(2**29, 2**20),
    )(gated, columns)


def fetch_and_project(turn, gated_ref, weight_hbm, _, top_ref, low_ref, columns_ref, sems):
    wait_all(fetch_columns(weight_hbm, turn, columns_ref, sems))
    project(gated_ref, columns_ref, top_ref, low_ref)


def fetched_part(turn, out_shape, gated, weight, behind, ring):
    return pl.pallas_call(
        functools.partial(fetch_and_project, turn),
        out_shape=out_shape,
        in_specs=[VMEM, HBM, VMEM],
        out_specs=(VMEM, VMEM),
        scratch_shapes=[pltpu.VMEM((gated.shape[1], weight.shape[1] // ring), jnp.bfloat16), DMA((CHUNKS,))],
        compiler_params=params(),
        cost_estimate=cost(2**29, 2**21),
    )(gated, in_hbm(weight), behind)


def last_part(gated, weight, behind, ring):
    top, low = cut_rows(gated.shape[0], weight.shape[1] // ring)
    return fetched_part(LAST, (short(*top), wide(*low)), gated, weight, behind, ring)


def own_part(gated, weight, behind, ring):
    top, low = cut_rows(gated.shape[0], weight.shape[1] // ring)
    return fetched_part(MINE, (wide(*top), wide(*low)), gated, weight, behind, ring)


def finish_kernel(mine_top, near_top, both_top, mine_low, near_low, both_low, out_hbm, out_buf, sems):
    row = 0
    copies = []
    for n, (mine, near, both) in enumerate(
        ((mine_top, near_top, both_top), (mine_low, near_low, both_low))
    ):
        rows = pl.ds(row, mine.shape[0])
        out_buf[rows, :] = (
            mine[...] + near[...].astype(jnp.float32) + both[...].astype(jnp.float32)
        ).astype(jnp.bfloat16)
        copies.append(pltpu.make_async_copy(out_buf.at[rows, :], out_hbm.at[rows, :], sems.at[n]))
        copies[-1].start()
        row += mine.shape[0]
    wait_all(copies)


def finish(*parts):
    length, width = parts[0].shape[0] + parts[3].shape[0], parts[0].shape[1]
    return pl.pallas_call(
        finish_kernel,
        out_shape=short(length, width),
        in_specs=[VMEM] * 6,
        out_specs=HBM,
        scratch_shapes=[pltpu.VMEM((length, width), jnp.bfloat16), DMA((2,))],
        compiler_params=params(),
        cost_estimate=cost(2**19, 2**21),
    )(*parts)


def scan_over_ctx(state, decay, length, index, work, load):
    devices = lax.axis_size("ctx")

    def power(blocks):
        blocks = jnp.asarray(blocks)
        reach = (length * jnp.maximum(blocks, 0)).astype(jnp.float32)
        return jnp.where(blocks >= 0, jnp.exp(-decay * reach), 0.0)

    total, before = state, jnp.zeros_like(state)
    span = 1
    for stage, (members, moves, forward) in enumerate(STAGES):
        mine, inside = index // span % members, index % span
        sent = total.astype(jnp.bfloat16)
        own = work(sent, members, span) if stage == WORK else power((members - 1 - mine) * span)
        if stage == len(STAGES) - 1:
            load(sent, before)
            before = jnp.zeros_like(state)
        got = []
        for k, flip in moves:
            pairs = [(i, i ^ flip) for i in range(devices)]
            if forward:
                pairs = [(i, j) for i, j in pairs if i < j]
            got.append((k, lax.ppermute(sent, "ctx", pairs).astype(jnp.float32)))
        total = total * own
        for k, theirs in got:
            other = mine ^ k
            before = before + theirs * power(
                jnp.where(other < mine, (mine - 1 - other) * span + inside, -1)
            )
            total = total + theirs * power((members - 1 - other) * span)
        span *= members
    return before


def on_device(gate_query, gate_key, value_in, residues, decay_rate, skip_gain, out_weight):
    index = lax.axis_index("ctx")
    length, chans = gate_key.shape
    groups = chans // LANES
    ring = lax.axis_size("tp")
    forth = [(i, (i + NEXT) % ring) for i in range(ring)]
    back = [(i, (i + LAST) % ring) for i in range(ring)]

    state, keyed, decay, residue, skip = block_state(
        gate_key, value_in, decay_rate.T, residues.T, skip_gain.reshape(groups, LANES)
    )
    scale = residue * jnp.sqrt(-jnp.expm1(-2.0 * decay))
    local = None

    def work(sent, members, apart):
        nonlocal local
        local, ahead = local_part(members, apart, keyed, decay, scale, sent, skip)
        return ahead

    entry = scale * jnp.exp(-decay)

    def load(sent, before):
        nonlocal begun
        begun = begin_part(local, decay, entry * before, sent, gate_query, out_weight, ring)

    begun = None
    carry = scan_over_ctx(state, decay, length, index, work, load)
    gated, far_top, far_low = end_part(begun, decay, entry * carry)
    far_a = lax.ppermute(far_top, "tp", forth)
    far_b = lax.ppermute(far_low, "tp", back)
    next_top, next_low = next_part(gated, begun[3])
    near_b = lax.ppermute(next_low, "tp", forth)
    last_top, last_low = last_part(gated, out_weight, next_low, ring)
    near_a = lax.ppermute(last_top, "tp", back)
    mine_top, mine_low = own_part(gated, out_weight, last_top, ring)
    both_a = lax.ppermute((next_top + far_a.astype(jnp.float32)).astype(jnp.bfloat16), "tp", forth)
    both_b = lax.ppermute((last_low + far_b.astype(jnp.float32)).astype(jnp.bfloat16), "tp", back)
    return finish(mine_top, near_a, both_a, mine_low, near_b, both_b)


def solution(mesh):
    in_specs = (
        P("ctx", "tp"),
        P("ctx", "tp"),
        P("ctx", "tp"),
        P("tp", None),
        P("tp", None),
        P("tp"),
        P("tp", None),
    )
    return jax.shard_map(
        on_device, mesh=mesh, in_specs=in_specs, out_specs=P("ctx", "tp"), check_vma=False
    )
```

time: 50 us -> 48.8 us (0.976)
  Pallas kernels: 14.8 us -> 14 us
  waiting for transfers between devices: 9.39 us -> 8.6 us
    ppermute x1, waiting for transfers between devices: 1.11 us -> 0.01 us  [on_device(): far_b = lax.ppermute(far_low, 'tp', back)]
    ppermute x1, waiting for transfers between devices: 0.01 us -> 0.93 us  [on_device(): far_a = lax.ppermute(far_top, 'tp', forth)]
    pallas_call x6 -> x7, Pallas kernels: 12.3 us -> 11.5 us  [the longest x2 4.66 us: fetched_part(): pl.pallas_call(functools.partial(fetch_and_project, turn), out_shape=out_...]
  transfers between devices with their start and end apart: 14 -> 14, of which waited for: 7 -> 7; matrix products, arithmetic and copies ran while one was open for 0% -> 1% of each run, Pallas kernels for 19% -> 22%
where the time goes in v3:
time: 48.8 us; the launch traced here: 48.6 us
  starting transfers between devices  25.3 us (52%)
  Pallas kernels  14 us (29%)
  waiting for transfers between devices  8.6 us (18%)
  other arithmetic  0.59 us (1%)
    ppermute x8, starting transfers between devices, scan_over_ctx(): got.append((k, lax.ppermute(sent, 'ctx', pairs).astype(jnp.float32)))  15.2 us
    ppermute x8, waiting for transfers between devices, scan_over_ctx(): got.append((k, lax.ppermute(sent, 'ctx', pairs).astype(jnp.float32)))  5.05 us
    pallas_call x2, Pallas kernels, fetched_part(): pl.pallas_call(functools.partial(fetch_and_project, turn), out_shape=out_...  4.66 us
    ppermute x1, starting transfers between devices, on_device(): near_a = lax.ppermute(last_top, 'tp', back)  3.02 us
    pallas_call x1, Pallas kernels, begin_part(): pl.pallas_call(begin_kernel, out_shape=(wide(*local.shape), short(length,...  2.55 us
    ppermute x1, starting transfers between devices, on_device(): lax.ppermute((last_low + far_b.astype(jnp.float32)).astype(jnp.bfloat16),...  2.54 us
    pallas_call x1, Pallas kernels, local_part(): pl.pallas_call(functools.partial(local_kernel, members, apart), out_shape...  2.52 us
    pallas_call x1, Pallas kernels, block_state(): pl.pallas_call(state_kernel, out_shape=(modes, wide(length * groups, LANE...  2.51 us
  transfers between devices with their start and end apart: 14, of which 7 were waited for; matrix products, arithmetic and copies ran while one was open for 1% of the time, Pallas kernels for 22%

profile of v3, /device:TPU:32, one launch (start us, length us, event | category | flops | bytes accessed | tf_op | source)
XLA Modules:
  0.0 48.6 jit_solution(16817590886936657053)
XLA Ops:
  0.0 2.5 %shard_map.73 = (f32[16,8,128]{2,1,0:T(8,128)S(1)}, f32[2048,128]{1,0:T(8,128)S(1)}, f32[16,8,128]{2,1,0:T(8,128)S(1)}, f32[16,8,128]{2,1,0:T(8,128)S(1)}, f32[8,128]{1,0:T(8,128)S(1)}) custom-call(bf16[256,1024]{1,0:T(8,128)(2,1)} %key_hbm.1, bf16[256,1024]{1,0:T(8,128)(2,1)} %value_hbm.1, f32[16,1024]{1,0:T(8,128)} %bitcast.3, f32[16,1024]{1,0:T(8,128)} %bitcast.4, ...), custom_call_target="tpu_custom_call" | custom-call | flops 8388608 | bytes 8388608 | tf_op jit(solution)/shard_map/pallas_call | solution.py:145
  2.7 1.2 %collective-permute-done = bf16[16,8,128]{2,1,0:T(8,128)(2,1)S(1)} collective-permute-done((bf16[16,8,128]{2,1,0:T(8,128)(2,1)S(1)}, bf16[16,8,128]{2,1,0:T(8,128)(2,1)S(1)}, u32[]{:S(2)}, u32[]{:S(2)}) %collective-permute-start) | collective-permute-done | bytes 32800 | tf_op jit(solution)/shard_map/ppermute | solution.py:410
  3.9 3.3 %collective-permute-start.3 = (bf16[16,8,128]{2,1,0:T(8,128)(2,1)S(1)}, bf16[16,8,128]{2,1,0:T(8,128)(2,1)S(1)}, u32[]{:S(2)}, u32[]{:S(2)}) collective-permute-start(bf16[16,8,128]{2,1,0:T(8,128)(2,1)S(1)} %get-tuple-element.53._), channel_id=1, source_target_pairs={{0,16},{4,20},{8,24},{12,28},{16,0},{20,4},{24,8},{28,12},{32,48},... | collective-permute-start | bytes 98312 | tf_op jit(solution)/shard_map/ppermute | solution.py:410
  7.2 1.1 %collective-permute-start.2 = (bf16[16,8,128]{2,1,0:T(8,128)(2,1)S(1)}, bf16[16,8,128]{2,1,0:T(8,128)(2,1)S(1)}, u32[]{:S(2)}, u32[]{:S(2)}) collective-permute-start(bf16[16,8,128]{2,1,0:T(8,128)(2,1)S(1)} %get-tuple-element.53._), channel_id=1, source_target_pairs={{0,24},{4,28},{8,16},{12,20},{16,8},{20,12},{24,0},{28,4},{32,56},... | collective-permute-start | bytes 98312 | tf_op jit(solution)/shard_map/ppermute | solution.py:410
  8.2 2.5 %shard_map.74 = (f32[2048,128]{1,0:T(8,128)S(1)}, f32[16,8,128]{2,1,0:T(8,128)S(1)}) custom-call(f32[2048,128]{1,0:T(8,128)S(1)} %get-tuple-element.28.keyed_ref, f32[16,8,128]{2,1,0:T(8,128)S(1)} %get-tuple-element.29.decay_ref, f32[16,8,128]{2,1,0:T(8,128)S(1)} %get-tuple-element.54.scale_ref, bf16[16,8,128]{2,1,0:T(8,128)(2,1)S(1)} %get-tuple-element.53._, ...), custom_call_target="tpu_custom_call" | custom-call | flops 8388608 | bytes 4194304 | tf_op jit(solution)/shard_map/pallas_call | solution.py:184
  10.8 1.5 %collective-permute-done.2 = bf16[16,8,128]{2,1,0:T(8,128)(2,1)S(1)} collective-permute-done((bf16[16,8,128]{2,1,0:T(8,128)(2,1)S(1)}, bf16[16,8,128]{2,1,0:T(8,128)(2,1)S(1)}, u32[]{:S(2)}, u32[]{:S(2)}) %collective-permute-start.2) | collective-permute-done | bytes 32800 | tf_op jit(solution)/shard_map/ppermute | solution.py:410
  12.4 3.4 %collective-permute-start.6 = (bf16[16,8,128]{2,1,0:T(8,128)(2,1)S(1)}, bf16[16,8,128]{2,1,0:T(8,128)(2,1)S(1)}, u32[]{:S(2)}, u32[]{:S(2)}) collective-permute-start(bf16[16,8,128]{2,1,0:T(8,128)(2,1)S(1)} %get-tuple-element.51), channel_id=1, source_target_pairs={{0,64},{4,68},{8,72},{12,76},{16,80},{20,84},{24,88},{28,92},{32,9... | collective-permute-start | bytes 98312 | tf_op jit(solution)/shard_map/ppermute | solution.py:410
  15.8 1.6 %collective-permute-start.4 = (bf16[16,8,128]{2,1,0:T(8,128)(2,1)S(1)}, bf16[16,8,128]{2,1,0:T(8,128)(2,1)S(1)}, u32[]{:S(2)}, u32[]{:S(2)}) collective-permute-start(bf16[16,8,128]{2,1,0:T(8,128)(2,1)S(1)} %get-tuple-element.51), channel_id=1, source_target_pairs={{0,32},{4,36},{8,40},{12,44},{16,48},{20,52},{24,56},{28,60},{32,0... | collective-permute-start | bytes 98312 | tf_op jit(solution)/shard_map/ppermute | solution.py:410
  17.3 0.6 %collective-permute-done.6 = bf16[16,8,128]{2,1,0:T(8,128)(2,1)S(1)} collective-permute-done((bf16[16,8,128]{2,1,0:T(8,128)(2,1)S(1)}, bf16[16,8,128]{2,1,0:T(8,128)(2,1)S(1)}, u32[]{:S(2)}, u32[]{:S(2)}) %collective-permute-start.6) | collective-permute-done | bytes 32800 | tf_op jit(solution)/shard_map/ppermute | solution.py:410
  18.0 1.7 %collective-permute-done.5 = bf16[16,8,128]{2,1,0:T(8,128)(2,1)S(1)} collective-permute-done((bf16[16,8,128]{2,1,0:T(8,128)(2,1)S(1)}, bf16[16,8,128]{2,1,0:T(8,128)(2,1)S(1)}, u32[]{:S(2)}, u32[]{:S(2)}) %collective-permute-start.5) | collective-permute-done | bytes 32800 | tf_op jit(solution)/shard_map/ppermute | solution.py:410
  19.8 5.8 %collective-permute-start.7 = (bf16[16,8,128]{2,1,0:T(8,128)(2,1)S(1)}, bf16[16,8,128]{2,1,0:T(8,128)(2,1)S(1)}, u32[]{:S(2)}, u32[]{:S(2)}) collective-permute-start(bf16[16,8,128]{2,1,0:T(8,128)(2,1)S(1)} %fusion.14._), channel_id=1, source_target_pairs={{0,192},{4,196},{8,200},{12,204},{16,208},{20,212},{24,216},{28,22... | collective-permute-start | bytes 98312 | tf_op jit(solution)/shard_map/ppermute | solution.py:410
  25.7 2.6 %shard_map.75 = (f32[2048,128]{1,0:T(8,128)S(1)}, bf16[256,1024]{1,0:T(8,128)(2,1)S(1)}, bf16[1024,1024]{1,0:T(8,128)(2,1)S(1)}, bf16[1024,1024]{1,0:T(8,128)(2,...) custom-call(f32[2048,128]{1,0:T(8,128)S(1)} %get-tuple-element.33.local_ref, ...), custom_call_target="tpu_custom_call" | custom-call | flops 8388608 | bytes 4194304 | tf_op jit(solution)/shard_map/pallas_call | solution.py:265
  28.5 1.6 %collective-permute-start.9 = (bf16[144,1024]{1,0:T(8,128)(2,1)S(1)}, bf16[144,1024]{1,0:T(8,128)(2,1)S(1)}, u32[]{:S(2)}, u32[]{:S(2)}) collective-permute-start(bf16[144,1024]{1,0:T(8,128)(2,1)S(1)} %get-tuple-element.47), channel_id=1, source_target_pairs={{0,1},{1,2},{2,3},{3,0},{4,5},{5,6},{6,7},{7,4},{8,9},{9,10},{10,1... | collective-permute-start | bytes 884744 | tf_op jit(solution)/shard_map/ppermute | solution.py:450
  30.1 1.7 %collective-permute-start.12 = (bf16[112,1024]{1,0:T(8,128)(2,1)S(1)}, bf16[112,1024]{1,0:T(8,128)(2,1)S(1)}, u32[]{:S(2)}, u32[]{:S(2)}) collective-permute-start(bf16[112,1024]{1,0:T(8,128)(2,1)S(1)} %get-tuple-element.50), channel_id=1, source_target_pairs={{0,3},{1,0},{2,1},{3,2},{4,7},{5,4},{6,5},{7,6},{8,11},{9,8},{10,9... | collective-permute-start | bytes 688136 | tf_op jit(solution)/shard_map/ppermute | solution.py:451
  31.8 0.8 %shard_map.77 = (f32[144,1024]{1,0:T(8,128)S(1)}, bf16[112,1024]{1,0:T(8,128)(2,1)S(1)}) custom-call(bf16[256,1024]{1,0:T(8,128)(2,1)S(1)} %get-tuple-element.41.gated_ref, bf16[1024,1024]{1,0:T(8,128)(2,1)S(1)} %get-tuple-element.42.columns_ref), custom_call_target="tpu_custom_call" | custom-call | flops 536870912 | bytes 1048576 | tf_op jit(solution)/shard_map/pallas_call | solution.py:322
  32.9 2.3 %shard_map.78 = (bf16[144,1024]{1,0:T(8,128)(2,1)S(1)}, f32[112,1024]{1,0:T(8,128)S(1)}) custom-call(bf16[256,1024]{1,0:T(8,128)(2,1)S(1)} %get-tuple-element.41.gated_ref, bf16[1024,4096]{1,0:T(8,128)(2,1)} %weight_hbm.5, bf16[112,1024]{1,0:T(8,128)(2,1)S(1)} %get-tuple-element.43._), custom_call_target="tpu_custom_call" | custom-call | flops 536870912 | bytes 2097152 | tf_op jit(solution)/shard_map/pallas_call | solution.py:338
  35.3 3.0 %collective-permute-start.8 = (bf16[144,1024]{1,0:T(8,128)(2,1)S(1)}, bf16[144,1024]{1,0:T(8,128)(2,1)S(1)}, u32[]{:S(2)}, u32[]{:S(2)}) collective-permute-start(bf16[144,1024]{1,0:T(8,128)(2,1)S(1)} %get-tuple-element.44._), channel_id=1, source_target_pairs={{0,3},{1,0},{2,1},{3,2},{4,7},{5,4},{6,5},{7,6},{8,11},{9,8},{10,9... | collective-permute-start | bytes 884744 | tf_op jit(solution)/shard_map/ppermute | solution.py:455
  38.3 0.9 %collective-permute-done.9 = bf16[144,1024]{1,0:T(8,128)(2,1)S(1)} collective-permute-done((bf16[144,1024]{1,0:T(8,128)(2,1)S(1)}, bf16[144,1024]{1,0:T(8,128)(2,1)S(1)}, u32[]{:S(2)}, u32[]{:S(2)}) %collective-permute-start.9) | collective-permute-done | bytes 294944 | tf_op jit(solution)/shard_map/ppermute | solution.py:450
  39.3 0.8 %collective-permute-start.10 = (bf16[144,1024]{1,0:T(8,128)(2,1)S(1)}, bf16[144,1024]{1,0:T(8,128)(2,1)S(1)}, u32[]{:S(2)}, u32[]{:S(2)}) collective-permute-start(bf16[144,1024]{1,0:T(8,128)(2,1)S(1)} %add_convert_fusion), channel_id=1, source_target_pairs={{0,1},{1,2},{2,3},{3,0},{4,5},{5,6},{6,7},{7,4},{8,9},{9,10},{10,1... | collective-permute-start | bytes 884744 | tf_op jit(solution)/shard_map/ppermute | solution.py:457
  40.2 2.5 %collective-permute-start.13 = (bf16[112,1024]{1,0:T(8,128)(2,1)S(1)}, bf16[112,1024]{1,0:T(8,128)(2,1)S(1)}, u32[]{:S(2)}, u32[]{:S(2)}) collective-permute-start(bf16[112,1024]{1,0:T(8,128)(2,1)S(1)} %add_convert_fusion.1), channel_id=1, source_target_pairs={{0,3},{1,0},{2,1},{3,2},{4,7},{5,4},{6,5},{7,6},{8,11},{9,8},{10,9... | collective-permute-start | bytes 688136 | tf_op jit(solution)/shard_map/ppermute | solution.py:458
  42.8 2.3 %shard_map.79 = (f32[144,1024]{1,0:T(8,128)S(1)}, f32[112,1024]{1,0:T(8,128)S(1)}) custom-call(bf16[256,1024]{1,0:T(8,128)(2,1)S(1)} %get-tuple-element.41.gated_ref, bf16[1024,4096]{1,0:T(8,128)(2,1)} %weight_hbm.5, bf16[144,1024]{1,0:T(8,128)(2,1)S(1)} %get-tuple-element.44._), custom_call_target="tpu_custom_call" | custom-call | flops 536870912 | bytes 2097152 | tf_op jit(solution)/shard_map/pallas_call | solution.py:338
  45.1 2.2 %collective-permute-done.13.both_low = bf16[112,1024]{1,0:T(8,128)(2,1)S(1)} collective-permute-done((bf16[112,1024]{1,0:T(8,128)(2,1)S(1)}, bf16[112,1024]{1,0:T(8,128)(2,1)S(1)}, u32[]{:S(2)}, u32[]{:S(2)}) %collective-permute-start.13) | collective-permute-done | bytes 229408 | tf_op jit(solution)/shard_map/ppermute | solution.py:458
  47.3 0.4 collective-permute-done.10.both_top
  47.7 0.9 %shard_map.80 = bf16[256,1024]{1,0:T(8,128)(2,1)} custom-call(f32[144,1024]{1,0:T(8,128)S(1)} %get-tuple-element.45.mine_top, bf16[144,1024]{1,0:T(8,128)(2,1)S(1)} %collective-permute-done.8.near_top, bf16[144,1024]{1,0:T(8,128)(2,1)S(1)} %collective-permute-done.10.both_top, f32[112,1024]{1,0:T(8,128)S(1)} %get-tuple-element.48.mine_low, ...), custom_call_target="tpu_custom_call" | custom-call | flops 524288 | bytes 2097152 | tf_op jit(solution)/shard_map/pallas_call | solution.py:377
  (20 shorter events, 1.2 us)
Async XLA Ops:
  2.5 1.3 %collective-permute-start = (bf16[16,8,128]{2,1,0:T(8,128)(2,1)S(1)}, bf16[16,8,128]{2,1,0:T(8,128)(2,1)S(1)}, u32[]{:S(2)}, u32[]{:S(2)}) collective-permute-start(bf16[16,8,128]{2,1,0:T(8,128)(2,1)S(1)} %convert_element_type.100), channel_id=1, source_target_pairs={{0,4},{4,0},{8,12},{12,8},{16,20},{20,16},{24,28},{28,24},{32,36},... | collective-permute-start | bytes 98312 | tf_op jit(solution)/shard_map/ppermute | solution.py:410
  3.9 6.9 %collective-permute-start.3 = (bf16[16,8,128]{2,1,0:T(8,128)(2,1)S(1)}, bf16[16,8,128]{2,1,0:T(8,128)(2,1)S(1)}, u32[]{:S(2)}, u32[]{:S(2)}) collective-permute-start(bf16[16,8,128]{2,1,0:T(8,128)(2,1)S(1)} %get-tuple-element.53._), channel_id=1, source_target_pairs={{0,16},{4,20},{8,24},{12,28},{16,0},{20,4},{24,8},{28,12},{32,48},... | collective-permute-start | bytes 98312 | tf_op jit(solution)/shard_map/ppermute | solution.py:410
  7.2 5.1 %collective-permute-start.2 = (bf16[16,8,128]{2,1,0:T(8,128)(2,1)S(1)}, bf16[16,8,128]{2,1,0:T(8,128)(2,1)S(1)}, u32[]{:S(2)}, u32[]{:S(2)}) collective-permute-start(bf16[16,8,128]{2,1,0:T(8,128)(2,1)S(1)} %get-tuple-element.53._), channel_id=1, source_target_pairs={{0,24},{4,28},{8,16},{12,20},{16,8},{20,12},{24,0},{28,4},{32,56},... | collective-permute-start | bytes 98312 | tf_op jit(solution)/shard_map/ppermute | solution.py:410
  8.2 4.1 %collective-permute-start.1 = (bf16[16,8,128]{2,1,0:T(8,128)(2,1)S(1)}, bf16[16,8,128]{2,1,0:T(8,128)(2,1)S(1)}, u32[]{:S(2)}, u32[]{:S(2)}) collective-permute-start(bf16[16,8,128]{2,1,0:T(8,128)(2,1)S(1)} %get-tuple-element.53._), channel_id=1, source_target_pairs={{0,8},{4,12},{8,0},{12,4},{16,24},{20,28},{24,16},{28,20},{32,40},... | collective-permute-start | bytes 98312 | tf_op jit(solution)/shard_map/ppermute | solution.py:410
  12.4 5.6 %collective-permute-start.6 = (bf16[16,8,128]{2,1,0:T(8,128)(2,1)S(1)}, bf16[16,8,128]{2,1,0:T(8,128)(2,1)S(1)}, u32[]{:S(2)}, u32[]{:S(2)}) collective-permute-start(bf16[16,8,128]{2,1,0:T(8,128)(2,1)S(1)} %get-tuple-element.51), channel_id=1, source_target_pairs={{0,64},{4,68},{8,72},{12,76},{16,80},{20,84},{24,88},{28,92},{32,9... | collective-permute-start | bytes 98312 | tf_op jit(solution)/shard_map/ppermute | solution.py:410
  15.8 3.9 %collective-permute-start.5 = (bf16[16,8,128]{2,1,0:T(8,128)(2,1)S(1)}, bf16[16,8,128]{2,1,0:T(8,128)(2,1)S(1)}, u32[]{:S(2)}, u32[]{:S(2)}) collective-permute-start(bf16[16,8,128]{2,1,0:T(8,128)(2,1)S(1)} %get-tuple-element.51), channel_id=1, source_target_pairs={{0,96},{4,100},{8,104},{12,108},{16,112},{20,116},{24,120},{28,124... | collective-permute-start | bytes 98312 | tf_op jit(solution)/shard_map/ppermute | solution.py:410
  15.8 3.9 %collective-permute-start.4 = (bf16[16,8,128]{2,1,0:T(8,128)(2,1)S(1)}, bf16[16,8,128]{2,1,0:T(8,128)(2,1)S(1)}, u32[]{:S(2)}, u32[]{:S(2)}) collective-permute-start(bf16[16,8,128]{2,1,0:T(8,128)(2,1)S(1)} %get-tuple-element.51), channel_id=1, source_target_pairs={{0,32},{4,36},{8,40},{12,44},{16,48},{20,52},{24,56},{28,60},{32,0... | collective-permute-start | bytes 98312 | tf_op jit(solution)/shard_map/ppermute | solution.py:410
  19.8 8.5 %collective-permute-start.7 = (bf16[16,8,128]{2,1,0:T(8,128)(2,1)S(1)}, bf16[16,8,128]{2,1,0:T(8,128)(2,1)S(1)}, u32[]{:S(2)}, u32[]{:S(2)}) collective-permute-start(bf16[16,8,128]{2,1,0:T(8,128)(2,1)S(1)} %fusion.14._), channel_id=1, source_target_pairs={{0,192},{4,196},{8,200},{12,204},{16,208},{20,212},{24,216},{28,22... | collective-permute-start | bytes 98312 | tf_op jit(solution)/shard_map/ppermute | solution.py:410
  28.5 10.8 %collective-permute-start.9 = (bf16[144,1024]{1,0:T(8,128)(2,1)S(1)}, bf16[144,1024]{1,0:T(8,128)(2,1)S(1)}, u32[]{:S(2)}, u32[]{:S(2)}) collective-permute-start(bf16[144,1024]{1,0:T(8,128)(2,1)S(1)} %get-tuple-element.47), channel_id=1, source_target_pairs={{0,1},{1,2},{2,3},{3,0},{4,5},{5,6},{6,7},{7,4},{8,9},{9,10},{10,1... | collective-permute-start | bytes 884744 | tf_op jit(solution)/shard_map/ppermute | solution.py:450
  30.1 10.1 %collective-permute-start.12 = (bf16[112,1024]{1,0:T(8,128)(2,1)S(1)}, bf16[112,1024]{1,0:T(8,128)(2,1)S(1)}, u32[]{:S(2)}, u32[]{:S(2)}) collective-permute-start(bf16[112,1024]{1,0:T(8,128)(2,1)S(1)} %get-tuple-element.50), channel_id=1, source_target_pairs={{0,3},{1,0},{2,1},{3,2},{4,7},{5,4},{6,5},{7,6},{8,11},{9,8},{10,9... | collective-permute-start | bytes 688136 | tf_op jit(solution)/shard_map/ppermute | solution.py:451
  32.6 12.5 %collective-permute-start.11 = (bf16[112,1024]{1,0:T(8,128)(2,1)S(1)}, bf16[112,1024]{1,0:T(8,128)(2,1)S(1)}, u32[]{:S(2)}, u32[]{:S(2)}) collective-permute-start(bf16[112,1024]{1,0:T(8,128)(2,1)S(1)} %get-tuple-element.43._), channel_id=1, source_target_pairs={{0,1},{1,2},{2,3},{3,0},{4,5},{5,6},{6,7},{7,4},{8,9},{9,10},{10,1... | collective-permute-start | bytes 688136 | tf_op jit(solution)/shard_map/ppermute | solution.py:453
  35.3 9.8 %collective-permute-start.8 = (bf16[144,1024]{1,0:T(8,128)(2,1)S(1)}, bf16[144,1024]{1,0:T(8,128)(2,1)S(1)}, u32[]{:S(2)}, u32[]{:S(2)}) collective-permute-start(bf16[144,1024]{1,0:T(8,128)(2,1)S(1)} %get-tuple-element.44._), channel_id=1, source_target_pairs={{0,3},{1,0},{2,1},{3,2},{4,7},{5,4},{6,5},{7,6},{8,11},{9,8},{10,9... | collective-permute-start | bytes 884744 | tf_op jit(solution)/shard_map/ppermute | solution.py:455
  39.3 8.4 %collective-permute-start.10 = (bf16[144,1024]{1,0:T(8,128)(2,1)S(1)}, bf16[144,1024]{1,0:T(8,128)(2,1)S(1)}, u32[]{:S(2)}, u32[]{:S(2)}) collective-permute-start(bf16[144,1024]{1,0:T(8,128)(2,1)S(1)} %add_convert_fusion), channel_id=1, source_target_pairs={{0,1},{1,2},{2,3},{3,0},{4,5},{5,6},{6,7},{7,4},{8,9},{9,10},{10,1... | collective-permute-start | bytes 884744 | tf_op jit(solution)/shard_map/ppermute | solution.py:457
  40.2 7.1 %collective-permute-start.13 = (bf16[112,1024]{1,0:T(8,128)(2,1)S(1)}, bf16[112,1024]{1,0:T(8,128)(2,1)S(1)}, u32[]{:S(2)}, u32[]{:S(2)}) collective-permute-start(bf16[112,1024]{1,0:T(8,128)(2,1)S(1)} %add_convert_fusion.1), channel_id=1, source_target_pairs={{0,3},{1,0},{2,1},{3,2},{4,7},{5,4},{6,5},{7,6},{8,11},{9,8},{10,9... | collective-permute-start | bytes 688136 | tf_op jit(solution)/shard_map/ppermute | solution.py:458

commit v4 on v3

--- a/solution.py
+++ b/solution.py
@@ -22,7 +22,7 @@
     (4, ((1, 8), (3, 24), (2, 16)), False),
     (2, ((1, 48),), False),
 )
-WORK = 1
+WORK = (1, 2)
 HBM = pl.BlockSpec(memory_space=pltpu.HBM)
 VMEM = pl.BlockSpec(memory_space=pltpu.VMEM)
 DMA = pltpu.SemaphoreType.DMA
@@ -159,9 +159,11 @@
     )(*(in_hbm(x) for x in (gate_key, value_in, decay, residue, skip)))
 
 
-def local_kernel(members, apart, keyed_ref, decay_ref, scale_ref, _, skip_ref, local_ref, ahead_ref):
+def local_kernel(part, members, apart, keyed_ref, decay_ref, scale_ref, held_ref, _, skip_ref,
+                 local_ref, ahead_ref, left_ref=None):
     groups = decay_ref.shape[1]
     span = groups * SUB
+    first = part * local_ref.shape[0]
     ahead = (members - 1 - lax.axis_index("ctx") // apart % members) * apart * (keyed_ref.shape[0] // groups)
     for r in range(MODES):
         ahead_ref[r] = jnp.exp(-decay_ref[r] * ahead.astype(jnp.float32))
@@ -171,24 +173,32 @@
 
     def block(i, held):
         for s in range(SUB):
-            at = pl.ds(i * span + s, groups, stride=SUB)
-            now = keyed_ref[at, :]
+            now = keyed_ref[pl.ds(first + i * span + s, groups, stride=SUB), :]
             held = [a * h + now for a, h in zip(step, held)]
-            local_ref[at, :] = total_of([c * h for c, h in zip(scale, held)] + [skip * now])
+            local_ref[pl.ds(i * span + s, groups, stride=SUB), :] = total_of(
+                [c * h for c, h in zip(scale, held)] + [skip * now]
+            )
         return held
 
-    lax.fori_loop(0, keyed_ref.shape[0] // span, block, [jnp.zeros((groups, LANES), jnp.float32)] * MODES)
-
-
-def local_part(members, apart, keyed, decay, scale, behind, skip):
-    return pl.pallas_call(
-        functools.partial(local_kernel, members, apart),
-        out_shape=(wide(*keyed.shape), wide(*decay.shape)),
-        in_specs=[VMEM] * 5,
-        out_specs=(VMEM, VMEM),
-        compiler_params=params(),
-        cost_estimate=cost(2**23, 2**22),
-    )(keyed, decay, scale, behind, skip)
+    if part:
+        held = [held_ref[r] for r in range(MODES)]
+    else:
+        held = [jnp.zeros((groups, LANES), jnp.float32)] * MODES
+    held = lax.fori_loop(0, local_ref.shape[0] // span, block, held)
+    if left_ref is not None:
+        for r in range(MODES):
+            left_ref[r] = held[r]
+
+
+def local_part(part, members, apart, keyed, decay, scale, held, behind, skip):
+    return pl.pallas_call(
+        functools.partial(local_kernel, part, members, apart),
+        out_shape=(wide(keyed.shape[0] // 2, LANES),) + (wide(*decay.shape),) * (2 - part),
+        in_specs=[VMEM] * 6,
+        out_specs=(VMEM,) * (3 - part),
+        compiler_params=params(),
+        cost_estimate=cost(2**22, 2**21),
+    )(keyed, decay, scale, held, behind, skip)
 
 
 def apply_gate(mixing, query_ref, gated_ref):
@@ -208,19 +218,25 @@
     lax.fori_loop(0, length // ROWS, block, 0)
 
 
-def add_tail(base_ref, decay_ref, start_ref, mix_ref):
+def add_tail(bases, decay_ref, start_ref, mix_ref):
     groups = decay_ref.shape[1]
     span = groups * SUB
     step = [jnp.exp(-decay_ref[r]) for r in range(MODES)]
 
-    def block(i, held):
-        for s in range(SUB):
-            at = pl.ds(i * span + s, groups, stride=SUB)
-            mix_ref[at, :] = base_ref[at, :] + total_of(held)
-            held = [a * h for a, h in zip(step, held)]
-        return held
-
-    lax.fori_loop(0, mix_ref.shape[0] // span, block, [start_ref[r] for r in range(MODES)])
+    held = [start_ref[r] for r in range(MODES)]
+    first = 0
+    for base_ref in bases:
+
+        def block(i, held, base_ref=base_ref, first=first):
+            for s in range(SUB):
+                mix_ref[pl.ds(first + i * span + s, groups, stride=SUB), :] = base_ref[
+                    pl.ds(i * span + s, groups, stride=SUB), :
+                ] + total_of(held)
+                held = [a * h for a, h in zip(step, held)]
+            return held
+
+        held = lax.fori_loop(0, base_ref.shape[0] // span, block, held)
+        first += base_ref.shape[0]
 
 
 def tile_of(mix_ref, groups):
@@ -234,14 +250,14 @@
     return lax.axis_index("ctx") >= lax.axis_size("ctx") // 2
 
 
-def begin_kernel(local_ref, decay_ref, start_ref, _, query_hbm, weight_hbm,
+def begin_kernel(early_ref, late_ref, decay_ref, start_ref, _, query_hbm, weight_hbm,
                  mix_ref, query_ref, far_ref, next_ref, gated_ref, far_top, far_low, sems):
     upper = in_upper_half()
     query_copy = pltpu.make_async_copy(query_hbm, query_ref, sems.at[CHUNKS])
     query_copy.start()
     far_copies = fetch_columns(weight_hbm, FAR, far_ref, sems)
     next_copies = fetch_columns(weight_hbm, NEXT, next_ref, sems, CHUNKS + 1)
-    add_tail(local_ref, decay_ref, start_ref, mix_ref)
+    add_tail((early_ref, late_ref), decay_ref, start_ref, mix_ref)
     query_copy.wait()
 
     @pl.when(jnp.logical_not(upper))
@@ -264,13 +280,13 @@
     top, low = cut_rows(length, width)
     return pl.pallas_call(
         begin_kernel,
-        out_shape=(wide(*local.shape), short(length, chans), columns, columns, short(length, chans), short(*top), short(*low)),
-        in_specs=[VMEM] * 4 + [HBM] * 2,
+        out_shape=(wide(2 * local[0].shape[0], LANES), short(length, chans), columns, columns, short(length, chans), short(*top), short(*low)),
+        in_specs=[VMEM] * 5 + [HBM] * 2,
         out_specs=(VMEM,) * 7,
         scratch_shapes=[DMA((2 * CHUNKS + 1,))],
         compiler_params=params(),
         cost_estimate=cost(2**23, 2**22),
-    )(local, decay, start, behind, in_hbm(gate_query), in_hbm(weight))
+    )(*local, decay, start, behind, in_hbm(gate_query), in_hbm(weight))
 
 
 def end_kernel(mix_ref, query_ref, far_ref, gated_in, top_in, low_in, decay_ref, start_ref,
@@ -279,7 +295,7 @@
 
     @pl.when(upper)
     def _():
-        add_tail(mix_ref, decay_ref, start_ref, sum_ref)
+        add_tail((mix_ref,), decay_ref, start_ref, sum_ref)
         apply_gate(tile_of(sum_ref, decay_ref.shape[1]), query_ref, gated_ref)
         project(gated_ref, far_ref, far_top, far_low)
 
@@ -398,7 +414,7 @@
     for stage, (members, moves, forward) in enumerate(STAGES):
         mine, inside = index // span % members, index % span
         sent = total.astype(jnp.bfloat16)
-        own = work(sent, members, span) if stage == WORK else power((members - 1 - mine) * span)
+        own = work(sent, members, span) if stage in WORK else power((members - 1 - mine) * span)
         if stage == len(STAGES) - 1:
             load(sent, before)
             before = jnp.zeros_like(state)
@@ -431,11 +447,13 @@
         gate_key, value_in, decay_rate.T, residues.T, skip_gain.reshape(groups, LANES)
     )
     scale = residue * jnp.sqrt(-jnp.expm1(-2.0 * decay))
-    local = None
+    local, held = [], state
 
     def work(sent, members, apart):
-        nonlocal local
-        local, ahead = local_part(members, apart, keyed, decay, scale, sent, skip)
+        nonlocal held
+        part, ahead, *left = local_part(len(local), members, apart, keyed, decay, scale, held, sent, skip)
+        local.append(part)
+        held = left[0] if left else held
         return ahead
 
     entry = scale * jnp.exp(-decay)

time: 48.8 us -> 48.8 us (level)
    pallas_call x2 -> x3, Pallas kernels: 5.08 us -> 5.12 us  [the longest x2 2.56 us: local_part(): pl.pallas_call(functools.partial(local_kernel, part, members, apart), out...]
  transfers between devices with their start and end apart: 14 -> 14, of which waited for: 7 -> 6; matrix products, arithmetic and copies ran while one was open for 1% -> 1% of each run, Pallas kernels for 22% -> 22%
where the time goes in v4:
time: 48.8 us; the launch traced here: 48.6 us
  starting transfers between devices  25.3 us (52%)
  Pallas kernels  14 us (29%)
  waiting for transfers between devices  8.54 us (18%)
  other arithmetic  0.59 us (1%)
    ppermute x8, starting transfers between devices, scan_over_ctx(): got.append((k, lax.ppermute(sent, 'ctx', pairs).astype(jnp.float32)))  15.2 us
    ppermute x8, waiting for transfers between devices, scan_over_ctx(): got.append((k, lax.ppermute(sent, 'ctx', pairs).astype(jnp.float32)))  5 us
    pallas_call x2, Pallas kernels, fetched_part(): pl.pallas_call(functools.partial(fetch_and_project, turn), out_shape=out_...  4.68 us
    ppermute x1, starting transfers between devices, on_device(): near_a = lax.ppermute(last_top, 'tp', back)  3.01 us
    pallas_call x2, Pallas kernels, local_part(): pl.pallas_call(functools.partial(local_kernel, part, members, apart), out...  2.56 us
    pallas_call x1, Pallas kernels, begin_part(): pl.pallas_call(begin_kernel, out_shape=(wide(2 * local[0].shape[0], LANES...  2.55 us
    ppermute x1, starting transfers between devices, on_device(): lax.ppermute((last_low + far_b.astype(jnp.float32)).astype(jnp.bfloat16),...  2.53 us
    pallas_call x1, Pallas kernels, block_state(): pl.pallas_call(state_kernel, out_shape=(modes, wide(length * groups, LANE...  2.51 us
  transfers between devices with their start and end apart: 14, of which 6 were waited for; matrix products, arithmetic and copies ran while one was open for 1% of the time, Pallas kernels for 22%

profile of v4, /device:TPU:32, one launch (start us, length us, event | category | flops | bytes accessed | tf_op | source)
XLA Modules:
  0.0 48.6 jit_solution(10032717278854687891)
XLA Ops:
  0.0 2.5 %shard_map.73 = (f32[16,8,128]{2,1,0:T(8,128)S(1)}, f32[2048,128]{1,0:T(8,128)S(1)}, f32[16,8,128]{2,1,0:T(8,128)S(1)}, f32[16,8,128]{2,1,0:T(8,128)S(1)}, f32[8,128]{1,0:T(8,128)S(1)}) custom-call(bf16[256,1024]{1,0:T(8,128)(2,1)} %key_hbm.1, bf16[256,1024]{1,0:T(8,128)(2,1)} %value_hbm.1, f32[16,1024]{1,0:T(8,128)} %bitcast.3, f32[16,1024]{1,0:T(8,128)} %bitcast.4, ...), custom_call_target="tpu_custom_call" | custom-call | flops 8388608 | bytes 8388608 | tf_op jit(solution)/shard_map/pallas_call | solution.py:145
  2.7 1.2 %collective-permute-done = bf16[16,8,128]{2,1,0:T(8,128)(2,1)S(1)} collective-permute-done((bf16[16,8,128]{2,1,0:T(8,128)(2,1)S(1)}, bf16[16,8,128]{2,1,0:T(8,128)(2,1)S(1)}, u32[]{:S(2)}, u32[]{:S(2)}) %collective-permute-start) | collective-permute-done | bytes 32800 | tf_op jit(solution)/shard_map/ppermute | solution.py:426
  3.9 3.3 %collective-permute-start.3 = (bf16[16,8,128]{2,1,0:T(8,128)(2,1)S(1)}, bf16[16,8,128]{2,1,0:T(8,128)(2,1)S(1)}, u32[]{:S(2)}, u32[]{:S(2)}) collective-permute-start(bf16[16,8,128]{2,1,0:T(8,128)(2,1)S(1)} %get-tuple-element.59._), channel_id=1, source_target_pairs={{0,16},{4,20},{8,24},{12,28},{16,0},{20,4},{24,8},{28,12},{32,48},... | collective-permute-start | bytes 98312 | tf_op jit(solution)/shard_map/ppermute | solution.py:426
  7.2 1.1 %collective-permute-start.2 = (bf16[16,8,128]{2,1,0:T(8,128)(2,1)S(1)}, bf16[16,8,128]{2,1,0:T(8,128)(2,1)S(1)}, u32[]{:S(2)}, u32[]{:S(2)}) collective-permute-start(bf16[16,8,128]{2,1,0:T(8,128)(2,1)S(1)} %get-tuple-element.59._), channel_id=1, source_target_pairs={{0,24},{4,28},{8,16},{12,20},{16,8},{20,12},{24,0},{28,4},{32,56},... | collective-permute-start | bytes 98312 | tf_op jit(solution)/shard_map/ppermute | solution.py:426
  8.2 1.3 %shard_map.74 = (f32[1024,128]{1,0:T(8,128)S(1)}, f32[16,8,128]{2,1,0:T(8,128)S(1)}, f32[16,8,128]{2,1,0:T(8,128)S(1)}) custom-call(f32[2048,128]{1,0:T(8,128)S(1)} %get-tuple-element.31.keyed_ref, f32[16,8,128]{2,1,0:T(8,128)S(1)} %get-tuple-element.32.decay_ref, f32[16,8,128]{2,1,0:T(8,128)S(1)} %get-tuple-element.60.scale_ref, ...), custom_call_target="tpu_custom_call" | custom-call | flops 4194304 | bytes 2097152 | tf_op jit(solution)/shard_map/pallas_call | solution.py:194
  9.6 2.8 %collective-permute-done.2 = bf16[16,8,128]{2,1,0:T(8,128)(2,1)S(1)} collective-permute-done((bf16[16,8,128]{2,1,0:T(8,128)(2,1)S(1)}, bf16[16,8,128]{2,1,0:T(8,128)(2,1)S(1)}, u32[]{:S(2)}, u32[]{:S(2)}) %collective-permute-start.2) | collective-permute-done | bytes 32800 | tf_op jit(solution)/shard_map/ppermute | solution.py:426
  12.4 3.4 %collective-permute-start.6 = (bf16[16,8,128]{2,1,0:T(8,128)(2,1)S(1)}, bf16[16,8,128]{2,1,0:T(8,128)(2,1)S(1)}, u32[]{:S(2)}, u32[]{:S(2)}) collective-permute-start(bf16[16,8,128]{2,1,0:T(8,128)(2,1)S(1)} %get-tuple-element.57._), channel_id=1, source_target_pairs={{0,64},{4,68},{8,72},{12,76},{16,80},{20,84},{24,88},{28,92},{32,9... | collective-permute-start | bytes 98312 | tf_op jit(solution)/shard_map/ppermute | solution.py:426
  15.8 1.6 %collective-permute-start.4 = (bf16[16,8,128]{2,1,0:T(8,128)(2,1)S(1)}, bf16[16,8,128]{2,1,0:T(8,128)(2,1)S(1)}, u32[]{:S(2)}, u32[]{:S(2)}) collective-permute-start(bf16[16,8,128]{2,1,0:T(8,128)(2,1)S(1)} %get-tuple-element.57._), channel_id=1, source_target_pairs={{0,32},{4,36},{8,40},{12,44},{16,48},{20,52},{24,56},{28,60},{32,0... | collective-permute-start | bytes 98312 | tf_op jit(solution)/shard_map/ppermute | solution.py:426
  17.3 1.3 %shard_map.75 = (f32[1024,128]{1,0:T(8,128)S(1)}, f32[16,8,128]{2,1,0:T(8,128)S(1)}) custom-call(f32[2048,128]{1,0:T(8,128)S(1)} %get-tuple-element.31.keyed_ref, f32[16,8,128]{2,1,0:T(8,128)S(1)} %get-tuple-element.32.decay_ref, f32[16,8,128]{2,1,0:T(8,128)S(1)} %get-tuple-element.60.scale_ref, f32[16,8,128]{2,1,0:T(8,128)S(1)} %get-tuple-element.37.held_ref, ...), custom_call_target="tpu_custom_call" | custom-call | flops 4194304 | bytes 2097152 | tf_op jit(solution)/shard_map/pallas_call | solution.py:194
  18.6 1.1 %collective-permute-done.5 = bf16[16,8,128]{2,1,0:T(8,128)(2,1)S(1)} collective-permute-done((bf16[16,8,128]{2,1,0:T(8,128)(2,1)S(1)}, bf16[16,8,128]{2,1,0:T(8,128)(2,1)S(1)}, u32[]{:S(2)}, u32[]{:S(2)}) %collective-permute-start.5) | collective-permute-done | bytes 32800 | tf_op jit(solution)/shard_map/ppermute | solution.py:426
  19.8 5.8 %collective-permute-start.7 = (bf16[16,8,128]{2,1,0:T(8,128)(2,1)S(1)}, bf16[16,8,128]{2,1,0:T(8,128)(2,1)S(1)}, u32[]{:S(2)}, u32[]{:S(2)}) collective-permute-start(bf16[16,8,128]{2,1,0:T(8,128)(2,1)S(1)} %fusion.14._), channel_id=1, source_target_pairs={{0,192},{4,196},{8,200},{12,204},{16,208},{20,212},{24,216},{28,22... | collective-permute-start | bytes 98312 | tf_op jit(solution)/shard_map/ppermute | solution.py:426
  25.7 2.6 %shard_map.76 = (f32[2048,128]{1,0:T(8,128)S(1)}, bf16[256,1024]{1,0:T(8,128)(2,1)S(1)}, bf16[1024,1024]{1,0:T(8,128)(2,1)S(1)}, bf16[1024,1024]{1,0:T(8,128)(2,...) custom-call(f32[1024,128]{1,0:T(8,128)S(1)} %get-tuple-element.36.early_ref, ...), custom_call_target="tpu_custom_call" | custom-call | flops 8388608 | bytes 4194304 | tf_op jit(solution)/shard_map/pallas_call | solution.py:281
  28.5 1.6 %collective-permute-start.9 = (bf16[144,1024]{1,0:T(8,128)(2,1)S(1)}, bf16[144,1024]{1,0:T(8,128)(2,1)S(1)}, u32[]{:S(2)}, u32[]{:S(2)}) collective-permute-start(bf16[144,1024]{1,0:T(8,128)(2,1)S(1)} %get-tuple-element.53), channel_id=1, source_target_pairs={{0,1},{1,2},{2,3},{3,0},{4,5},{5,6},{6,7},{7,4},{8,9},{9,10},{10,1... | collective-permute-start | bytes 884744 | tf_op jit(solution)/shard_map/ppermute | solution.py:468
  30.1 1.7 %collective-permute-start.12 = (bf16[112,1024]{1,0:T(8,128)(2,1)S(1)}, bf16[112,1024]{1,0:T(8,128)(2,1)S(1)}, u32[]{:S(2)}, u32[]{:S(2)}) collective-permute-start(bf16[112,1024]{1,0:T(8,128)(2,1)S(1)} %get-tuple-element.56), channel_id=1, source_target_pairs={{0,3},{1,0},{2,1},{3,2},{4,7},{5,4},{6,5},{7,6},{8,11},{9,8},{10,9... | collective-permute-start | bytes 688136 | tf_op jit(solution)/shard_map/ppermute | solution.py:469
  31.8 0.8 %shard_map.78 = (f32[144,1024]{1,0:T(8,128)S(1)}, bf16[112,1024]{1,0:T(8,128)(2,1)S(1)}) custom-call(bf16[256,1024]{1,0:T(8,128)(2,1)S(1)} %get-tuple-element.47.gated_ref, bf16[1024,1024]{1,0:T(8,128)(2,1)S(1)} %get-tuple-element.48.columns_ref), custom_call_target="tpu_custom_call" | custom-call | flops 536870912 | bytes 1048576 | tf_op jit(solution)/shard_map/pallas_call | solution.py:338
  32.9 2.3 %shard_map.79 = (bf16[144,1024]{1,0:T(8,128)(2,1)S(1)}, f32[112,1024]{1,0:T(8,128)S(1)}) custom-call(bf16[256,1024]{1,0:T(8,128)(2,1)S(1)} %get-tuple-element.47.gated_ref, bf16[1024,4096]{1,0:T(8,128)(2,1)} %weight_hbm.5, bf16[112,1024]{1,0:T(8,128)(2,1)S(1)} %get-tuple-element.49._), custom_call_target="tpu_custom_call" | custom-call | flops 536870912 | bytes 2097152 | tf_op jit(solution)/shard_map/pallas_call | solution.py:354
  35.3 3.0 %collective-permute-start.8 = (bf16[144,1024]{1,0:T(8,128)(2,1)S(1)}, bf16[144,1024]{1,0:T(8,128)(2,1)S(1)}, u32[]{:S(2)}, u32[]{:S(2)}) collective-permute-start(bf16[144,1024]{1,0:T(8,128)(2,1)S(1)} %get-tuple-element.50._), channel_id=1, source_target_pairs={{0,3},{1,0},{2,1},{3,2},{4,7},{5,4},{6,5},{7,6},{8,11},{9,8},{10,9... | collective-permute-start | bytes 884744 | tf_op jit(solution)/shard_map/ppermute | solution.py:473
  38.3 0.9 %collective-permute-done.9 = bf16[144,1024]{1,0:T(8,128)(2,1)S(1)} collective-permute-done((bf16[144,1024]{1,0:T(8,128)(2,1)S(1)}, bf16[144,1024]{1,0:T(8,128)(2,1)S(1)}, u32[]{:S(2)}, u32[]{:S(2)}) %collective-permute-start.9) | collective-permute-done | bytes 294944 | tf_op jit(solution)/shard_map/ppermute | solution.py:468
  39.3 0.9 %collective-permute-start.10 = (bf16[144,1024]{1,0:T(8,128)(2,1)S(1)}, bf16[144,1024]{1,0:T(8,128)(2,1)S(1)}, u32[]{:S(2)}, u32[]{:S(2)}) collective-permute-start(bf16[144,1024]{1,0:T(8,128)(2,1)S(1)} %add_convert_fusion), channel_id=1, source_target_pairs={{0,1},{1,2},{2,3},{3,0},{4,5},{5,6},{6,7},{7,4},{8,9},{9,10},{10,1... | collective-permute-start | bytes 884744 | tf_op jit(solution)/shard_map/ppermute | solution.py:475
  40.2 2.5 %collective-permute-start.13 = (bf16[112,1024]{1,0:T(8,128)(2,1)S(1)}, bf16[112,1024]{1,0:T(8,128)(2,1)S(1)}, u32[]{:S(2)}, u32[]{:S(2)}) collective-permute-start(bf16[112,1024]{1,0:T(8,128)(2,1)S(1)} %add_convert_fusion.1), channel_id=1, source_target_pairs={{0,3},{1,0},{2,1},{3,2},{4,7},{5,4},{6,5},{7,6},{8,11},{9,8},{10,9... | collective-permute-start | bytes 688136 | tf_op jit(solution)/shard_map/ppermute | solution.py:476
  42.7 2.3 %shard_map.80 = (f32[144,1024]{1,0:T(8,128)S(1)}, f32[112,1024]{1,0:T(8,128)S(1)}) custom-call(bf16[256,1024]{1,0:T(8,128)(2,1)S(1)} %get-tuple-element.47.gated_ref, bf16[1024,4096]{1,0:T(8,128)(2,1)} %weight_hbm.5, bf16[144,1024]{1,0:T(8,128)(2,1)S(1)} %get-tuple-element.50._), custom_call_target="tpu_custom_call" | custom-call | flops 536870912 | bytes 2097152 | tf_op jit(solution)/shard_map/pallas_call | solution.py:354
  45.1 2.2 %collective-permute-done.13.both_low = bf16[112,1024]{1,0:T(8,128)(2,1)S(1)} collective-permute-done((bf16[112,1024]{1,0:T(8,128)(2,1)S(1)}, bf16[112,1024]{1,0:T(8,128)(2,1)S(1)}, u32[]{:S(2)}, u32[]{:S(2)}) %collective-permute-start.13) | collective-permute-done | bytes 229408 | tf_op jit(solution)/shard_map/ppermute | solution.py:476
  47.3 0.4 collective-permute-done.10.both_top
  47.7 0.9 %shard_map.81 = bf16[256,1024]{1,0:T(8,128)(2,1)} custom-call(f32[144,1024]{1,0:T(8,128)S(1)} %get-tuple-element.51.mine_top, bf16[144,1024]{1,0:T(8,128)(2,1)S(1)} %collective-permute-done.8.near_top, bf16[144,1024]{1,0:T(8,128)(2,1)S(1)} %collective-permute-done.10.both_top, f32[112,1024]{1,0:T(8,128)S(1)} %get-tuple-element.54.mine_low, ...), custom_call_target="tpu_custom_call" | custom-call | flops 524288 | bytes 2097152 | tf_op jit(solution)/shard_map/pallas_call | solution.py:393
  (21 shorter events, 1.2 us)
Async XLA Ops:
  2.5 1.3 %collective-permute-start = (bf16[16,8,128]{2,1,0:T(8,128)(2,1)S(1)}, bf16[16,8,128]{2,1,0:T(8,128)(2,1)S(1)}, u32[]{:S(2)}, u32[]{:S(2)}) collective-permute-start(bf16[16,8,128]{2,1,0:T(8,128)(2,1)S(1)} %convert_element_type.97), channel_id=1, source_target_pairs={{0,4},{4,0},{8,12},{12,8},{16,20},{20,16},{24,28},{28,24},{32,36},... | collective-permute-start | bytes 98312 | tf_op jit(solution)/shard_map/ppermute | solution.py:426
  3.9 5.6 %collective-permute-start.3 = (bf16[16,8,128]{2,1,0:T(8,128)(2,1)S(1)}, bf16[16,8,128]{2,1,0:T(8,128)(2,1)S(1)}, u32[]{:S(2)}, u32[]{:S(2)}) collective-permute-start(bf16[16,8,128]{2,1,0:T(8,128)(2,1)S(1)} %get-tuple-element.59._), channel_id=1, source_target_pairs={{0,16},{4,20},{8,24},{12,28},{16,0},{20,4},{24,8},{28,12},{32,48},... | collective-permute-start | bytes 98312 | tf_op jit(solution)/shard_map/ppermute | solution.py:426
  7.2 5.1 %collective-permute-start.2 = (bf16[16,8,128]{2,1,0:T(8,128)(2,1)S(1)}, bf16[16,8,128]{2,1,0:T(8,128)(2,1)S(1)}, u32[]{:S(2)}, u32[]{:S(2)}) collective-permute-start(bf16[16,8,128]{2,1,0:T(8,128)(2,1)S(1)} %get-tuple-element.59._), channel_id=1, source_target_pairs={{0,24},{4,28},{8,16},{12,20},{16,8},{20,12},{24,0},{28,4},{32,56},... | collective-permute-start | bytes 98312 | tf_op jit(solution)/shard_map/ppermute | solution.py:426
  8.2 4.1 %collective-permute-start.1 = (bf16[16,8,128]{2,1,0:T(8,128)(2,1)S(1)}, bf16[16,8,128]{2,1,0:T(8,128)(2,1)S(1)}, u32[]{:S(2)}, u32[]{:S(2)}) collective-permute-start(bf16[16,8,128]{2,1,0:T(8,128)(2,1)S(1)} %get-tuple-element.59._), channel_id=1, source_target_pairs={{0,8},{4,12},{8,0},{12,4},{16,24},{20,28},{24,16},{28,20},{32,40},... | collective-permute-start | bytes 98312 | tf_op jit(solution)/shard_map/ppermute | solution.py:426
  12.4 6.2 %collective-permute-start.6 = (bf16[16,8,128]{2,1,0:T(8,128)(2,1)S(1)}, bf16[16,8,128]{2,1,0:T(8,128)(2,1)S(1)}, u32[]{:S(2)}, u32[]{:S(2)}) collective-permute-start(bf16[16,8,128]{2,1,0:T(8,128)(2,1)S(1)} %get-tuple-element.57._), channel_id=1, source_target_pairs={{0,64},{4,68},{8,72},{12,76},{16,80},{20,84},{24,88},{28,92},{32,9... | collective-permute-start | bytes 98312 | tf_op jit(solution)/shard_map/ppermute | solution.py:426
  15.8 3.9 %collective-permute-start.5 = (bf16[16,8,128]{2,1,0:T(8,128)(2,1)S(1)}, bf16[16,8,128]{2,1,0:T(8,128)(2,1)S(1)}, u32[]{:S(2)}, u32[]{:S(2)}) collective-permute-start(bf16[16,8,128]{2,1,0:T(8,128)(2,1)S(1)} %get-tuple-element.57._), channel_id=1, source_target_pairs={{0,96},{4,100},{8,104},{12,108},{16,112},{20,116},{24,120},{28,124... | collective-permute-start | bytes 98312 | tf_op jit(solution)/shard_map/ppermute | solution.py:426
  15.8 3.9 %collective-permute-start.4 = (bf16[16,8,128]{2,1,0:T(8,128)(2,1)S(1)}, bf16[16,8,128]{2,1,0:T(8,128)(2,1)S(1)}, u32[]{:S(2)}, u32[]{:S(2)}) collective-permute-start(bf16[16,8,128]{2,1,0:T(8,128)(2,1)S(1)} %get-tuple-element.57._), channel_id=1, source_target_pairs={{0,32},{4,36},{8,40},{12,44},{16,48},{20,52},{24,56},{28,60},{32,0... | collective-permute-start | bytes 98312 | tf_op jit(solution)/shard_map/ppermute | solution.py:426
  19.8 8.5 %collective-permute-start.7 = (bf16[16,8,128]{2,1,0:T(8,128)(2,1)S(1)}, bf16[16,8,128]{2,1,0:T(8,128)(2,1)S(1)}, u32[]{:S(2)}, u32[]{:S(2)}) collective-permute-start(bf16[16,8,128]{2,1,0:T(8,128)(2,1)S(1)} %fusion.14._), channel_id=1, source_target_pairs={{0,192},{4,196},{8,200},{12,204},{16,208},{20,212},{24,216},{28,22... | collective-permute-start | bytes 98312 | tf_op jit(solution)/shard_map/ppermute | solution.py:426
  28.5 10.7 %collective-permute-start.9 = (bf16[144,1024]{1,0:T(8,128)(2,1)S(1)}, bf16[144,1024]{1,0:T(8,128)(2,1)S(1)}, u32[]{:S(2)}, u32[]{:S(2)}) collective-permute-start(bf16[144,1024]{1,0:T(8,128)(2,1)S(1)} %get-tuple-element.53), channel_id=1, source_target_pairs={{0,1},{1,2},{2,3},{3,0},{4,5},{5,6},{6,7},{7,4},{8,9},{9,10},{10,1... | collective-permute-start | bytes 884744 | tf_op jit(solution)/shard_map/ppermute | solution.py:468
  30.1 10.1 %collective-permute-start.12 = (bf16[112,1024]{1,0:T(8,128)(2,1)S(1)}, bf16[112,1024]{1,0:T(8,128)(2,1)S(1)}, u32[]{:S(2)}, u32[]{:S(2)}) collective-permute-start(bf16[112,1024]{1,0:T(8,128)(2,1)S(1)} %get-tuple-element.56), channel_id=1, source_target_pairs={{0,3},{1,0},{2,1},{3,2},{4,7},{5,4},{6,5},{7,6},{8,11},{9,8},{10,9... | collective-permute-start | bytes 688136 | tf_op jit(solution)/shard_map/ppermute | solution.py:469
  32.6 12.5 %collective-permute-start.11 = (bf16[112,1024]{1,0:T(8,128)(2,1)S(1)}, bf16[112,1024]{1,0:T(8,128)(2,1)S(1)}, u32[]{:S(2)}, u32[]{:S(2)}) collective-permute-start(bf16[112,1024]{1,0:T(8,128)(2,1)S(1)} %get-tuple-element.49._), channel_id=1, source_target_pairs={{0,1},{1,2},{2,3},{3,0},{4,5},{5,6},{6,7},{7,4},{8,9},{9,10},{10,1... | collective-permute-start | bytes 688136 | tf_op jit(solution)/shard_map/ppermute | solution.py:471
  35.3 9.8 %collective-permute-start.8 = (bf16[144,1024]{1,0:T(8,128)(2,1)S(1)}, bf16[144,1024]{1,0:T(8,128)(2,1)S(1)}, u32[]{:S(2)}, u32[]{:S(2)}) collective-permute-start(bf16[144,1024]{1,0:T(8,128)(2,1)S(1)} %get-tuple-element.50._), channel_id=1, source_target_pairs={{0,3},{1,0},{2,1},{3,2},{4,7},{5,4},{6,5},{7,6},{8,11},{9,8},{10,9... | collective-permute-start | bytes 884744 | tf_op jit(solution)/shard_map/ppermute | solution.py:473
  39.3 8.4 %collective-permute-start.10 = (bf16[144,1024]{1,0:T(8,128)(2,1)S(1)}, bf16[144,1024]{1,0:T(8,128)(2,1)S(1)}, u32[]{:S(2)}, u32[]{:S(2)}) collective-permute-start(bf16[144,1024]{1,0:T(8,128)(2,1)S(1)} %add_convert_fusion), channel_id=1, source_target_pairs={{0,1},{1,2},{2,3},{3,0},{4,5},{5,6},{6,7},{7,4},{8,9},{9,10},{10,1... | collective-permute-start | bytes 884744 | tf_op jit(solution)/shard_map/ppermute | solution.py:475
  40.2 7.1 %collective-permute-start.13 = (bf16[112,1024]{1,0:T(8,128)(2,1)S(1)}, bf16[112,1024]{1,0:T(8,128)(2,1)S(1)}, u32[]{:S(2)}, u32[]{:S(2)}) collective-permute-start(bf16[112,1024]{1,0:T(8,128)(2,1)S(1)} %add_convert_fusion.1), channel_id=1, source_target_pairs={{0,3},{1,0},{2,1},{3,2},{4,7},{5,4},{6,5},{7,6},{8,11},{9,8},{10,9... | collective-permute-start | bytes 688136 | tf_op jit(solution)/shard_map/ppermute | solution.py:476

commit v5 on v4

--- a/solution.py
+++ b/solution.py
@@ -113,7 +113,7 @@
 
     def block(i, held):
         rows = pl.ds(pl.multiple_of(i * ROWS, ROWS), ROWS)
-        keyed = key_buf[rows, :].astype(jnp.float32) * value_buf[rows, :].astype(jnp.float32)
+        keyed = (key_buf[rows, :] * value_buf[rows, :]).astype(jnp.float32)
         for half in range(ROWS // SUB):
             base = (i * (ROWS // SUB) + half) * span
             for g in range(groups):
@@ -289,15 +289,55 @@
     )(*local, decay, start, behind, in_hbm(gate_query), in_hbm(weight))
 
 
+def carry_gate_project(bases, decay_ref, start_ref, mix_ref, query_ref, far_ref, gated_ref, far_top, far_low):
+    groups = decay_ref.shape[1]
+    span = groups * SUB
+    cut = far_top.shape[0]
+    step = [jnp.exp(-decay_ref[r]) for r in range(MODES)]
+    tile = tile_of(mix_ref, groups)
+
+    def advance(base_ref, first, i, held):
+        for s in range(SUB):
+            mix_ref[pl.ds(first + i * span + s, groups, stride=SUB), :] = base_ref[
+                pl.ds(i * span + s, groups, stride=SUB), :
+            ] + total_of(held)
+            held = [a * h for a, h in zip(step, held)]
+        return held
+
+    def gate(i):
+        rows = pl.ds(i * ROWS, ROWS)
+        for g in range(groups):
+            cols = slice(g * LANES, (g + 1) * LANES)
+            tiles = [tile(i * (ROWS // SUB) + half, g) for half in range(ROWS // SUB)]
+            gated_ref[rows, cols] = (
+                query_ref[rows, cols].astype(jnp.float32) * jnp.concatenate(tiles, axis=0)
+            ).astype(jnp.bfloat16)
+
+    held = [start_ref[r] for r in range(MODES)]
+    first, done, rest = 0, 0, []
+    for base_ref in bases:
+        blocks = base_ref.shape[0] // span
+        top = min(blocks, cut // SUB - done)
+        held = lax.fori_loop(0, top, functools.partial(advance, base_ref, first), held)
+        rest += [(base_ref, first, i) for i in range(top, blocks)]
+        first += base_ref.shape[0]
+        done += top
+    lax.fori_loop(0, cut // ROWS, lambda i, _: (gate(i), 0)[1], 0)
+    far_top[...] = jnp.dot(gated_ref[:cut, :], far_ref[...], preferred_element_type=jnp.float32).astype(jnp.bfloat16)
+    for base_ref, first, i in rest:
+        held = advance(base_ref, first, i, held)
+    for i in range(cut // ROWS, gated_ref.shape[0] // ROWS):
+        gate(i)
+    far_low[...] = jnp.dot(gated_ref[cut:, :], far_ref[...], preferred_element_type=jnp.float32).astype(jnp.bfloat16)
+
+
 def end_kernel(mix_ref, query_ref, far_ref, gated_in, top_in, low_in, decay_ref, start_ref,
                gated_ref, far_top, far_low, sum_ref):
     upper = in_upper_half()
 
     @pl.when(upper)
     def _():
-        add_tail((mix_ref,), decay_ref, start_ref, sum_ref)
-        apply_gate(tile_of(sum_ref, decay_ref.shape[1]), query_ref, gated_ref)
-        project(gated_ref, far_ref, far_top, far_low)
+        carry_gate_project((mix_ref,), decay_ref, start_ref, sum_ref, query_ref, far_ref, gated_ref, far_top, far_low)
 
     @pl.when(jnp.logical_not(upper))
     def _():
@@ -375,16 +415,19 @@
 def finish_kernel(mine_top, near_top, both_top, mine_low, near_low, both_low, out_hbm, out_buf, sems):
     row = 0
     copies = []
-    for n, (mine, near, both) in enumerate(
-        ((mine_top, near_top, both_top), (mine_low, near_low, both_low))
-    ):
-        rows = pl.ds(row, mine.shape[0])
-        out_buf[rows, :] = (
-            mine[...] + near[...].astype(jnp.float32) + both[...].astype(jnp.float32)
-        ).astype(jnp.bfloat16)
-        copies.append(pltpu.make_async_copy(out_buf.at[rows, :], out_hbm.at[rows, :], sems.at[n]))
-        copies[-1].start()
-        row += mine.shape[0]
+    for mine, near, both in ((mine_top, near_top, both_top), (mine_low, near_low, both_low)):
+        length = mine.shape[0]
+        middle = length // (2 * ROWS) * ROWS
+        for part in (slice(0, middle), slice(middle, length)):
+            rows = pl.ds(row, part.stop - part.start)
+            out_buf[rows, :] = (
+                mine[part, :] + near[part, :].astype(jnp.float32) + both[part, :].astype(jnp.float32)
+            ).astype(jnp.bfloat16)
+            copies.append(
+                pltpu.make_async_copy(out_buf.at[rows, :], out_hbm.at[rows, :], sems.at[len(copies)])
+            )
+            copies[-1].start()
+            row += part.stop - part.start
     wait_all(copies)
 
 
@@ -395,7 +438,7 @@
         out_shape=short(length, width),
         in_specs=[VMEM] * 6,
         out_specs=HBM,
-        scratch_shapes=[pltpu.VMEM((length, width), jnp.bfloat16), DMA((2,))],
+        scratch_shapes=[pltpu.VMEM((length, width), jnp.bfloat16), DMA((4,))],
         compiler_params=params(),
         cost_estimate=cost(2**19, 2**21),
     )(*parts)

time: 48.8 us -> 48.9 us (level)
  no operation moved by 1% of the time
where the time goes in v5:
time: 48.9 us; the launch traced here: 48.7 us
  starting transfers between devices  25.4 us (52%)
  Pallas kernels  14 us (29%)
  waiting for transfers between devices  8.37 us (17%)
  other arithmetic  0.59 us (1%)
    ppermute x8, starting transfers between devices, scan_over_ctx(): got.append((k, lax.ppermute(sent, 'ctx', pairs).astype(jnp.float32)))  15.2 us
    ppermute x8, waiting for transfers between devices, scan_over_ctx(): got.append((k, lax.ppermute(sent, 'ctx', pairs).astype(jnp.float32)))  5 us
    pallas_call x2, Pallas kernels, fetched_part(): pl.pallas_call(functools.partial(fetch_and_project, turn), out_shape=out_...  4.66 us
    ppermute x1, starting transfers between devices, on_device(): near_a = lax.ppermute(last_top, 'tp', back)  3.2 us
    pallas_call x2, Pallas kernels, local_part(): pl.pallas_call(functools.partial(local_kernel, part, members, apart), out...  2.56 us
    pallas_call x1, Pallas kernels, begin_part(): pl.pallas_call(begin_kernel, out_shape=(wide(2 * local[0].shape[0], LANES...  2.55 us
    ppermute x1, starting transfers between devices, on_device(): lax.ppermute((last_low + far_b.astype(jnp.float32)).astype(jnp.bfloat16),...  2.5 us
    pallas_call x1, Pallas kernels, block_state(): pl.pallas_call(state_kernel, out_shape=(modes, wide(length * groups, LANE...  2.45 us
  transfers between devices with their start and end apart: 14, of which 6 were waited for; matrix products, arithmetic and copies ran while one was open for 1% of the time, Pallas kernels for 22%

profile of v5, /device:TPU:32, one launch (start us, length us, event | category | flops | bytes accessed | tf_op | source)
XLA Modules:
  0.0 48.7 jit_solution(11973490803418167995)
XLA Ops:
  0.0 2.5 %shard_map.73 = (f32[16,8,128]{2,1,0:T(8,128)S(1)}, f32[2048,128]{1,0:T(8,128)S(1)}, f32[16,8,128]{2,1,0:T(8,128)S(1)}, f32[16,8,128]{2,1,0:T(8,128)S(1)}, f32[8,128]{1,0:T(8,128)S(1)}) custom-call(bf16[256,1024]{1,0:T(8,128)(2,1)} %key_hbm.1, bf16[256,1024]{1,0:T(8,128)(2,1)} %value_hbm.1, f32[16,1024]{1,0:T(8,128)} %bitcast.3, f32[16,1024]{1,0:T(8,128)} %bitcast.4, ...), custom_call_target="tpu_custom_call" | custom-call | flops 8388608 | bytes 8388608 | tf_op jit(solution)/shard_map/pallas_call | solution.py:145
  2.6 1.2 %collective-permute-done = bf16[16,8,128]{2,1,0:T(8,128)(2,1)S(1)} collective-permute-done((bf16[16,8,128]{2,1,0:T(8,128)(2,1)S(1)}, bf16[16,8,128]{2,1,0:T(8,128)(2,1)S(1)}, u32[]{:S(2)}, u32[]{:S(2)}) %collective-permute-start) | collective-permute-done | bytes 32800 | tf_op jit(solution)/shard_map/ppermute | solution.py:469
  3.9 3.3 %collective-permute-start.3 = (bf16[16,8,128]{2,1,0:T(8,128)(2,1)S(1)}, bf16[16,8,128]{2,1,0:T(8,128)(2,1)S(1)}, u32[]{:S(2)}, u32[]{:S(2)}) collective-permute-start(bf16[16,8,128]{2,1,0:T(8,128)(2,1)S(1)} %get-tuple-element.59._), channel_id=1, source_target_pairs={{0,16},{4,20},{8,24},{12,28},{16,0},{20,4},{24,8},{28,12},{32,48},... | collective-permute-start | bytes 98312 | tf_op jit(solution)/shard_map/ppermute | solution.py:469
  7.1 1.1 %collective-permute-start.2 = (bf16[16,8,128]{2,1,0:T(8,128)(2,1)S(1)}, bf16[16,8,128]{2,1,0:T(8,128)(2,1)S(1)}, u32[]{:S(2)}, u32[]{:S(2)}) collective-permute-start(bf16[16,8,128]{2,1,0:T(8,128)(2,1)S(1)} %get-tuple-element.59._), channel_id=1, source_target_pairs={{0,24},{4,28},{8,16},{12,20},{16,8},{20,12},{24,0},{28,4},{32,56},... | collective-permute-start | bytes 98312 | tf_op jit(solution)/shard_map/ppermute | solution.py:469
  8.2 1.3 %shard_map.74 = (f32[1024,128]{1,0:T(8,128)S(1)}, f32[16,8,128]{2,1,0:T(8,128)S(1)}, f32[16,8,128]{2,1,0:T(8,128)S(1)}) custom-call(f32[2048,128]{1,0:T(8,128)S(1)} %get-tuple-element.31.keyed_ref, f32[16,8,128]{2,1,0:T(8,128)S(1)} %get-tuple-element.32.decay_ref, f32[16,8,128]{2,1,0:T(8,128)S(1)} %get-tuple-element.60.scale_ref, ...), custom_call_target="tpu_custom_call" | custom-call | flops 4194304 | bytes 2097152 | tf_op jit(solution)/shard_map/pallas_call | solution.py:194
  9.5 2.8 %collective-permute-done.2 = bf16[16,8,128]{2,1,0:T(8,128)(2,1)S(1)} collective-permute-done((bf16[16,8,128]{2,1,0:T(8,128)(2,1)S(1)}, bf16[16,8,128]{2,1,0:T(8,128)(2,1)S(1)}, u32[]{:S(2)}, u32[]{:S(2)}) %collective-permute-start.2) | collective-permute-done | bytes 32800 | tf_op jit(solution)/shard_map/ppermute | solution.py:469
  12.4 3.4 %collective-permute-start.6 = (bf16[16,8,128]{2,1,0:T(8,128)(2,1)S(1)}, bf16[16,8,128]{2,1,0:T(8,128)(2,1)S(1)}, u32[]{:S(2)}, u32[]{:S(2)}) collective-permute-start(bf16[16,8,128]{2,1,0:T(8,128)(2,1)S(1)} %get-tuple-element.57._), channel_id=1, source_target_pairs={{0,64},{4,68},{8,72},{12,76},{16,80},{20,84},{24,88},{28,92},{32,9... | collective-permute-start | bytes 98312 | tf_op jit(solution)/shard_map/ppermute | solution.py:469
  15.7 1.6 %collective-permute-start.4 = (bf16[16,8,128]{2,1,0:T(8,128)(2,1)S(1)}, bf16[16,8,128]{2,1,0:T(8,128)(2,1)S(1)}, u32[]{:S(2)}, u32[]{:S(2)}) collective-permute-start(bf16[16,8,128]{2,1,0:T(8,128)(2,1)S(1)} %get-tuple-element.57._), channel_id=1, source_target_pairs={{0,32},{4,36},{8,40},{12,44},{16,48},{20,52},{24,56},{28,60},{32,0... | collective-permute-start | bytes 98312 | tf_op jit(solution)/shard_map/ppermute | solution.py:469
  17.3 1.3 %shard_map.75 = (f32[1024,128]{1,0:T(8,128)S(1)}, f32[16,8,128]{2,1,0:T(8,128)S(1)}) custom-call(f32[2048,128]{1,0:T(8,128)S(1)} %get-tuple-element.31.keyed_ref, f32[16,8,128]{2,1,0:T(8,128)S(1)} %get-tuple-element.32.decay_ref, f32[16,8,128]{2,1,0:T(8,128)S(1)} %get-tuple-element.60.scale_ref, f32[16,8,128]{2,1,0:T(8,128)S(1)} %get-tuple-element.37.held_ref, ...), custom_call_target="tpu_custom_call" | custom-call | flops 4194304 | bytes 2097152 | tf_op jit(solution)/shard_map/pallas_call | solution.py:194
  18.6 1.1 %collective-permute-done.5 = bf16[16,8,128]{2,1,0:T(8,128)(2,1)S(1)} collective-permute-done((bf16[16,8,128]{2,1,0:T(8,128)(2,1)S(1)}, bf16[16,8,128]{2,1,0:T(8,128)(2,1)S(1)}, u32[]{:S(2)}, u32[]{:S(2)}) %collective-permute-start.5) | collective-permute-done | bytes 32800 | tf_op jit(solution)/shard_map/ppermute | solution.py:469
  19.7 5.8 %collective-permute-start.7 = (bf16[16,8,128]{2,1,0:T(8,128)(2,1)S(1)}, bf16[16,8,128]{2,1,0:T(8,128)(2,1)S(1)}, u32[]{:S(2)}, u32[]{:S(2)}) collective-permute-start(bf16[16,8,128]{2,1,0:T(8,128)(2,1)S(1)} %fusion.14._), channel_id=1, source_target_pairs={{0,192},{4,196},{8,200},{12,204},{16,208},{20,212},{24,216},{28,22... | collective-permute-start | bytes 98312 | tf_op jit(solution)/shard_map/ppermute | solution.py:469
  25.7 2.6 %shard_map.76 = (f32[2048,128]{1,0:T(8,128)S(1)}, bf16[256,1024]{1,0:T(8,128)(2,1)S(1)}, bf16[1024,1024]{1,0:T(8,128)(2,1)S(1)}, bf16[1024,1024]{1,0:T(8,128)(2,...) custom-call(f32[1024,128]{1,0:T(8,128)S(1)} %get-tuple-element.36.early_ref, ...), custom_call_target="tpu_custom_call" | custom-call | flops 8388608 | bytes 4194304 | tf_op jit(solution)/shard_map/pallas_call | solution.py:281
  28.4 1.6 %collective-permute-start.9 = (bf16[144,1024]{1,0:T(8,128)(2,1)S(1)}, bf16[144,1024]{1,0:T(8,128)(2,1)S(1)}, u32[]{:S(2)}, u32[]{:S(2)}) collective-permute-start(bf16[144,1024]{1,0:T(8,128)(2,1)S(1)} %get-tuple-element.53), channel_id=1, source_target_pairs={{0,1},{1,2},{2,3},{3,0},{4,5},{5,6},{6,7},{7,4},{8,9},{9,10},{10,1... | collective-permute-start | bytes 884744 | tf_op jit(solution)/shard_map/ppermute | solution.py:511
  30.0 1.7 %collective-permute-start.12 = (bf16[112,1024]{1,0:T(8,128)(2,1)S(1)}, bf16[112,1024]{1,0:T(8,128)(2,1)S(1)}, u32[]{:S(2)}, u32[]{:S(2)}) collective-permute-start(bf16[112,1024]{1,0:T(8,128)(2,1)S(1)} %get-tuple-element.56), channel_id=1, source_target_pairs={{0,3},{1,0},{2,1},{3,2},{4,7},{5,4},{6,5},{7,6},{8,11},{9,8},{10,9... | collective-permute-start | bytes 688136 | tf_op jit(solution)/shard_map/ppermute | solution.py:512
  31.7 0.8 %shard_map.78 = (f32[144,1024]{1,0:T(8,128)S(1)}, bf16[112,1024]{1,0:T(8,128)(2,1)S(1)}) custom-call(bf16[256,1024]{1,0:T(8,128)(2,1)S(1)} %get-tuple-element.47.gated_ref, bf16[1024,1024]{1,0:T(8,128)(2,1)S(1)} %get-tuple-element.48.columns_ref), custom_call_target="tpu_custom_call" | custom-call | flops 536870912 | bytes 1048576 | tf_op jit(solution)/shard_map/pallas_call | solution.py:378
  32.9 2.3 %shard_map.79 = (bf16[144,1024]{1,0:T(8,128)(2,1)S(1)}, f32[112,1024]{1,0:T(8,128)S(1)}) custom-call(bf16[256,1024]{1,0:T(8,128)(2,1)S(1)} %get-tuple-element.47.gated_ref, bf16[1024,4096]{1,0:T(8,128)(2,1)} %weight_hbm.5, bf16[112,1024]{1,0:T(8,128)(2,1)S(1)} %get-tuple-element.49._), custom_call_target="tpu_custom_call" | custom-call | flops 536870912 | bytes 2097152 | tf_op jit(solution)/shard_map/pallas_call | solution.py:394
  35.2 3.2 %collective-permute-start.8 = (bf16[144,1024]{1,0:T(8,128)(2,1)S(1)}, bf16[144,1024]{1,0:T(8,128)(2,1)S(1)}, u32[]{:S(2)}, u32[]{:S(2)}) collective-permute-start(bf16[144,1024]{1,0:T(8,128)(2,1)S(1)} %get-tuple-element.50._), channel_id=1, source_target_pairs={{0,3},{1,0},{2,1},{3,2},{4,7},{5,4},{6,5},{7,6},{8,11},{9,8},{10,9... | collective-permute-start | bytes 884744 | tf_op jit(solution)/shard_map/ppermute | solution.py:516
  38.4 0.6 %collective-permute-done.9 = bf16[144,1024]{1,0:T(8,128)(2,1)S(1)} collective-permute-done((bf16[144,1024]{1,0:T(8,128)(2,1)S(1)}, bf16[144,1024]{1,0:T(8,128)(2,1)S(1)}, u32[]{:S(2)}, u32[]{:S(2)}) %collective-permute-start.9) | collective-permute-done | bytes 294944 | tf_op jit(solution)/shard_map/ppermute | solution.py:511
  39.1 0.9 %collective-permute-start.10 = (bf16[144,1024]{1,0:T(8,128)(2,1)S(1)}, bf16[144,1024]{1,0:T(8,128)(2,1)S(1)}, u32[]{:S(2)}, u32[]{:S(2)}) collective-permute-start(bf16[144,1024]{1,0:T(8,128)(2,1)S(1)} %add_convert_fusion), channel_id=1, source_target_pairs={{0,1},{1,2},{2,3},{3,0},{4,5},{5,6},{6,7},{7,4},{8,9},{9,10},{10,1... | collective-permute-start | bytes 884744 | tf_op jit(solution)/shard_map/ppermute | solution.py:518
  40.0 2.5 %collective-permute-start.13 = (bf16[112,1024]{1,0:T(8,128)(2,1)S(1)}, bf16[112,1024]{1,0:T(8,128)(2,1)S(1)}, u32[]{:S(2)}, u32[]{:S(2)}) collective-permute-start(bf16[112,1024]{1,0:T(8,128)(2,1)S(1)} %add_convert_fusion.1), channel_id=1, source_target_pairs={{0,3},{1,0},{2,1},{3,2},{4,7},{5,4},{6,5},{7,6},{8,11},{9,8},{10,9... | collective-permute-start | bytes 688136 | tf_op jit(solution)/shard_map/ppermute | solution.py:519
  42.5 2.3 %shard_map.80 = (f32[144,1024]{1,0:T(8,128)S(1)}, f32[112,1024]{1,0:T(8,128)S(1)}) custom-call(bf16[256,1024]{1,0:T(8,128)(2,1)S(1)} %get-tuple-element.47.gated_ref, bf16[1024,4096]{1,0:T(8,128)(2,1)} %weight_hbm.5, bf16[144,1024]{1,0:T(8,128)(2,1)S(1)} %get-tuple-element.50._), custom_call_target="tpu_custom_call" | custom-call | flops 536870912 | bytes 2097152 | tf_op jit(solution)/shard_map/pallas_call | solution.py:394
  44.9 2.4 %collective-permute-done.13.both_low = bf16[112,1024]{1,0:T(8,128)(2,1)S(1)} collective-permute-done((bf16[112,1024]{1,0:T(8,128)(2,1)S(1)}, bf16[112,1024]{1,0:T(8,128)(2,1)S(1)}, u32[]{:S(2)}, u32[]{:S(2)}) %collective-permute-start.13) | collective-permute-done | bytes 229408 | tf_op jit(solution)/shard_map/ppermute | solution.py:519
  47.3 0.4 collective-permute-done.10.both_top
  47.7 0.9 %shard_map.81 = bf16[256,1024]{1,0:T(8,128)(2,1)} custom-call(f32[144,1024]{1,0:T(8,128)S(1)} %get-tuple-element.51.mine_top, bf16[144,1024]{1,0:T(8,128)(2,1)S(1)} %collective-permute-done.8.near_top, bf16[144,1024]{1,0:T(8,128)(2,1)S(1)} %collective-permute-done.10.both_top, f32[112,1024]{1,0:T(8,128)S(1)} %get-tuple-element.54.mine_low, ...), custom_call_target="tpu_custom_call" | custom-call | flops 524288 | bytes 2097152 | tf_op jit(solution)/shard_map/pallas_call | solution.py:436
  (21 shorter events, 1.2 us)
Async XLA Ops:
  2.5 1.3 %collective-permute-start = (bf16[16,8,128]{2,1,0:T(8,128)(2,1)S(1)}, bf16[16,8,128]{2,1,0:T(8,128)(2,1)S(1)}, u32[]{:S(2)}, u32[]{:S(2)}) collective-permute-start(bf16[16,8,128]{2,1,0:T(8,128)(2,1)S(1)} %convert_element_type.97), channel_id=1, source_target_pairs={{0,4},{4,0},{8,12},{12,8},{16,20},{20,16},{24,28},{28,24},{32,36},... | collective-permute-start | bytes 98312 | tf_op jit(solution)/shard_map/ppermute | solution.py:469
  3.9 5.6 %collective-permute-start.3 = (bf16[16,8,128]{2,1,0:T(8,128)(2,1)S(1)}, bf16[16,8,128]{2,1,0:T(8,128)(2,1)S(1)}, u32[]{:S(2)}, u32[]{:S(2)}) collective-permute-start(bf16[16,8,128]{2,1,0:T(8,128)(2,1)S(1)} %get-tuple-element.59._), channel_id=1, source_target_pairs={{0,16},{4,20},{8,24},{12,28},{16,0},{20,4},{24,8},{28,12},{32,48},... | collective-permute-start | bytes 98312 | tf_op jit(solution)/shard_map/ppermute | solution.py:469
  7.1 5.1 %collective-permute-start.2 = (bf16[16,8,128]{2,1,0:T(8,128)(2,1)S(1)}, bf16[16,8,128]{2,1,0:T(8,128)(2,1)S(1)}, u32[]{:S(2)}, u32[]{:S(2)}) collective-permute-start(bf16[16,8,128]{2,1,0:T(8,128)(2,1)S(1)} %get-tuple-element.59._), channel_id=1, source_target_pairs={{0,24},{4,28},{8,16},{12,20},{16,8},{20,12},{24,0},{28,4},{32,56},... | collective-permute-start | bytes 98312 | tf_op jit(solution)/shard_map/ppermute | solution.py:469
  8.2 4.1 %collective-permute-start.1 = (bf16[16,8,128]{2,1,0:T(8,128)(2,1)S(1)}, bf16[16,8,128]{2,1,0:T(8,128)(2,1)S(1)}, u32[]{:S(2)}, u32[]{:S(2)}) collective-permute-start(bf16[16,8,128]{2,1,0:T(8,128)(2,1)S(1)} %get-tuple-element.59._), channel_id=1, source_target_pairs={{0,8},{4,12},{8,0},{12,4},{16,24},{20,28},{24,16},{28,20},{32,40},... | collective-permute-start | bytes 98312 | tf_op jit(solution)/shard_map/ppermute | solution.py:469
  12.4 6.2 %collective-permute-start.6 = (bf16[16,8,128]{2,1,0:T(8,128)(2,1)S(1)}, bf16[16,8,128]{2,1,0:T(8,128)(2,1)S(1)}, u32[]{:S(2)}, u32[]{:S(2)}) collective-permute-start(bf16[16,8,128]{2,1,0:T(8,128)(2,1)S(1)} %get-tuple-element.57._), channel_id=1, source_target_pairs={{0,64},{4,68},{8,72},{12,76},{16,80},{20,84},{24,88},{28,92},{32,9... | collective-permute-start | bytes 98312 | tf_op jit(solution)/shard_map/ppermute | solution.py:469
  15.7 3.9 %collective-permute-start.5 = (bf16[16,8,128]{2,1,0:T(8,128)(2,1)S(1)}, bf16[16,8,128]{2,1,0:T(8,128)(2,1)S(1)}, u32[]{:S(2)}, u32[]{:S(2)}) collective-permute-start(bf16[16,8,128]{2,1,0:T(8,128)(2,1)S(1)} %get-tuple-element.57._), channel_id=1, source_target_pairs={{0,96},{4,100},{8,104},{12,108},{16,112},{20,116},{24,120},{28,124... | collective-permute-start | bytes 98312 | tf_op jit(solution)/shard_map/ppermute | solution.py:469
  15.7 3.9 %collective-permute-start.4 = (bf16[16,8,128]{2,1,0:T(8,128)(2,1)S(1)}, bf16[16,8,128]{2,1,0:T(8,128)(2,1)S(1)}, u32[]{:S(2)}, u32[]{:S(2)}) collective-permute-start(bf16[16,8,128]{2,1,0:T(8,128)(2,1)S(1)} %get-tuple-element.57._), channel_id=1, source_target_pairs={{0,32},{4,36},{8,40},{12,44},{16,48},{20,52},{24,56},{28,60},{32,0... | collective-permute-start | bytes 98312 | tf_op jit(solution)/shard_map/ppermute | solution.py:469
  19.7 8.5 %collective-permute-start.7 = (bf16[16,8,128]{2,1,0:T(8,128)(2,1)S(1)}, bf16[16,8,128]{2,1,0:T(8,128)(2,1)S(1)}, u32[]{:S(2)}, u32[]{:S(2)}) collective-permute-start(bf16[16,8,128]{2,1,0:T(8,128)(2,1)S(1)} %fusion.14._), channel_id=1, source_target_pairs={{0,192},{4,196},{8,200},{12,204},{16,208},{20,212},{24,216},{28,22... | collective-permute-start | bytes 98312 | tf_op jit(solution)/shard_map/ppermute | solution.py:469
  28.4 10.6 %collective-permute-start.9 = (bf16[144,1024]{1,0:T(8,128)(2,1)S(1)}, bf16[144,1024]{1,0:T(8,128)(2,1)S(1)}, u32[]{:S(2)}, u32[]{:S(2)}) collective-permute-start(bf16[144,1024]{1,0:T(8,128)(2,1)S(1)} %get-tuple-element.53), channel_id=1, source_target_pairs={{0,1},{1,2},{2,3},{3,0},{4,5},{5,6},{6,7},{7,4},{8,9},{9,10},{10,1... | collective-permute-start | bytes 884744 | tf_op jit(solution)/shard_map/ppermute | solution.py:511
  30.0 10.0 %collective-permute-start.12 = (bf16[112,1024]{1,0:T(8,128)(2,1)S(1)}, bf16[112,1024]{1,0:T(8,128)(2,1)S(1)}, u32[]{:S(2)}, u32[]{:S(2)}) collective-permute-start(bf16[112,1024]{1,0:T(8,128)(2,1)S(1)} %get-tuple-element.56), channel_id=1, source_target_pairs={{0,3},{1,0},{2,1},{3,2},{4,7},{5,4},{6,5},{7,6},{8,11},{9,8},{10,9... | collective-permute-start | bytes 688136 | tf_op jit(solution)/shard_map/ppermute | solution.py:512
  32.5 12.3 %collective-permute-start.11 = (bf16[112,1024]{1,0:T(8,128)(2,1)S(1)}, bf16[112,1024]{1,0:T(8,128)(2,1)S(1)}, u32[]{:S(2)}, u32[]{:S(2)}) collective-permute-start(bf16[112,1024]{1,0:T(8,128)(2,1)S(1)} %get-tuple-element.49._), channel_id=1, source_target_pairs={{0,1},{1,2},{2,3},{3,0},{4,5},{5,6},{6,7},{7,4},{8,9},{9,10},{10,1... | collective-permute-start | bytes 688136 | tf_op jit(solution)/shard_map/ppermute | solution.py:514
  35.2 9.6 %collective-permute-start.8 = (bf16[144,1024]{1,0:T(8,128)(2,1)S(1)}, bf16[144,1024]{1,0:T(8,128)(2,1)S(1)}, u32[]{:S(2)}, u32[]{:S(2)}) collective-permute-start(bf16[144,1024]{1,0:T(8,128)(2,1)S(1)} %get-tuple-element.50._), channel_id=1, source_target_pairs={{0,3},{1,0},{2,1},{3,2},{4,7},{5,4},{6,5},{7,6},{8,11},{9,8},{10,9... | collective-permute-start | bytes 884744 | tf_op jit(solution)/shard_map/ppermute | solution.py:516
  39.1 8.6 %collective-permute-start.10 = (bf16[144,1024]{1,0:T(8,128)(2,1)S(1)}, bf16[144,1024]{1,0:T(8,128)(2,1)S(1)}, u32[]{:S(2)}, u32[]{:S(2)}) collective-permute-start(bf16[144,1024]{1,0:T(8,128)(2,1)S(1)} %add_convert_fusion), channel_id=1, source_target_pairs={{0,1},{1,2},{2,3},{3,0},{4,5},{5,6},{6,7},{7,4},{8,9},{9,10},{10,1... | collective-permute-start | bytes 884744 | tf_op jit(solution)/shard_map/ppermute | solution.py:518
  40.0 7.2 %collective-permute-start.13 = (bf16[112,1024]{1,0:T(8,128)(2,1)S(1)}, bf16[112,1024]{1,0:T(8,128)(2,1)S(1)}, u32[]{:S(2)}, u32[]{:S(2)}) collective-permute-start(bf16[112,1024]{1,0:T(8,128)(2,1)S(1)} %add_convert_fusion.1), channel_id=1, source_target_pairs={{0,3},{1,0},{2,1},{3,2},{4,7},{5,4},{6,5},{7,6},{8,11},{9,8},{10,9... | collective-permute-start | bytes 688136 | tf_op jit(solution)/shard_map/ppermute | solution.py:519
